TPU v7x, 128 devices: a whole 4x4x4 slice. The times are simulated.
128 devices in a mesh: gx: 8 (over x, core), gy: 16 (over y, z).
Axes of the slice: x: 4, y: 4, z: 4, core: 2. Of those that a mesh axis runs over, the one named last changes fastest.
Arguments:
- conductivity: float32 [16, 512, 2048], P(None, 'gx', 'gy'), may hold values from 0.2 to 5
- storage: float32 [16, 512, 2048], P(None, 'gx', 'gy'), may hold values from 0.5 to 5
- recharge: float32 [16, 512, 2048], P(None, 'gx', 'gy'), may hold values from -30 to 30
- block_ids: int32 [16384], replicated, may hold values from 0 to 131071, as said below
- neighbours: int32 [16384, 6], P(('gx', 'gy')), may hold values from -1 to 16383, as said below
- concentration: float32 [16384, 128], P(('gx', 'gy')), may hold values from 0.1 to 3
- sorption: float32 [16384, 128], P(('gx', 'gy')), may hold values from 0.3 to 3
Outputs:
- head: float32 [16, 512, 2048], P(None, 'gx', 'gy')
- solute: float32 [16384, 128], P(('gx', 'gy'))
Inputs may be any that keep to these rules, and one draw needn't show every extreme that they name: `block_ids`: distinct block numbers in the layout above. The blocks of one owner lie in 64 of the bricks, exactly 2 in each of those; the order of an owner's entries is arbitrary. `neighbours`: entry j of row i is the active block that shares block i's west, east, south, north, lower or upper side (j = 0 to 5), or -1; the relation is symmetric.
All inputs are finite; a program needn't handle non-finite values.
Results may differ from a plain program's by a relative error of at most 0.0003.
Values sent between devices are 32-bit elements; how exact they have to be, the bound alone decides.
No kernel may reach another device: no remote copies, remote signals or barrier semaphores. Data moves between devices by JAX's collectives and lax.ppermute only.
A program may use at most 128 MiB of HBM per device.

v0:
```python
import functools

import jax
import jax.numpy as jnp
from jax import lax
from jax.experimental import pallas as pl
from jax.experimental.pallas import tpu as pltpu
from jax.sharding import PartitionSpec as P

PICARD = 3
POROSITY = 0.35
BULK_DENSITY = 1.6
EXPONENT = 0.7
SOFTEN = 0.05
DISPERSION = 0.5
TIME_STEP = 0.1
ADVECT = 1.0
VERTICAL = 2.0
COUPLING = TIME_STEP * DISPERSION

AXES = ("gx", "gy")
ROWS = 9
NONE = -5000
F32 = jnp.float32
BF16 = jnp.bfloat16


def params(mib):
    return pltpu.CompilerParams(vmem_limit_bytes=mib * 1024 * 1024)


def iota(shape, dim):
    return lax.broadcasted_iota(jnp.int32, shape, dim)


def roll(x, shift, axis):
    return pltpu.roll(x, shift % x.shape[axis] if isinstance(shift, int) else shift, axis)


def split(x):
    high = x.astype(BF16)
    rest = x - high.astype(F32)
    middle = rest.astype(BF16)
    low = (rest - middle.astype(F32)).astype(BF16)
    return high, middle, low


def pick(mask, parts):
    chosen = jnp.where(mask, 1.0, 0.0).astype(BF16)
    high, middle, low = (jnp.dot(chosen, part, preferred_element_type=F32) for part in parts)
    return (low + middle) + high


def rows_of(parts, start, stop):
    return tuple(part[start:stop] for part in parts)


def place():
    across = lax.axis_size("gy")
    return lax.axis_index("gx") * across + lax.axis_index("gy")


def edges_kernel(k_low, k_high, s_low, s_high, r_low, r_high, east_ref, west_ref):
    shape = k_low.shape[1:]
    sub = iota(shape, 0)
    for z in range(k_low.shape[0]):
        east_ref[z] = jnp.where(
            sub >= 5,
            k_high[z],
            jnp.where(sub >= 3, roll(s_high[z], -3, 0), roll(r_high[z], -5, 0)),
        )
        west_ref[z] = jnp.where(
            sub < 3, k_low[z], jnp.where(sub < 5, roll(s_low[z], 3, 0), roll(r_low[z], 5, 0))
        )


def pack_edges(conductivity, storage, recharge):
    layers, rows, width = conductivity.shape
    low = pl.BlockSpec((layers, 8, width), lambda i: (0, 0, 0))
    high = pl.BlockSpec((layers, 8, width), lambda i: (0, rows // 8 - 1, 0))
    tile = jax.ShapeDtypeStruct((layers, 8, width), F32)
    return pl.pallas_call(
        edges_kernel,
        grid=(1,),
        in_specs=[low, high] * 3,
        out_specs=[pl.BlockSpec((layers, 8, width), lambda i: (0, 0, 0))] * 2,
        out_shape=[tile, tile],
        name="pack_edges",
    )(conductivity, conductivity, storage, storage, recharge, recharge)


def widened(index, z, own_ref, west_ref, east_ref):
    shift = (0, 3, 5)[index]
    top, bottom = west_ref[z], east_ref[z]
    if shift:
        top, bottom = roll(top, shift, 0), roll(bottom, -shift, 0)
    return jnp.concatenate([top, own_ref[z], bottom], 0)


def strip_kernel(k_ref, s_ref, r_ref, west_ref, east_ref, out_ref):
    layers = k_ref.shape[0]
    for index, own in enumerate((k_ref, s_ref, r_ref)):
        strip = None
        for z in range(layers):
            wide = roll(widened(index, z, own, west_ref, east_ref), z * 8 + 4, 1)
            if strip is None:
                strip = wide
            else:
                strip = jnp.where(iota(wide.shape, 1) >= z * 8, wide, strip)
        out_ref[index] = strip


def pack_strip(conductivity, storage, recharge, west, east):
    layers, rows, width = conductivity.shape
    return pl.pallas_call(
        strip_kernel,
        out_shape=jax.ShapeDtypeStruct((3, rows + 16, width), F32),
        compiler_params=params(16),
        name="pack_strip",
    )(conductivity, storage, recharge, west, east)


def column(row):
    n = row.shape[1]
    return jnp.sum(jnp.where(iota((n, n), 0) == iota((n, n), 1), row, 0.0), 1, keepdims=True)


def as_row(col):
    n = col.shape[0]
    return jnp.sum(jnp.where(iota((n, n), 0) == iota((n, n), 1), col, 0.0), 0, keepdims=True)


def send_kernel(down, across, rows_x, layers, ids_ref, conc_ref, sorp_ref, out_ref, col_ref, row_ref):
    devices, owned = ids_ref.shape
    lines = layers * rows_x
    me = place()
    ids = ids_ref[...]
    brick = ids // lines
    key = iota(ids.shape, 1) * lines + ids % lines
    gx, gy = me // across, me % across
    cols, rows = [], []
    for target, ok, edge in (
        (me, None, None),
        (me - across, gx > 0, rows_x - 1),
        (me + across, gx < down - 1, 0),
        (me - 1, gy > 0, None),
        (me + 1, gy < across - 1, None),
    ):
        if ok is not None:
            target = jnp.where(ok, target, -1)
        mine = brick == target
        first = jnp.min(jnp.where(mine, key, owned * lines).astype(F32), 1, keepdims=True)
        second = jnp.max(jnp.where(mine, key, -1).astype(F32), 1, keepdims=True)
        for code in (first, second):
            line = code.astype(jnp.int32) % lines
            keep = second >= 0.0
            if edge is not None:
                keep = keep & (line % rows_x == edge)
                line = line // rows_x
            value = jnp.where(keep, line, NONE).astype(F32)
            cols.append(value)
            rows.append(as_row(value))
    lane = iota((devices, 128), 1)
    packed = jnp.zeros((devices, 128), F32)
    for at, value in enumerate(cols):
        packed = jnp.where(lane == at, value, packed)
    col_ref[...] = packed.astype(jnp.int32)
    row_ref[...] = jnp.concatenate(
        rows + [jnp.zeros((16 - len(rows), devices), F32)], 0
    ).astype(jnp.int32)
    own = ids_ref[pl.ds(me, 1), :]
    own_brick = own // lines
    own_row = own % lines % rows_x
    brick_col = column(own_brick.astype(F32)).astype(jnp.int32)
    square = (owned, owned)
    same = (brick_col == own_brick) & (iota(square, 0) < iota(square, 1))
    rank = jnp.sum(jnp.where(same, 1.0, 0.0), 0, keepdims=True).astype(jnp.int32)
    dest = iota((devices, owned), 0)
    conc = conc_ref[...]
    conc_parts = split(conc)
    sorp_parts = split(sorp_ref[...])
    lane = iota((owned, conc.shape[1]), 1)
    misc = jnp.zeros((devices, conc.shape[1]), F32)
    for k in range(2):
        ranked = rank == k
        home = (dest == own_brick) & ranked
        out_ref[pl.ds(k, devices, stride=ROWS), :] = pick(home, conc_parts)
        out_ref[pl.ds(2 + k, devices, stride=ROWS), :] = pick(home, sorp_parts)
        after = (dest == own_brick + across) & ranked & (own_row == rows_x - 1)
        out_ref[pl.ds(4 + k, devices, stride=ROWS), :] = pick(after, conc_parts)
        before = (dest == own_brick - across) & ranked & (own_row == 0)
        out_ref[pl.ds(6 + k, devices, stride=ROWS), :] = pick(before, conc_parts)
        tails = jnp.where(lane // 2 == k, roll(conc, 2 + 2 * k, 1), 0.0)
        heads = jnp.where(lane // 2 == 2 + k, roll(conc, 4 + 2 * k, 1), 0.0)
        north = (dest == own_brick + 1) & ranked & (own_brick % across < across - 1)
        south = (dest == own_brick - 1) & ranked & (own_brick % across > 0)
        misc = misc + pick(north, split(tails)) + pick(south, split(heads))
    out_ref[pl.ds(8, devices, stride=ROWS), :] = misc


def pack_send(ids, concentration, sorption, layers, rows_x):
    devices, owned = ids.shape
    width = concentration.shape[1]
    kernel = functools.partial(
        send_kernel, lax.axis_size("gx"), lax.axis_size("gy"), rows_x, layers
    )
    return pl.pallas_call(
        kernel,
        out_shape=[
            jax.ShapeDtypeStruct((devices * ROWS, width), F32),
            jax.ShapeDtypeStruct((devices, 128), jnp.int32),
            jax.ShapeDtypeStruct((16, devices), jnp.int32),
        ],
        compiler_params=params(16),
        name="pack_send",
    )(ids, concentration, sorption)


def harmonic(a, c):
    return jnp.where(jnp.minimum(a, c) > 0.0, 2.0 * a * c / (a + c), jnp.maximum(a, c))


def flow_kernel(
    k_ref, s_ref, r_ref, west_ref, east_ref, strip_ref, south_ref, north_ref, send_ref,
    d_out, w_out, x_out, send_out,
    kx, sx, fw, fs, fb, rd, dd, ww,
):
    layers, rows, width = k_ref.shape
    tall = rows + 16
    shape = (tall, width)
    lane = iota(shape, 1)
    slot = lane % 8
    devices = send_ref.shape[0] // ROWS

    send_out[...] = send_ref[...]

    def side(low):
        def joined(index):
            if low:
                return jnp.where(slot < 4, south_ref[index], strip_ref[index])
            return jnp.where(slot < 4, strip_ref[index], north_ref[index])

        k, s, r = joined(0), joined(1), joined(2)
        face_w = harmonic(k, roll(k, 1, 0))
        face_s = harmonic(k, roll(k, 1, 1))
        face_b = jnp.where(lane >= 8, VERTICAL * harmonic(k, roll(k, 8, 1)), 0.0)
        diagonal = (
            s + face_w + roll(face_w, -1, 0) + face_s + roll(face_s, -1, 1) + face_b + roll(face_b, -8, 1)
        )
        inverse = jnp.where(k > 0.0, 1.0 / diagonal, 0.0)
        d = r * inverse
        flux_w = face_w * (roll(d, 1, 0) - d)
        flux_s = face_s * (roll(d, 1, 1) - d)
        flux_b = face_b * (roll(d, 8, 1) - d)
        image = (
            s * d
            + (roll(flux_w, -1, 0) - flux_w)
            + (roll(flux_s, -1, 1) - flux_s)
            + (roll(flux_b, -8, 1) - flux_b)
        )
        w = image * inverse
        return face_s, flux_s, face_s * (roll(w, 1, 1) - w)

    low_face, low_d, low_w = side(True)
    high_face, high_d, high_w = side(False)

    def with_low(z, field, strip):
        return jnp.where(lane == 0, roll(strip, width - 4 - z * 8, 1), field)

    def north_of(z, field, strip):
        shift = lax.rem(width - 5 + width - z * 8, width)
        return jnp.where(lane == width - 1, roll(strip, shift, 1), roll(field, -1, 1))

    def widen(z, carry):
        kx[z] = widened(0, z, k_ref, west_ref, east_ref)
        return carry

    lax.fori_loop(0, layers, widen, 0)
    fb[0] = jnp.zeros(shape, F32)

    def faces(z, carry):
        k = kx[z]
        face_w = harmonic(k, roll(k, 1, 0))
        face_s = with_low(z, harmonic(k, roll(k, 1, 1)), low_face)
        face_n = north_of(z, face_s, high_face)
        upper = kx[jnp.minimum(z + 1, layers - 1)]
        face_a = jnp.where(z < layers - 1, VERTICAL * harmonic(k, upper), 0.0)
        s = widened(1, z, s_ref, west_ref, east_ref)
        r = widened(2, z, r_ref, west_ref, east_ref)
        diagonal = s + face_w + roll(face_w, -1, 0) + face_s + face_n + fb[z] + face_a
        inverse = jnp.where(k > 0.0, 1.0 / diagonal, 0.0)
        fw[z] = face_w
        fs[z] = face_s
        fb[z + 1] = face_a
        rd[z] = inverse
        dd[z] = r * inverse
        sx[z] = s
        return carry

    lax.fori_loop(0, layers, faces, 0)

    def total(x):
        return jnp.sum(x[8 : 8 + rows].reshape(rows // 8, 8, width), 0)

    def apply(z, field, low, high, block):
        h = field[z]
        below = field[jnp.maximum(z - 1, 0)]
        above = field[jnp.minimum(z + 1, layers - 1)]
        flux_w = fw[z] * (roll(h, 1, 0) - h)
        flux_e = roll(flux_w, -1, 0)
        flux_b = fb[z] * (below - h)
        flux_a = fb[z + 1] * (h - above)
        flux_s = with_low(z, fs[z] * (roll(h, 1, 1) - h), low)
        flux_n = north_of(z, flux_s, high)
        for at, flux in enumerate((flux_w, flux_e, flux_b, flux_a, flux_s, flux_n)):
            x_out[block + at, pl.ds(pl.multiple_of(z * rows, rows), rows), :] = flux[8 : 8 + rows]
        return h, sx[z] * h + (flux_e - flux_w) + (flux_a - flux_b) + (flux_n - flux_s)

    zero = jnp.zeros((8, width), F32)

    def first(z, sums):
        d, image = apply(z, dd, low_d, high_d, 0)
        w = image * rd[z]
        ww[z] = w
        d_out[z] = d[8 : 8 + rows]
        w_out[z] = w[8 : 8 + rows]
        r = r_ref[z]
        gamma = jnp.sum((r * d[8 : 8 + rows]).reshape(rows // 8, 8, width), 0)
        return sums[0] + gamma, sums[1] + total(d * image), sums[2] + total(image * w)

    gamma, bend, curve = lax.fori_loop(0, layers, first, (zero, zero, zero))

    def second(z, acc):
        w, image = apply(z, ww, low_w, high_w, 6)
        return acc + total(w * image)

    twist = lax.fori_loop(0, layers, second, zero)
    lane_row = iota((devices, width), 1)
    misc = send_ref[pl.ds(8, devices, stride=ROWS), :]
    for at, part in enumerate((gamma, bend, curve, twist)):
        value = jnp.sum(jnp.sum(part, 0, keepdims=True), 1, keepdims=True)
        misc = jnp.where(lane_row == 8 + at, value, misc)
    send_out[pl.ds(8, devices, stride=ROWS), :] = misc


def flow(conductivity, storage, recharge, west, east, strip, south, north, send):
    layers, rows, width = conductivity.shape
    tall = pltpu.VMEM((layers, rows + 16, width), F32)
    return pl.pallas_call(
        flow_kernel,
        out_shape=[
            jax.ShapeDtypeStruct(conductivity.shape, F32),
            jax.ShapeDtypeStruct(conductivity.shape, F32),
            jax.ShapeDtypeStruct((12, layers * rows, width), F32),
            jax.ShapeDtypeStruct(send.shape, F32),
        ],
        scratch_shapes=[tall] * 4
        + [pltpu.VMEM((layers + 1, rows + 16, width), F32)]
        + [tall] * 3,
        compiler_params=params(28),
        name="flow",
    )(conductivity, storage, recharge, west, east, strip, south, north, send)


def gather_kernel(x_ref, col_ref, out_ref):
    lines = x_ref.shape[1]
    cols = col_ref[...]
    own = jnp.concatenate([cols[:, 0:1], cols[:, 1:2]], 0)
    mask = own == iota((own.shape[0], lines), 1)
    chosen = jnp.where(mask, 1.0, 0.0).astype(BF16)
    for at in range(x_ref.shape[0]):
        parts = split(x_ref[at])
        high, middle, low = (jnp.dot(chosen, part, preferred_element_type=F32) for part in parts)
        out_ref[at] = (low + middle) + high


def gather_fluxes(fluxes, cols):
    count, lines, width = fluxes.shape
    return pl.pallas_call(
        gather_kernel,
        out_shape=jax.ShapeDtypeStruct((count, 2 * cols.shape[0], width), F32),
        compiler_params=params(28),
        name="gather_fluxes",
    )(fluxes, cols)


def minmod(a, d):
    return jnp.maximum(jnp.minimum(a, d), 0.0) + jnp.minimum(jnp.maximum(a, d), 0.0)


def tridiagonal(diagonal, right):
    width = diagonal.shape[1]
    side = jnp.where(iota(diagonal.shape, 1) == 0, 0.0, -COUPLING)
    step = 1
    while step < width:
        inverse = 1.0 / diagonal
        scaled = side * inverse
        value = right * inverse
        before = roll(inverse, step, 1)
        right = right - side * roll(value, step, 1) - roll(side * value, -step, 1)
        diagonal = diagonal - side * (side * before) - roll(side * scaled, -step, 1)
        side = -side * roll(scaled, step, 1)
        step *= 2
    return right / diagonal


def transport(c, sorption, fluxes, west, east, lower, upper, ends):
    lane = iota(c.shape, 1)
    width = c.shape[1]
    last = lane == width - 1
    south_one = roll(ends, -1, 1)
    north_one = roll(ends, width - 5, 1)
    back = jnp.where(lane == 0, south_one, roll(c, 1, 1))
    back2 = jnp.where(lane < 2, ends, roll(c, 2, 1))
    ahead = jnp.where(last, north_one, roll(c, -1, 1))
    ahead2 = jnp.where(lane >= width - 2, roll(ends, width - 6, 1), roll(c, -2, 1))
    q_w, q_e, q_b, q_a, q_s, q_n = fluxes

    def face(q, far_left, left, right, far_right):
        rise = right - left
        positive = left + 0.5 * minmod(rise, left - far_left)
        negative = right + 0.5 * minmod(-rise, right - far_right)
        return jnp.maximum(q, 0.0) * positive + jnp.minimum(q, 0.0) * negative

    along = face(q_s, back2, back, c, ahead)
    beyond = face(q_n, back, c, ahead, ahead2)
    advect = along - jnp.where(last, beyond, roll(along, -1, 1))
    advect = advect + jnp.maximum(q_w, 0.0) * west + jnp.minimum(q_w, 0.0) * c
    advect = advect - jnp.maximum(q_e, 0.0) * c - jnp.minimum(q_e, 0.0) * east
    advect = advect + jnp.maximum(q_b, 0.0) * lower + jnp.minimum(q_b, 0.0) * c
    advect = advect - jnp.maximum(q_a, 0.0) * c - jnp.minimum(q_a, 0.0) * upper
    advect = ADVECT * advect
    advect = advect + COUPLING * (
        jnp.where(lane == 0, south_one, 0.0) + jnp.where(last, north_one, 0.0)
    )
    weight = BULK_DENSITY * sorption
    v = c
    source = None
    for sweep in range(PICARD):
        square = v * v + SOFTEN * SOFTEN
        power = weight * jnp.exp((0.5 * (EXPONENT - 1.0)) * jnp.log(square))
        retard = POROSITY + power
        root = jnp.sqrt(square)
        if sweep == 0:
            source = POROSITY * c + power * root + advect
            target = retard * c + advect
        else:
            target = power * (v - root) + source
        v = tridiagonal(retard + 2.0 * COUPLING, target)
    return v


def neighbour_values(c, cols, rows, west_edge, east_edge, south_misc, north_misc, rows_x):
    own_c = jnp.concatenate([cols[:, 0:1], cols[:, 1:2]], 0)
    own_r = jnp.concatenate([rows[0:1], rows[1:2]], 1)
    layers = west_edge.shape[0]
    active = own_c >= 0
    row_c = own_c % rows_x
    layer_c = own_c // rows_x
    first = active & (row_c == 0)
    final = active & (row_c == rows_x - 1)
    at_layer = iota((own_c.shape[0], layers), 1) == layer_c
    parts = split(c)
    west = pick((own_r == own_c - 1) & (row_c != 0), parts) + pick(
        at_layer & first, split(west_edge)
    )
    east = pick((own_r == own_c + 1) & (row_c != rows_x - 1), parts) + pick(
        at_layer & final, split(east_edge)
    )
    lower = pick(own_r == own_c - rows_x, parts)
    upper = pick(own_r == own_c + rows_x, parts)
    lane = iota(south_misc.shape, 1)
    ends = None
    for k in range(2):
        tails = split(jnp.where(lane // 2 == k, south_misc, 0.0))
        heads = split(jnp.where(lane // 2 == 2 + k, north_misc, 0.0))
        part = pick((rows[6 + k : 7 + k] == own_c) & active, tails)
        part = part + pick((rows[8 + k : 9 + k] == own_c) & active, heads)
        ends = part if ends is None else ends + part
    return west, east, lower, upper, ends + roll(ends, -2, 1)


def first_kernel(
    rows_x, recv_ref, gath_ref, col_ref, row_ref, c_out, s_out, flux_out, east_out, west_out, misc_out, scal_out
):
    devices = recv_ref.shape[0] // ROWS
    width = recv_ref.shape[1]

    def received(at):
        return recv_ref[pl.ds(at, devices, stride=ROWS), :]

    cols, rows = col_ref[...], row_ref[...]
    layers = east_out.shape[0]
    misc = received(8)
    sums = jnp.sum(misc, 0, keepdims=True)
    at = iota(sums.shape, 1)
    gamma, bend, curve, twist = (
        jnp.sum(jnp.where(at == 8 + i, sums, 0.0), 1, keepdims=True) for i in range(4)
    )
    alpha = gamma / bend
    gamma_next = alpha * alpha * curve - gamma
    beta = gamma_next / gamma
    cross = bend - alpha * curve
    bend_next = bend - 2.0 * alpha * curve + alpha * alpha * twist + 2.0 * beta * cross + beta * beta * bend
    alpha_next = gamma_next / bend_next
    on_d = alpha + alpha_next * (1.0 + beta)
    on_w = -alpha * alpha_next
    lane8 = iota((8, width), 1)
    scal_out[...] = jnp.where(lane8 == 0, on_d, on_w)

    c = jnp.concatenate([received(0), received(1)], 0)
    s = jnp.concatenate([received(2), received(3)], 0)
    layer = iota((layers, 2 * devices), 0)
    west_codes = jnp.concatenate([rows[2:3], rows[3:4]], 1)
    east_codes = jnp.concatenate([rows[4:5], rows[5:6]], 1)
    west_edge = pick(layer == west_codes, split(jnp.concatenate([received(4), received(5)], 0)))
    east_edge = pick(layer == east_codes, split(jnp.concatenate([received(6), received(7)], 0)))
    fluxes = []
    for i in range(6):
        flux = on_d * gath_ref[i] + on_w * gath_ref[6 + i]
        flux_out[i] = flux
        fluxes.append(flux)
    beside = neighbour_values(c, cols, rows, west_edge, east_edge, misc, misc, rows_x)
    c = transport(c, s, fluxes, *beside)
    c_out[...] = c
    s_out[...] = s
    own_r = jnp.concatenate([rows[0:1], rows[1:2]], 1)
    here = (own_r // rows_x == layer) & (own_r >= 0)
    parts = split(c)
    east_out[...] = pick(here & (own_r % rows_x == rows_x - 1), parts)
    west_out[...] = pick(here & (own_r % rows_x == 0), parts)
    lane = iota((devices, width), 1)
    c0, c1 = c[:devices], c[devices:]
    misc_out[...] = jnp.where(
        lane < 2,
        roll(c0, 2, 1),
        jnp.where(lane < 4, roll(c1, 4, 1), jnp.where(lane < 6, roll(c0, 4, 1), roll(c1, 6, 1))),
    )


def first_step(received, gathered, cols, rows, layers, rows_x):
    width = received.shape[1]
    devices = cols.shape[0]
    lines = jax.ShapeDtypeStruct((2 * devices, width), F32)
    edge = jax.ShapeDtypeStruct((layers, width), F32)
    return pl.pallas_call(
        functools.partial(first_kernel, rows_x),
        out_shape=[
            lines,
            lines,
            jax.ShapeDtypeStruct((6, 2 * devices, width), F32),
            edge,
            edge,
            jax.ShapeDtypeStruct((devices, width), F32),
            jax.ShapeDtypeStruct((8, width), F32),
        ],
        compiler_params=params(16),
        name="first_step",
    )(received, gathered, cols, rows)


def second_kernel(
    rows_x, c_ref, s_ref, flux_ref, col_ref, row_ref, west_ref, east_ref, south_ref, north_ref, out_ref
):
    c, s = c_ref[...], s_ref[...]
    devices = c.shape[0] // 2
    beside = neighbour_values(
        c, col_ref[...], row_ref[...], west_ref[...], east_ref[...], south_ref[...], north_ref[...], rows_x
    )
    c = transport(c, s, [flux_ref[i] for i in range(6)], *beside)
    for k in range(2):
        out_ref[pl.ds(k, devices, stride=2), :] = c[k * devices : (k + 1) * devices]


def second_step(c, s, fluxes, cols, rows, west, east, south, north, rows_x):
    return pl.pallas_call(
        functools.partial(second_kernel, rows_x),
        out_shape=jax.ShapeDtypeStruct(c.shape, F32),
        compiler_params=params(16),
        name="second_step",
    )(c, s, fluxes, cols, rows, west, east, south, north)


def owner_kernel(lines, ids_ref, recv_ref, out_ref):
    devices, owned = ids_ref.shape
    own = ids_ref[pl.ds(place(), 1), :]
    brick = own // lines
    brick_col = column(brick.astype(F32)).astype(jnp.int32)
    square = (owned, owned)
    same = (brick_col == brick) & (iota(square, 1) < iota(square, 0))
    rank = jnp.sum(jnp.where(same, 1.0, 0.0), 1, keepdims=True).astype(jnp.int32)
    mask = brick_col * 2 + rank == iota((owned, 2 * devices), 1)
    out_ref[...] = pick(mask, split(recv_ref[...]))


def to_owner(ids, received, lines):
    return pl.pallas_call(
        functools.partial(owner_kernel, lines),
        out_shape=jax.ShapeDtypeStruct((ids.shape[1], received.shape[1]), F32),
        compiler_params=params(16),
        name="to_owner",
    )(ids, received)


def exchange(low_side, high_side, axis):
    count = lax.axis_size(axis)
    forward = [(i, i + 1) for i in range(count - 1)]
    backward = [(i + 1, i) for i in range(count - 1)]
    return lax.ppermute(high_side, axis, forward), lax.ppermute(low_side, axis, backward)


def body(conductivity, storage, recharge, block_ids, neighbours, concentration, sorption):
    layers, rows_x, width = conductivity.shape
    devices = lax.axis_size(AXES)
    owned = concentration.shape[0]
    ids = block_ids.reshape(devices, owned)
    to_east, to_west = pack_edges(conductivity, storage, recharge)
    west, east = exchange(to_west, to_east, "gx")
    send, cols, rows = pack_send(ids, concentration, sorption, layers, rows_x)
    strip = pack_strip(conductivity, storage, recharge, west, east)
    south, north = exchange(strip, strip, "gy")
    base, image, fluxes, send = flow(
        conductivity, storage, recharge, west, east, strip, south, north, send
    )
    received = lax.all_to_all(
        send.reshape(devices, 1, ROWS * width), AXES, split_axis=0, concat_axis=0, tiled=True
    ).reshape(devices * ROWS, width)
    gathered = gather_fluxes(fluxes, cols)
    c, s, flux, to_east, to_west, misc, scal = first_step(
        received, gathered, cols, rows, layers, rows_x
    )
    west, east = exchange(to_west, to_east, "gx")
    south, north = exchange(misc, misc, "gy")
    head = scal[0, 0] * base + scal[0, 1] * image
    result = second_step(c, s, flux, cols, rows, west, east, south, north, rows_x)
    returned = lax.all_to_all(
        result.reshape(devices, 2, width), AXES, split_axis=0, concat_axis=0, tiled=True
    ).reshape(devices * 2, width)
    return head, to_owner(ids, returned, layers * rows_x)


def solution(mesh):
    return jax.shard_map(
        body,
        mesh=mesh,
        in_specs=(
            P(None, "gx", "gy"),
            P(None, "gx", "gy"),
            P(None, "gx", "gy"),
            P(),
            P(("gx", "gy"), None),
            P(("gx", "gy"), None),
            P(("gx", "gy"), None),
        ),
        out_specs=(P(None, "gx", "gy"), P(("gx", "gy"), None)),
        check_vma=False,
    )
```

profile of v0, /device:TPU:1, one launch (start us, length us, event | category | flops | bytes accessed | tf_op | source)
XLA Modules:
  0.0 108.8 jit_solution(8763817171455016716)
XLA Ops:
  0.6 1.7 %pack_edges.1 = (f32[16,8,128]{2,1,0:T(8,128)}, f32[16,8,128]{2,1,0:T(8,128)}) custom-call(f32[16,64,128]{2,1,0:T(8,128)} %k_ref.3, f32[16,64,128]{2,1,0:T(8,128)} %k_ref.3, f32[16,64,128]{2,1,0:T(8,128)} %s_ref.3, f32[16,64,128]{2,1,0:T(8,128)} %s_ref.3, f32[16,64,128]{2,1,0:T(8,128)} %r_ref.3, f32[16,64,128]{2,1,0:T(8,128)} %r_ref.3), custom_call_target="tpu_custom_call" | custom-call | tf_op jit(solution)/shard_map/pack_edges/pallas_call | solution.py:82
  2.3 4.5 %collective-permute-start = (f32[16,8,128]{2,1,0:T(8,128)}, f32[16,8,128]{2,1,0:T(8,128)S(1)}, u32[]{:S(2)}, u32[]{:S(2)}) collective-permute-start(f32[16,8,128]{2,1,0:T(8,128)} %get-tuple-element.18), channel_id=1, source_target_pairs={{0,16},{16,32},{32,48},{48,64},{64,80},{80,96},{96,112},{1,17},{17... | collective-permute-start | bytes 196616 | tf_op jit(solution)/shard_map/ppermute | solution.py:609
  6.8 1.9 %collective-permute-start.1 = (f32[16,8,128]{2,1,0:T(8,128)}, f32[16,8,128]{2,1,0:T(8,128)S(1)}, u32[]{:S(2)}, u32[]{:S(2)}) collective-permute-start(f32[16,8,128]{2,1,0:T(8,128)} %get-tuple-element.19), channel_id=1, source_target_pairs={{16,0},{32,16},{48,32},{64,48},{80,64},{96,80},{112,96},{17,1},{33... | collective-permute-start | bytes 196616 | tf_op jit(solution)/shard_map/ppermute | solution.py:609
  8.8 3.9 %collective-permute-done.1.east_ref = f32[16,8,128]{2,1,0:T(8,128)S(1)} collective-permute-done((f32[16,8,128]{2,1,0:T(8,128)}, f32[16,8,128]{2,1,0:T(8,128)S(1)}, u32[]{:S(2)}, u32[]{:S(2)}) %collective-permute-start.1) | collective-permute-done | bytes 65568 | tf_op jit(solution)/shard_map/ppermute | solution.py:609
  12.6 1.0 copy-done
  13.7 1.0 copy-done.2
  14.7 1.0 copy-done.4
  16.3 1.3 %collective-permute-start.3 = (f32[3,80,128]{2,1,0:T(8,128)S(1)}, f32[3,80,128]{2,1,0:T(8,128)S(1)}, u32[]{:S(2)}, u32[]{:S(2)}) collective-permute-start(f32[3,80,128]{2,1,0:T(8,128)S(1)} %pack_strip.1.strip_ref), channel_id=1, source_target_pairs={{1,0},{2,1},{3,2},{4,3},{5,4},{6,5},{7,6},{8,7},{9,8},{10,9},{11,1... | collective-permute-start | bytes 368648 | tf_op jit(solution)/shard_map/ppermute | solution.py:609
  17.6 4.2 %collective-permute-start.2 = (f32[3,80,128]{2,1,0:T(8,128)S(1)}, f32[3,80,128]{2,1,0:T(8,128)S(1)}, u32[]{:S(2)}, u32[]{:S(2)}) collective-permute-start(f32[3,80,128]{2,1,0:T(8,128)S(1)} %pack_strip.1.strip_ref), channel_id=1, source_target_pairs={{0,1},{1,2},{2,3},{3,4},{4,5},{5,6},{6,7},{7,8},{8,9},{9,10},{10,1... | collective-permute-start | bytes 368648 | tf_op jit(solution)/shard_map/ppermute | solution.py:609
  22.6 0.8 copy-done.10
  23.5 0.8 copy-done.11
  24.3 1.2 %pack_send.1 = (f32[1152,128]{1,0:T(8,128)S(1)}, s32[128,128]{1,0:T(8,128)S(1)}, s32[16,128]{1,0:T(8,128)S(1)}) custom-call(s32[128,128]{1,0:T(8,128)S(1)} %bitcast.9, f32[128,128]{1,0:T(8,128)S(1)} %copy-done.10, f32[128,128]{1,0:T(8,128)S(1)} %copy-done.11), custom_call_target="tpu_custom_call" | custom-call | tf_op jit(solution)/shard_map/pack_send/pallas_call | solution.py:207
  25.6 1.0 copy-done.1
  26.6 1.0 copy-done.3
  27.6 1.0 copy-done.5
  28.7 9.4 %flow.1 = (f32[16,64,128]{2,1,0:T(8,128)S(1)}, f32[16,64,128]{2,1,0:T(8,128)S(1)}, f32[12,1024,128]{2,1,0:T(8,128)S(1)}, f32[1152,128]{1,0:T(8,128)}) custom-call(f32[16,64,128]{2,1,0:T(8,128)S(1)} %copy-done.1, f32[16,64,128]{2,1,0:T(8,128)S(1)} %copy-done.3, f32[16,64,128]{2,1,0:T(8,128)S(1)} %copy-done.5, ...), custom_call_target="tpu_custom_call" | custom-call | tf_op jit(solution)/shard_map/flow/pallas_call | solution.py:349
  38.1 2.6 %copy-done.6 = f32[12,1024,128]{2,1,0:T(8,128)} copy-done((f32[12,1024,128]{2,1,0:T(8,128)}, f32[12,1024,128]{2,1,0:T(8,128)S(1)}, u32[]{:S(2)}) %copy-start.6) | copy-done | bytes 6291480
  40.7 12.4 %all-to-all-start = ((f32[128,1,1152]{2,1,0:T(1,128)}), f32[128,1,1152]{2,1,0:T(1,128)S(1)}, u32[]{:S(2)}, u32[]{:S(2)}) async-start(f32[128,1,1152]{2,1,0:T(1,128)} %bitcast.1), calls=%async_computation | async-start | bytes 1179648 | tf_op jit(solution)/shard_map/all_to_all | solution.py:625
  53.1 2.8 %copy-done.7 = f32[12,1024,128]{2,1,0:T(8,128)S(1)} copy-done((f32[12,1024,128]{2,1,0:T(8,128)S(1)}, f32[12,1024,128]{2,1,0:T(8,128)}, u32[]{:S(2)}) %copy-start.7) | copy-done | bytes 6291480
  55.9 5.3 %gather_fluxes.1.gath_ref = f32[12,256,128]{2,1,0:T(8,128)S(1)} custom-call(f32[12,1024,128]{2,1,0:T(8,128)S(1)} %copy-done.7, s32[128,128]{1,0:T(8,128)S(1)} %get-tuple-element.23.col_ref), custom_call_target="tpu_custom_call" | custom-call | tf_op jit(solution)/shard_map/gather_fluxes/pallas_call | solution.py:379
  61.2 6.5 %all-to-all-done = f32[128,1,1152]{2,1,0:T(1,128)S(1)} async-done(((f32[128,1,1152]{2,1,0:T(1,128)}), f32[128,1,1152]{2,1,0:T(1,128)S(1)}, u32[]{:S(2)}, u32[]{:S(2)}) %all-to-all-start) | async-done | bytes 589856 | tf_op jit(solution)/shard_map/all_to_all | solution.py:625
  67.7 5.3 %first_step.1 = (f32[256,128]{1,0:T(8,128)S(1)}, f32[256,128]{1,0:T(8,128)S(1)}, f32[6,256,128]{2,1,0:T(8,128)S(1)}, f32[16,128]{1,0:T(8,128)S(1)}, f32[16,128]{...) custom-call(f32[1152,128]{1,0:T(8,128)S(1)} %bitcast.7, f32[12,256,128]{2,1,0:T(8,128)S(1)} %gather_fluxes.1.gath_ref, ...), custom_call_target="tpu_custom_call" | custom-call | tf_op jit(solution)/shard_map/first_step/pallas_call | solution.py:546
  73.0 1.3 %collective-permute-start.7 = (f32[128,128]{1,0:T(8,128)S(1)}, f32[128,128]{1,0:T(8,128)S(1)}, u32[]{:S(2)}, u32[]{:S(2)}) collective-permute-start(f32[128,128]{1,0:T(8,128)S(1)} %get-tuple-element.33), channel_id=1, source_target_pairs={{1,0},{2,1},{3,2},{4,3},{5,4},{6,5},{7,6},{8,7},{9,8},{10,9},{11,1... | collective-permute-start | bytes 196616 | tf_op jit(solution)/shard_map/ppermute | solution.py:609
  74.3 4.0 %collective-permute-start.6 = (f32[128,128]{1,0:T(8,128)S(1)}, f32[128,128]{1,0:T(8,128)S(1)}, u32[]{:S(2)}, u32[]{:S(2)}) collective-permute-start(f32[128,128]{1,0:T(8,128)S(1)} %get-tuple-element.33), channel_id=1, source_target_pairs={{0,1},{1,2},{2,3},{3,4},{4,5},{5,6},{6,7},{7,8},{8,9},{9,10},{10,1... | collective-permute-start | bytes 196616 | tf_op jit(solution)/shard_map/ppermute | solution.py:609
  78.3 3.5 %collective-permute-start.4 = (f32[16,128]{1,0:T(8,128)S(1)}, f32[16,128]{1,0:T(8,128)S(1)}, u32[]{:S(2)}, u32[]{:S(2)}) collective-permute-start(f32[16,128]{1,0:T(8,128)S(1)} %get-tuple-element.31), channel_id=1, source_target_pairs={{0,16},{16,32},{32,48},{48,64},{64,80},{80,96},{96,112},{1,17},{17... | collective-permute-start | bytes 24584 | tf_op jit(solution)/shard_map/ppermute | solution.py:609
  81.8 2.1 %collective-permute-start.5 = (f32[16,128]{1,0:T(8,128)S(1)}, f32[16,128]{1,0:T(8,128)S(1)}, u32[]{:S(2)}, u32[]{:S(2)}) collective-permute-start(f32[16,128]{1,0:T(8,128)S(1)} %get-tuple-element.32), channel_id=1, source_target_pairs={{16,0},{32,16},{48,32},{64,48},{80,64},{96,80},{112,96},{17,1},{33... | collective-permute-start | bytes 24584 | tf_op jit(solution)/shard_map/ppermute | solution.py:609
  84.6 2.2 %collective-permute-done.5.east_ref = f32[16,128]{1,0:T(8,128)S(1)} collective-permute-done((f32[16,128]{1,0:T(8,128)S(1)}, f32[16,128]{1,0:T(8,128)S(1)}, u32[]{:S(2)}, u32[]{:S(2)}) %collective-permute-start.5) | collective-permute-done | bytes 8224 | tf_op jit(solution)/shard_map/ppermute | solution.py:609
  86.8 5.8 %second_step.1 = f32[256,128]{1,0:T(8,128)} custom-call(f32[256,128]{1,0:T(8,128)S(1)} %get-tuple-element.28.c_ref, f32[256,128]{1,0:T(8,128)S(1)} %get-tuple-element.29.s_ref, f32[6,256,128]{2,1,0:T(8,128)S(1)} %get-tuple-element.30.flux_ref, s32[128,128]{1,0:T(8,128)S(1)} %get-tuple-element.23.col_ref, s32[16,128]{1,0:T(8,128)S(1)} %get-tuple-element.24.row_ref, ...), custom_call_target="tpu_custom_call" | custom-call | tf_op jit(solution)/shard_map/second_step/pallas_call | solution.py:576
  92.6 5.3 %all-to-all-start.1 = ((f32[128,2,128]{2,1,0:T(2,128)}), f32[128,2,128]{2,1,0:T(2,128)S(1)}, u32[]{:S(2)}, u32[]{:S(2)}) async-start(f32[128,2,128]{2,1,0:T(2,128)} %bitcast.5), calls=%async_computation.1 | async-start | bytes 262144 | tf_op jit(solution)/shard_map/all_to_all | solution.py:636
  97.8 2.2 %multiply_add_fusion = f32[16,64,128]{2,1,0:T(8,128)} fusion(f32[16,64,128]{2,1,0:T(8,128)S(1)} %get-tuple-element.27, f32[16,64,128]{2,1,0:T(8,128)S(1)} %get-tuple-element.26, f32[]{:T(128)} %bitcast.4, f32[]{:T(128)} %bitcast.3), kind=kLoop, calls=%fused_computation | loop fusion | flops 393216 | bytes 1572872 | tf_op jit(solution)/shard_map/add | solution.py:634
  100.0 7.8 %all-to-all-done.1 = f32[128,2,128]{2,1,0:T(2,128)S(1)} async-done(((f32[128,2,128]{2,1,0:T(2,128)}), f32[128,2,128]{2,1,0:T(2,128)S(1)}, u32[]{:S(2)}, u32[]{:S(2)}) %all-to-all-start.1) | async-done | bytes 131104 | tf_op jit(solution)/shard_map/all_to_all | solution.py:636
  107.9 1.0 to_owner.1
  (22 shorter events, 2.1 us)
Async XLA Ops:
  2.3 6.4 %collective-permute-start = (f32[16,8,128]{2,1,0:T(8,128)}, f32[16,8,128]{2,1,0:T(8,128)S(1)}, u32[]{:S(2)}, u32[]{:S(2)}) collective-permute-start(f32[16,8,128]{2,1,0:T(8,128)} %get-tuple-element.18), channel_id=1, source_target_pairs={{0,16},{16,32},{32,48},{48,64},{64,80},{80,96},{96,112},{1,17},{17... | collective-permute-start | bytes 196616 | tf_op jit(solution)/shard_map/ppermute | solution.py:609
  6.8 5.8 %collective-permute-start.1 = (f32[16,8,128]{2,1,0:T(8,128)}, f32[16,8,128]{2,1,0:T(8,128)S(1)}, u32[]{:S(2)}, u32[]{:S(2)}) collective-permute-start(f32[16,8,128]{2,1,0:T(8,128)} %get-tuple-element.19), channel_id=1, source_target_pairs={{16,0},{32,16},{48,32},{64,48},{80,64},{96,80},{112,96},{17,1},{33... | collective-permute-start | bytes 196616 | tf_op jit(solution)/shard_map/ppermute | solution.py:609
  12.6 1.0 copy-start
  13.7 1.0 copy-start.2
  14.7 1.0 copy-start.4
  16.3 9.2 %collective-permute-start.3 = (f32[3,80,128]{2,1,0:T(8,128)S(1)}, f32[3,80,128]{2,1,0:T(8,128)S(1)}, u32[]{:S(2)}, u32[]{:S(2)}) collective-permute-start(f32[3,80,128]{2,1,0:T(8,128)S(1)} %pack_strip.1.strip_ref), channel_id=1, source_target_pairs={{1,0},{2,1},{3,2},{4,3},{5,4},{6,5},{7,6},{8,7},{9,8},{10,9},{11,1... | collective-permute-start | bytes 368648 | tf_op jit(solution)/shard_map/ppermute | solution.py:609
  17.6 7.9 %collective-permute-start.2 = (f32[3,80,128]{2,1,0:T(8,128)S(1)}, f32[3,80,128]{2,1,0:T(8,128)S(1)}, u32[]{:S(2)}, u32[]{:S(2)}) collective-permute-start(f32[3,80,128]{2,1,0:T(8,128)S(1)} %pack_strip.1.strip_ref), channel_id=1, source_target_pairs={{0,1},{1,2},{2,3},{3,4},{4,5},{5,6},{6,7},{7,8},{8,9},{9,10},{10,1... | collective-permute-start | bytes 368648 | tf_op jit(solution)/shard_map/ppermute | solution.py:609
  21.8 0.8 copy-start.8
  22.6 0.8 copy-start.10
  23.5 0.8 copy-start.11
  25.6 1.0 copy-start.1
  26.6 1.0 copy-start.3
  27.6 1.0 copy-start.5
  38.1 2.6 %copy-start.6 = (f32[12,1024,128]{2,1,0:T(8,128)}, f32[12,1024,128]{2,1,0:T(8,128)S(1)}, u32[]{:S(2)}) copy-start(f32[12,1024,128]{2,1,0:T(8,128)S(1)} %get-tuple-element.22.x_ref) | copy-start | bytes 18874372
  40.7 26.9 %all-to-all-start = ((f32[128,1,1152]{2,1,0:T(1,128)}), f32[128,1,1152]{2,1,0:T(1,128)S(1)}, u32[]{:S(2)}, u32[]{:S(2)}) async-start(f32[128,1,1152]{2,1,0:T(1,128)} %bitcast.1), calls=%async_computation | async-start | bytes 1179648 | tf_op jit(solution)/shard_map/all_to_all | solution.py:625
  53.1 2.8 %copy-start.7 = (f32[12,1024,128]{2,1,0:T(8,128)S(1)}, f32[12,1024,128]{2,1,0:T(8,128)}, u32[]{:S(2)}) copy-start(f32[12,1024,128]{2,1,0:T(8,128)} %copy-done.6) | copy-start | bytes 18874372
  55.9 51.9 %copy-start.9 = (s32[16384]{0:T(1024)S(1)}, s32[16384]{0:T(1024)}, u32[]{:S(2)}) copy-start(s32[16384]{0:T(1024)} %param.10) | copy-start | bytes 196612
  73.0 13.8 %collective-permute-start.7 = (f32[128,128]{1,0:T(8,128)S(1)}, f32[128,128]{1,0:T(8,128)S(1)}, u32[]{:S(2)}, u32[]{:S(2)}) collective-permute-start(f32[128,128]{1,0:T(8,128)S(1)} %get-tuple-element.33), channel_id=1, source_target_pairs={{1,0},{2,1},{3,2},{4,3},{5,4},{6,5},{7,6},{8,7},{9,8},{10,9},{11,1... | collective-permute-start | bytes 196616 | tf_op jit(solution)/shard_map/ppermute | solution.py:609
  74.3 12.5 %collective-permute-start.6 = (f32[128,128]{1,0:T(8,128)S(1)}, f32[128,128]{1,0:T(8,128)S(1)}, u32[]{:S(2)}, u32[]{:S(2)}) collective-permute-start(f32[128,128]{1,0:T(8,128)S(1)} %get-tuple-element.33), channel_id=1, source_target_pairs={{0,1},{1,2},{2,3},{3,4},{4,5},{5,6},{6,7},{7,8},{8,9},{9,10},{10,1... | collective-permute-start | bytes 196616 | tf_op jit(solution)/shard_map/ppermute | solution.py:609
  78.3 6.3 %collective-permute-start.4 = (f32[16,128]{1,0:T(8,128)S(1)}, f32[16,128]{1,0:T(8,128)S(1)}, u32[]{:S(2)}, u32[]{:S(2)}) collective-permute-start(f32[16,128]{1,0:T(8,128)S(1)} %get-tuple-element.31), channel_id=1, source_target_pairs={{0,16},{16,32},{32,48},{48,64},{64,80},{80,96},{96,112},{1,17},{17... | collective-permute-start | bytes 24584 | tf_op jit(solution)/shard_map/ppermute | solution.py:609
  81.8 5.0 %collective-permute-start.5 = (f32[16,128]{1,0:T(8,128)S(1)}, f32[16,128]{1,0:T(8,128)S(1)}, u32[]{:S(2)}, u32[]{:S(2)}) collective-permute-start(f32[16,128]{1,0:T(8,128)S(1)} %get-tuple-element.32), channel_id=1, source_target_pairs={{16,0},{32,16},{48,32},{64,48},{80,64},{96,80},{112,96},{17,1},{33... | collective-permute-start | bytes 24584 | tf_op jit(solution)/shard_map/ppermute | solution.py:609
  92.6 15.3 %all-to-all-start.1 = ((f32[128,2,128]{2,1,0:T(2,128)}), f32[128,2,128]{2,1,0:T(2,128)S(1)}, u32[]{:S(2)}, u32[]{:S(2)}) async-start(f32[128,2,128]{2,1,0:T(2,128)} %bitcast.5), calls=%async_computation.1 | async-start | bytes 262144 | tf_op jit(solution)/shard_map/all_to_all | solution.py:636
where the time goes:
time: 110 us; the launch traced here: 109 us
  starting transfers between devices  40.5 us (37%)
  Pallas kernels  30.2 us (27%)
  waiting for transfers between devices  20.3 us (18%)
  local copies, waits for them, and re-layouts  14.8 us (13%)
  other arithmetic  2.18 us (2%)
    ppermute x4, starting transfers between devices, exchange(): lax.ppermute(high_side, axis, forward)  16.2 us
    unnamed x24, local copies, waits for them, and re-layouts  14.2 us
    all_to_all x1, starting transfers between devices, body(): lax.all_to_all(send.reshape(devices, 1, ROWS * width), AXES, split_axis=0...  12.4 us
    pallas_call x1, Pallas kernels, flow(): pl.pallas_call(flow_kernel, out_shape=[jax.ShapeDtypeStruct(conductivity....  9.38 us
    all_to_all x1, waiting for transfers between devices, body(): lax.all_to_all(result.reshape(devices, 2, width), AXES, split_axis=0, con...  7.82 us
    ppermute x4, starting transfers between devices, exchange(): lax.ppermute(low_side, axis, backward)  6.65 us
    all_to_all x1, waiting for transfers between devices, body(): lax.all_to_all(send.reshape(devices, 1, ROWS * width), AXES, split_axis=0...  6.45 us
    ppermute x4, waiting for transfers between devices, exchange(): lax.ppermute(low_side, axis, backward)  6.03 us
  transfers between devices with their start and end apart: 10, of which 4 were waited for; matrix products, arithmetic and copies ran while one was open for 3% of the time, Pallas kernels for 6%

commit v1 on v0

--- a/solution.py
+++ b/solution.py
@@ -26,7 +26,7 @@
 
 
 def params(mib):
-    return pltpu.CompilerParams(vmem_limit_bytes=mib * 1024 * 1024)
+    return pltpu.CompilerParams(vmem_limit_bytes=int(mib * 1024 * 1024))
 
 
 def iota(shape, dim):
@@ -60,64 +60,102 @@
     return lax.axis_index("gx") * across + lax.axis_index("gy")
 
 
-def edges_kernel(k_low, k_high, s_low, s_high, r_low, r_high, east_ref, west_ref):
-    shape = k_low.shape[1:]
-    sub = iota(shape, 0)
-    for z in range(k_low.shape[0]):
+HBM = pl.BlockSpec(memory_space=pltpu.HBM)
+SMEM = pl.BlockSpec(memory_space=pltpu.SMEM)
+VMEM = pl.BlockSpec(memory_space=pltpu.VMEM)
+
+
+def fetch(pairs, sems):
+    copies = [pltpu.make_async_copy(src, dst, sems.at[i]) for i, (src, dst) in enumerate(pairs)]
+    for copy in copies:
+        copy.start()
+    return copies
+
+
+def load_kernel(
+    k_hbm, s_hbm, r_hbm, ids_hbm, conc_hbm, sorp_hbm,
+    east_ref, west_ref, k_ref, s_ref, r_ref, ids_ref, conc_ref, sorp_ref, sems,
+):
+    copies = fetch(
+        [
+            (k_hbm, k_ref),
+            (s_hbm, s_ref),
+            (r_hbm, r_ref),
+            (ids_hbm, ids_ref),
+            (conc_hbm, conc_ref),
+            (sorp_hbm, sorp_ref),
+        ],
+        sems,
+    )
+    for copy in copies:
+        copy.wait()
+    high = k_ref.shape[1] - 8
+    sub = iota(east_ref.shape[1:], 0)
+    for z in range(east_ref.shape[0]):
         east_ref[z] = jnp.where(
             sub >= 5,
-            k_high[z],
-            jnp.where(sub >= 3, roll(s_high[z], -3, 0), roll(r_high[z], -5, 0)),
+            k_ref[z, high:],
+            jnp.where(sub >= 3, roll(s_ref[z, high:], -3, 0), roll(r_ref[z, high:], -5, 0)),
         )
         west_ref[z] = jnp.where(
-            sub < 3, k_low[z], jnp.where(sub < 5, roll(s_low[z], 3, 0), roll(r_low[z], 5, 0))
+            sub < 3,
+            k_ref[z, :8],
+            jnp.where(sub < 5, roll(s_ref[z, :8], 3, 0), roll(r_ref[z, :8], 5, 0)),
         )
 
 
-def pack_edges(conductivity, storage, recharge):
-    layers, rows, width = conductivity.shape
-    low = pl.BlockSpec((layers, 8, width), lambda i: (0, 0, 0))
-    high = pl.BlockSpec((layers, 8, width), lambda i: (0, rows // 8 - 1, 0))
+def load(*arrays):
+    layers, rows, width = arrays[0].shape
     tile = jax.ShapeDtypeStruct((layers, 8, width), F32)
     return pl.pallas_call(
-        edges_kernel,
-        grid=(1,),
-        in_specs=[low, high] * 3,
-        out_specs=[pl.BlockSpec((layers, 8, width), lambda i: (0, 0, 0))] * 2,
-        out_shape=[tile, tile],
-        name="pack_edges",
-    )(conductivity, conductivity, storage, storage, recharge, recharge)
-
-
-def widened(index, z, own_ref, west_ref, east_ref):
+        load_kernel,
+        in_specs=[HBM] * 6,
+        out_specs=[VMEM] * 8,
+        out_shape=[tile, tile] + [jax.ShapeDtypeStruct(x.shape, x.dtype) for x in arrays],
+        scratch_shapes=[pltpu.SemaphoreType.DMA((6,))],
+        compiler_params=params(8),
+        name="load",
+    )(*(pltpu.with_memory_space_constraint(x, pltpu.HBM) for x in arrays))
+
+
+def beside(index, z, west_ref, east_ref):
     shift = (0, 3, 5)[index]
     top, bottom = west_ref[z], east_ref[z]
     if shift:
         top, bottom = roll(top, shift, 0), roll(bottom, -shift, 0)
+    return top, bottom
+
+
+def widened(index, z, own_ref, west_ref, east_ref):
+    top, bottom = beside(index, z, west_ref, east_ref)
     return jnp.concatenate([top, own_ref[z], bottom], 0)
 
 
-def strip_kernel(k_ref, s_ref, r_ref, west_ref, east_ref, out_ref):
-    layers = k_ref.shape[0]
-    for index, own in enumerate((k_ref, s_ref, r_ref)):
-        strip = None
-        for z in range(layers):
-            wide = roll(widened(index, z, own, west_ref, east_ref), z * 8 + 4, 1)
-            if strip is None:
-                strip = wide
-            else:
-                strip = jnp.where(iota(wide.shape, 1) >= z * 8, wide, strip)
-        out_ref[index] = strip
-
-
-def pack_strip(conductivity, storage, recharge, west, east):
-    layers, rows, width = conductivity.shape
+def strip_of(layers, layer):
+    strip = None
+    for z in range(layers):
+        turned = roll(layer(z), z * 8 + 4, 1)
+        strip = turned if strip is None else jnp.where(iota(turned.shape, 1) >= z * 8, turned, strip)
+    return strip
+
+
+def strip_kernel(inner_ref, west_ref, east_ref, out_ref):
+    layers = west_ref.shape[0]
+    rows = inner_ref.shape[1]
+    for index in range(3):
+        out_ref[index, 8 : 8 + rows] = inner_ref[index]
+        out_ref[index, 0:8] = strip_of(layers, lambda z: beside(index, z, west_ref, east_ref)[0])
+        out_ref[index, 8 + rows :] = strip_of(layers, lambda z: beside(index, z, west_ref, east_ref)[1])
+
+
+def pack_strip(inner, west, east):
+    rows, width = inner.shape[1:]
     return pl.pallas_call(
         strip_kernel,
         out_shape=jax.ShapeDtypeStruct((3, rows + 16, width), F32),
-        compiler_params=params(16),
+        compiler_params=params(4),
         name="pack_strip",
-    )(conductivity, storage, recharge, west, east)
+    )(inner, west, east)
 
 
 def column(row):
@@ -130,7 +168,10 @@
     return jnp.sum(jnp.where(iota((n, n), 0) == iota((n, n), 1), col, 0.0), 0, keepdims=True)
 
 
-def send_kernel(down, across, rows_x, layers, ids_ref, conc_ref, sorp_ref, out_ref, col_ref, row_ref):
+def prepare_kernel(
+    down, across, k_ref, s_ref, r_ref, ids_ref, conc_ref, sorp_ref, inner_ref, out_ref, col_ref, row_ref
+):
+    layers, rows_x = k_ref.shape[:2]
     devices, owned = ids_ref.shape
     lines = layers * rows_x
     me = place()
@@ -196,24 +237,25 @@
         south = (dest == own_brick - 1) & ranked & (own_brick % across > 0)
         misc = misc + pick(north, split(tails)) + pick(south, split(heads))
     out_ref[pl.ds(8, devices, stride=ROWS), :] = misc
-
-
-def pack_send(ids, concentration, sorption, layers, rows_x):
+    for index, ref in enumerate((k_ref, s_ref, r_ref)):
+        inner_ref[index] = strip_of(layers, lambda z: ref[z])
+
+
+def prepare(conductivity, storage, recharge, ids, concentration, sorption):
     devices, owned = ids.shape
-    width = concentration.shape[1]
-    kernel = functools.partial(
-        send_kernel, lax.axis_size("gx"), lax.axis_size("gy"), rows_x, layers
-    )
+    layers, rows_x, width = conductivity.shape
+    kernel = functools.partial(prepare_kernel, lax.axis_size("gx"), lax.axis_size("gy"))
     return pl.pallas_call(
         kernel,
         out_shape=[
+            jax.ShapeDtypeStruct((3, rows_x, width), F32),
             jax.ShapeDtypeStruct((devices * ROWS, width), F32),
             jax.ShapeDtypeStruct((devices, 128), jnp.int32),
             jax.ShapeDtypeStruct((16, devices), jnp.int32),
         ],
-        compiler_params=params(16),
-        name="pack_send",
-    )(ids, concentration, sorption)
+        compiler_params=params(8),
+        name="prepare",
+    )(conductivity, storage, recharge, ids, concentration, sorption)
 
 
 def harmonic(a, c):
@@ -221,9 +263,9 @@
 
 
 def flow_kernel(
-    k_ref, s_ref, r_ref, west_ref, east_ref, strip_ref, south_ref, north_ref, send_ref,
-    d_out, w_out, x_out, send_out,
-    kx, sx, fw, fs, fb, rd, dd, ww,
+    k_ref, s_ref, r_ref, west_ref, east_ref, strip_ref, south_ref, north_ref, send_ref, slots_ref,
+    d_out, w_out, gath_out, send_out,
+    kx, sx, fw, fs, fb, rd, dd, ww, lines_ref,
 ):
     layers, rows, width = k_ref.shape
     tall = rows + 16
@@ -275,7 +317,7 @@
         kx[z] = widened(0, z, k_ref, west_ref, east_ref)
         return carry
 
-    lax.fori_loop(0, layers, widen, 0)
+    lax.fori_loop(0, layers, widen, 0, unroll=4)
     fb[0] = jnp.zeros(shape, F32)
 
     def faces(z, carry):
@@ -297,7 +339,7 @@
         sx[z] = s
         return carry
 
-    lax.fori_loop(0, layers, faces, 0)
+    lax.fori_loop(0, layers, faces, 0, unroll=2)
 
     def total(x):
         return jnp.sum(x[8 : 8 + rows].reshape(rows // 8, 8, width), 0)
@@ -313,7 +355,8 @@
         flux_s = with_low(z, fs[z] * (roll(h, 1, 1) - h), low)
         flux_n = north_of(z, flux_s, high)
         for at, flux in enumerate((flux_w, flux_e, flux_b, flux_a, flux_s, flux_n)):
-            x_out[block + at, pl.ds(pl.multiple_of(z * rows, rows), rows), :] = flux[8 : 8 + rows]
+            start = z * (rows * 16) + (block + at)
+            lines_ref[pl.ds(start, rows, stride=16), :] = flux[8 : 8 + rows]
         return h, sx[z] * h + (flux_e - flux_w) + (flux_a - flux_b) + (flux_n - flux_s)
 
     zero = jnp.zeros((8, width), F32)
@@ -328,22 +371,31 @@
         gamma = jnp.sum((r * d[8 : 8 + rows]).reshape(rows // 8, 8, width), 0)
         return sums[0] + gamma, sums[1] + total(d * image), sums[2] + total(image * w)
 
-    gamma, bend, curve = lax.fori_loop(0, layers, first, (zero, zero, zero))
+    gamma, bend, curve = lax.fori_loop(0, layers, first, (zero, zero, zero), unroll=2)
 
     def second(z, acc):
         w, image = apply(z, ww, low_w, high_w, 6)
         return acc + total(w * image)
 
-    twist = lax.fori_loop(0, layers, second, zero)
+    twist = lax.fori_loop(0, layers, second, zero, unroll=2)
     lane_row = iota((devices, width), 1)
     misc = send_ref[pl.ds(8, devices, stride=ROWS), :]
     for at, part in enumerate((gamma, bend, curve, twist)):
         value = jnp.sum(jnp.sum(part, 0, keepdims=True), 1, keepdims=True)
         misc = jnp.where(lane_row == 8 + at, value, misc)
     send_out[pl.ds(8, devices, stride=ROWS), :] = misc
-
-
-def flow(conductivity, storage, recharge, west, east, strip, south, north, send):
+    for k in range(2):
+
+        def gather(i, carry):
+            line = pl.multiple_of(jnp.maximum(slots_ref[k, i], 0) * 16, 16)
+            slot = pl.multiple_of((k * devices + i) * 16, 16)
+            gath_out[pl.ds(slot, 16), :] = lines_ref[pl.ds(line, 16), :]
+            return carry
+
+        lax.fori_loop(0, devices, gather, 0, unroll=8)
+
+
+def flow(conductivity, storage, recharge, west, east, strip, south, north, send, slots):
     layers, rows, width = conductivity.shape
     tall = pltpu.VMEM((layers, rows + 16, width), F32)
     return pl.pallas_call(
@@ -351,37 +403,18 @@
         out_shape=[
             jax.ShapeDtypeStruct(conductivity.shape, F32),
             jax.ShapeDtypeStruct(conductivity.shape, F32),
-            jax.ShapeDtypeStruct((12, layers * rows, width), F32),
+            jax.ShapeDtypeStruct((2 * slots.shape[1] * 16, width), F32),
             jax.ShapeDtypeStruct(send.shape, F32),
         ],
+        in_specs=[VMEM] * 9 + [SMEM],
+        out_specs=[VMEM] * 4,
         scratch_shapes=[tall] * 4
         + [pltpu.VMEM((layers + 1, rows + 16, width), F32)]
-        + [tall] * 3,
-        compiler_params=params(28),
+        + [tall] * 3
+        + [pltpu.VMEM((layers * rows * 16, width), F32)],
+        compiler_params=params(30),
         name="flow",
-    )(conductivity, storage, recharge, west, east, strip, south, north, send)
-
-
-def gather_kernel(x_ref, col_ref, out_ref):
-    lines = x_ref.shape[1]
-    cols = col_ref[...]
-    own = jnp.concatenate([cols[:, 0:1], cols[:, 1:2]], 0)
-    mask = own == iota((own.shape[0], lines), 1)
-    chosen = jnp.where(mask, 1.0, 0.0).astype(BF16)
-    for at in range(x_ref.shape[0]):
-        parts = split(x_ref[at])
-        high, middle, low = (jnp.dot(chosen, part, preferred_element_type=F32) for part in parts)
-        out_ref[at] = (low + middle) + high
-
-
-def gather_fluxes(fluxes, cols):
-    count, lines, width = fluxes.shape
-    return pl.pallas_call(
-        gather_kernel,
-        out_shape=jax.ShapeDtypeStruct((count, 2 * cols.shape[0], width), F32),
-        compiler_params=params(28),
-        name="gather_fluxes",
-    )(fluxes, cols)
+    )(conductivity, storage, recharge, west, east, strip, south, north, send, slots)
 
 
 def minmod(a, d):
@@ -517,7 +550,9 @@
     east_edge = pick(layer == east_codes, split(jnp.concatenate([received(6), received(7)], 0)))
     fluxes = []
     for i in range(6):
-        flux = on_d * gath_ref[i] + on_w * gath_ref[6 + i]
+        slots = 2 * devices
+        flux = on_d * gath_ref[pl.ds(i, slots, stride=16), :]
+        flux = flux + on_w * gath_ref[pl.ds(6 + i, slots, stride=16), :]
         flux_out[i] = flux
         fluxes.append(flux)
     beside = neighbour_values(c, cols, rows, west_edge, east_edge, misc, misc, rows_x)
@@ -614,18 +649,19 @@
     devices = lax.axis_size(AXES)
     owned = concentration.shape[0]
     ids = block_ids.reshape(devices, owned)
-    to_east, to_west = pack_edges(conductivity, storage, recharge)
+    to_east, to_west, conductivity, storage, recharge, ids, concentration, sorption = load(
+        conductivity, storage, recharge, ids, concentration, sorption
+    )
     west, east = exchange(to_west, to_east, "gx")
-    send, cols, rows = pack_send(ids, concentration, sorption, layers, rows_x)
-    strip = pack_strip(conductivity, storage, recharge, west, east)
+    inner, send, cols, rows = prepare(conductivity, storage, recharge, ids, concentration, sorption)
+    strip = pack_strip(inner, west, east)
     south, north = exchange(strip, strip, "gy")
-    base, image, fluxes, send = flow(
-        conductivity, storage, recharge, west, east, strip, south, north, send
+    base, image, gathered, send = flow(
+        conductivity, storage, recharge, west, east, strip, south, north, send, rows[:2]
     )
     received = lax.all_to_all(
         send.reshape(devices, 1, ROWS * width), AXES, split_axis=0, concat_axis=0, tiled=True
     ).reshape(devices * ROWS, width)
-    gathered = gather_fluxes(fluxes, cols)
     c, s, flux, to_east, to_west, misc, scal = first_step(
         received, gathered, cols, rows, layers, rows_x
     )

time: 110 us -> 97.6 us (0.89)
  blocking collectives: 0 us -> 28.4 us
  local copies, waits for them, and re-layouts: 14.8 us -> 0.62 us
  starting transfers between devices: 40.5 us -> 28.1 us
  Pallas kernels: 30.2 us -> 22.9 us
  waiting for transfers between devices: 20.3 us -> 14.2 us
    all_to_all x0 -> x1, blocking collectives: none -> 28.4 us  [body(): lax.all_to_all(send.reshape(devices, 1, ROWS * width), AXES, split_axis=0...]
    unnamed x24 -> x0, local copies, waits for them, and re-layouts: 14.2 us -> none
    all_to_all x1 -> x0, starting transfers between devices: 12.4 us -> none  [body(): lax.all_to_all(send.reshape(devices, 1, ROWS * width), AXES, split_axis=0...]
    all_to_all x1 -> x0, waiting for transfers between devices: 6.45 us -> none  [body(): lax.all_to_all(send.reshape(devices, 1, ROWS * width), AXES, split_axis=0...]
    pallas_call x3 -> x2, Pallas kernels: 8.18 us -> 2.8 us  [the longest x1 1.44 us: load(): pl.pallas_call(load_kernel, in_specs=[HBM] * 6, out_specs=[VMEM] * 8, out...]
    pallas_call x1, Pallas kernels: 9.38 us -> 7.35 us  [flow(): pl.pallas_call(flow_kernel, out_shape=[jax.ShapeDtypeStruct(conductivity....]
    ppermute x4, waiting for transfers between devices: 0.01 us -> 1.53 us  [exchange(): lax.ppermute(high_side, axis, forward)]
    ppermute x4, waiting for transfers between devices: 6.03 us -> 4.84 us  [exchange(): lax.ppermute(low_side, axis, backward)]
  transfers between devices with their start and end apart: 10 -> 9, of which waited for: 4 -> 5; matrix products, arithmetic and copies ran while one was open for 3% -> 3% of each run, Pallas kernels for 6% -> 1%
where the time goes in v1:
time: 97.6 us; the launch traced here: 97.2 us
  blocking collectives  28.4 us (29%)
  starting transfers between devices  28.1 us (29%)
  Pallas kernels  22.9 us (23%)
  waiting for transfers between devices  14.2 us (15%)
  other arithmetic  2.14 us (2%)
    all_to_all x1, blocking collectives, body(): lax.all_to_all(send.reshape(devices, 1, ROWS * width), AXES, split_axis=0...  28.4 us
    ppermute x4, starting transfers between devices, exchange(): lax.ppermute(high_side, axis, forward)  16.2 us
    all_to_all x1, waiting for transfers between devices, body(): lax.all_to_all(result.reshape(devices, 2, width), AXES, split_axis=0, con...  7.86 us
    pallas_call x1, Pallas kernels, flow(): pl.pallas_call(flow_kernel, out_shape=[jax.ShapeDtypeStruct(conductivity....  7.35 us
    ppermute x4, starting transfers between devices, exchange(): lax.ppermute(low_side, axis, backward)  6.61 us
    pallas_call x1, Pallas kernels, first_step(): pl.pallas_call(functools.partial(first_kernel, rows_x), out_shape=[lines,...  5.83 us
    pallas_call x1, Pallas kernels, second_step(): pl.pallas_call(functools.partial(second_kernel, rows_x), out_shape=jax.Sh...  5.8 us
    all_to_all x1, starting transfers between devices, body(): lax.all_to_all(result.reshape(devices, 2, width), AXES, split_axis=0, con...  5.26 us
  transfers between devices with their start and end apart: 9, of which 5 were waited for; matrix products, arithmetic and copies ran while one was open for 3% of the time, Pallas kernels for 1%

profile of v1, /device:TPU:1, one launch (start us, length us, event | category | flops | bytes accessed | tf_op | source)
XLA Modules:
  0.0 97.2 jit_solution(9431234406246290703)
XLA Ops:
  0.6 1.4 %load.1 = (f32[16,8,128]{2,1,0:T(8,128)S(1)}, f32[16,8,128]{2,1,0:T(8,128)S(1)}, f32[16,64,128]{2,1,0:T(8,128)S(1)}, f32[16,64,128]{2,1,0:T(8,128)S(1)}, f32[16,...) custom-call(f32[16,64,128]{2,1,0:T(8,128)} %k_hbm.1, ...), custom_call_target="tpu_custom_call" | custom-call | tf_op jit(solution)/shard_map/load/pallas_call | solution.py:110
  2.1 4.5 %collective-permute-start = (f32[16,8,128]{2,1,0:T(8,128)S(1)}, f32[16,8,128]{2,1,0:T(8,128)S(1)}, u32[]{:S(2)}, u32[]{:S(2)}) collective-permute-start(f32[16,8,128]{2,1,0:T(8,128)S(1)} %get-tuple-element.28), channel_id=1, source_target_pairs={{0,16},{16,32},{32,48},{48,64},{64,80},{80,96},{96,112},{1,17},{17... | collective-permute-start | bytes 196616 | tf_op jit(solution)/shard_map/ppermute | solution.py:644
  6.6 1.9 %collective-permute-start.1 = (f32[16,8,128]{2,1,0:T(8,128)S(1)}, f32[16,8,128]{2,1,0:T(8,128)S(1)}, u32[]{:S(2)}, u32[]{:S(2)}) collective-permute-start(f32[16,8,128]{2,1,0:T(8,128)S(1)} %get-tuple-element.29), channel_id=1, source_target_pairs={{16,0},{32,16},{48,32},{64,48},{80,64},{96,80},{112,96},{17,1},{33... | collective-permute-start | bytes 196616 | tf_op jit(solution)/shard_map/ppermute | solution.py:644
  8.5 1.4 %prepare.1 = (f32[3,64,128]{2,1,0:T(8,128)S(1)}, f32[1152,128]{1,0:T(8,128)S(1)}, s32[128,128]{1,0:T(8,128)S(1)}, s32[16,128]{1,0:T(8,128)S(1)}) custom-call(f32[16,64,128]{2,1,0:T(8,128)S(1)} %get-tuple-element.25.k_ref, f32[16,64,128]{2,1,0:T(8,128)S(1)} %get-tuple-element.26.s_ref, f32[16,64,128]{2,1,0:T(8,128)S(1)} %get-tuple-element.27.r_ref, ...), custom_call_target="tpu_custom_call" | custom-call | tf_op jit(solution)/shard_map/prepare/pallas_call | solution.py:248
  9.9 0.0 collective-permute-done.west_ref
  9.9 2.3 %collective-permute-done.1.east_ref = f32[16,8,128]{2,1,0:T(8,128)S(1)} collective-permute-done((f32[16,8,128]{2,1,0:T(8,128)S(1)}, f32[16,8,128]{2,1,0:T(8,128)S(1)}, u32[]{:S(2)}, u32[]{:S(2)}) %collective-permute-start.1) | collective-permute-done | bytes 65568 | tf_op jit(solution)/shard_map/ppermute | solution.py:644
  12.2 0.2 pack_strip.1.strip_ref
  12.3 1.3 %collective-permute-start.3 = (f32[3,80,128]{2,1,0:T(8,128)S(1)}, f32[3,80,128]{2,1,0:T(8,128)S(1)}, u32[]{:S(2)}, u32[]{:S(2)}) collective-permute-start(f32[3,80,128]{2,1,0:T(8,128)S(1)} %pack_strip.1.strip_ref), channel_id=1, source_target_pairs={{1,0},{2,1},{3,2},{4,3},{5,4},{6,5},{7,6},{8,7},{9,8},{10,9},{11,1... | collective-permute-start | bytes 368648 | tf_op jit(solution)/shard_map/ppermute | solution.py:644
  13.6 4.2 %collective-permute-start.2 = (f32[3,80,128]{2,1,0:T(8,128)S(1)}, f32[3,80,128]{2,1,0:T(8,128)S(1)}, u32[]{:S(2)}, u32[]{:S(2)}) collective-permute-start(f32[3,80,128]{2,1,0:T(8,128)S(1)} %pack_strip.1.strip_ref), channel_id=1, source_target_pairs={{0,1},{1,2},{2,3},{3,4},{4,5},{5,6},{6,7},{7,8},{8,9},{9,10},{10,1... | collective-permute-start | bytes 368648 | tf_op jit(solution)/shard_map/ppermute | solution.py:644
  17.8 0.3 collective-permute-done.3.north_ref
  18.2 1.5 %collective-permute-done.2.south_ref = f32[3,80,128]{2,1,0:T(8,128)S(1)} collective-permute-done((f32[3,80,128]{2,1,0:T(8,128)S(1)}, f32[3,80,128]{2,1,0:T(8,128)S(1)}, u32[]{:S(2)}, u32[]{:S(2)}) %collective-permute-start.2) | collective-permute-done | bytes 122912 | tf_op jit(solution)/shard_map/ppermute | solution.py:644
  19.7 7.4 %flow.1 = (f32[16,64,128]{2,1,0:T(8,128)S(1)}, f32[16,64,128]{2,1,0:T(8,128)S(1)}, f32[4096,128]{1,0:T(8,128)S(1)}, f32[1152,128]{1,0:T(8,128)S(1)}) custom-call(f32[16,64,128]{2,1,0:T(8,128)S(1)} %get-tuple-element.25.k_ref, f32[16,64,128]{2,1,0:T(8,128)S(1)} %get-tuple-element.26.s_ref, f32[16,64,128]{2,1,0:T(8,128)S(1)} %get-tuple-element.27.r_ref, ...), custom_call_target="tpu_custom_call" | custom-call | tf_op jit(solution)/shard_map/flow/pallas_call | solution.py:401
  27.0 28.4 %all_to_all.10 = f32[128,1,1152]{2,1,0:T(1,128)S(1)} all-to-all(f32[128,1,1152]{2,1,0:T(1,128)S(1)} %bitcast.8), channel_id=1, replica_groups=mesh['gx'=8,'gy'=16] {'gx','gy'}, dimensions={0} | all-to-all | bytes 1179648 | tf_op jit(solution)/shard_map/all_to_all | solution.py:662
  55.5 5.8 %first_step.1 = (f32[256,128]{1,0:T(8,128)S(1)}, f32[256,128]{1,0:T(8,128)S(1)}, f32[6,256,128]{2,1,0:T(8,128)S(1)}, f32[16,128]{1,0:T(8,128)S(1)}, f32[16,128]{...) custom-call(f32[1152,128]{1,0:T(8,128)S(1)} %bitcast.7, f32[4096,128]{1,0:T(8,128)S(1)} %get-tuple-element.37.gath_ref, ...), custom_call_target="tpu_custom_call" | custom-call | tf_op jit(solution)/shard_map/first_step/pallas_call | solution.py:581
  61.3 1.3 %collective-permute-start.7 = (f32[128,128]{1,0:T(8,128)S(1)}, f32[128,128]{1,0:T(8,128)S(1)}, u32[]{:S(2)}, u32[]{:S(2)}) collective-permute-start(f32[128,128]{1,0:T(8,128)S(1)} %get-tuple-element.47), channel_id=1, source_target_pairs={{1,0},{2,1},{3,2},{4,3},{5,4},{6,5},{7,6},{8,7},{9,8},{10,9},{11,1... | collective-permute-start | bytes 196616 | tf_op jit(solution)/shard_map/ppermute | solution.py:644
  62.6 4.0 %collective-permute-start.6 = (f32[128,128]{1,0:T(8,128)S(1)}, f32[128,128]{1,0:T(8,128)S(1)}, u32[]{:S(2)}, u32[]{:S(2)}) collective-permute-start(f32[128,128]{1,0:T(8,128)S(1)} %get-tuple-element.47), channel_id=1, source_target_pairs={{0,1},{1,2},{2,3},{3,4},{4,5},{5,6},{6,7},{7,8},{8,9},{9,10},{10,1... | collective-permute-start | bytes 196616 | tf_op jit(solution)/shard_map/ppermute | solution.py:644
  66.6 3.5 %collective-permute-start.4 = (f32[16,128]{1,0:T(8,128)S(1)}, f32[16,128]{1,0:T(8,128)S(1)}, u32[]{:S(2)}, u32[]{:S(2)}) collective-permute-start(f32[16,128]{1,0:T(8,128)S(1)} %get-tuple-element.45), channel_id=1, source_target_pairs={{0,16},{16,32},{32,48},{48,64},{64,80},{80,96},{96,112},{1,17},{17... | collective-permute-start | bytes 24584 | tf_op jit(solution)/shard_map/ppermute | solution.py:644
  70.2 2.1 %collective-permute-start.5 = (f32[16,128]{1,0:T(8,128)S(1)}, f32[16,128]{1,0:T(8,128)S(1)}, u32[]{:S(2)}, u32[]{:S(2)}) collective-permute-start(f32[16,128]{1,0:T(8,128)S(1)} %get-tuple-element.46), channel_id=1, source_target_pairs={{16,0},{32,16},{48,32},{64,48},{80,64},{96,80},{112,96},{17,1},{33... | collective-permute-start | bytes 24584 | tf_op jit(solution)/shard_map/ppermute | solution.py:644
  72.3 0.6 fusion
  72.9 0.0 collective-permute-done.4.west_ref
  72.9 2.2 %collective-permute-done.5.east_ref = f32[16,128]{1,0:T(8,128)S(1)} collective-permute-done((f32[16,128]{1,0:T(8,128)S(1)}, f32[16,128]{1,0:T(8,128)S(1)}, u32[]{:S(2)}, u32[]{:S(2)}) %collective-permute-start.5) | collective-permute-done | bytes 8224 | tf_op jit(solution)/shard_map/ppermute | solution.py:644
  75.1 0.0 collective-permute-done.7.north_ref
  75.1 0.0 collective-permute-done.6.south_ref
  75.1 5.8 %second_step.1 = f32[256,128]{1,0:T(8,128)} custom-call(f32[256,128]{1,0:T(8,128)S(1)} %get-tuple-element.42.c_ref, f32[256,128]{1,0:T(8,128)S(1)} %get-tuple-element.43.s_ref, f32[6,256,128]{2,1,0:T(8,128)S(1)} %get-tuple-element.44.flux_ref, s32[128,128]{1,0:T(8,128)S(1)} %get-tuple-element.38.col_ref, s32[16,128]{1,0:T(8,128)S(1)} %get-tuple-element.35.row_ref, ...), custom_call_target="tpu_custom_call" | custom-call | tf_op jit(solution)/shard_map/second_step/pallas_call | solution.py:611
  80.9 5.3 %all-to-all-start.1 = ((f32[128,2,128]{2,1,0:T(2,128)}), f32[128,2,128]{2,1,0:T(2,128)S(1)}, u32[]{:S(2)}, u32[]{:S(2)}) async-start(f32[128,2,128]{2,1,0:T(2,128)} %bitcast.5), calls=%async_computation.1 | async-start | bytes 262144 | tf_op jit(solution)/shard_map/all_to_all | solution.py:672
  86.2 2.1 %multiply_add_fusion = f32[16,64,128]{2,1,0:T(8,128)} fusion(f32[16,64,128]{2,1,0:T(8,128)S(1)} %get-tuple-element.41, f32[16,64,128]{2,1,0:T(8,128)S(1)} %get-tuple-element.40, f32[]{:T(128)} %bitcast.4, f32[]{:T(128)} %bitcast.3), kind=kLoop, calls=%fused_computation | loop fusion | flops 393216 | bytes 1572872 | tf_op jit(solution)/shard_map/add | solution.py:670
  88.3 7.9 %all-to-all-done.1 = f32[128,2,128]{2,1,0:T(2,128)S(1)} async-done(((f32[128,2,128]{2,1,0:T(2,128)}), f32[128,2,128]{2,1,0:T(2,128)S(1)}, u32[]{:S(2)}, u32[]{:S(2)}) %all-to-all-start.1) | async-done | bytes 131104 | tf_op jit(solution)/shard_map/all_to_all | solution.py:672
  96.2 1.0 %to_owner.1 = f32[128,128]{1,0:T(8,128)} custom-call(s32[128,128]{1,0:T(8,128)S(1)} %get-tuple-element.30.ids_ref, f32[256,128]{1,0:T(8,128)S(1)} %bitcast.9), custom_call_target="tpu_custom_call" | custom-call | tf_op jit(solution)/shard_map/to_owner/pallas_call | solution.py:632
  (1 shorter events, 0.0 us)
Async XLA Ops:
  2.1 7.8 %collective-permute-start = (f32[16,8,128]{2,1,0:T(8,128)S(1)}, f32[16,8,128]{2,1,0:T(8,128)S(1)}, u32[]{:S(2)}, u32[]{:S(2)}) collective-permute-start(f32[16,8,128]{2,1,0:T(8,128)S(1)} %get-tuple-element.28), channel_id=1, source_target_pairs={{0,16},{16,32},{32,48},{48,64},{64,80},{80,96},{96,112},{1,17},{17... | collective-permute-start | bytes 196616 | tf_op jit(solution)/shard_map/ppermute | solution.py:644
  6.6 5.6 %collective-permute-start.1 = (f32[16,8,128]{2,1,0:T(8,128)S(1)}, f32[16,8,128]{2,1,0:T(8,128)S(1)}, u32[]{:S(2)}, u32[]{:S(2)}) collective-permute-start(f32[16,8,128]{2,1,0:T(8,128)S(1)} %get-tuple-element.29), channel_id=1, source_target_pairs={{16,0},{32,16},{48,32},{64,48},{80,64},{96,80},{112,96},{17,1},{33... | collective-permute-start | bytes 196616 | tf_op jit(solution)/shard_map/ppermute | solution.py:644
  12.3 5.8 %collective-permute-start.3 = (f32[3,80,128]{2,1,0:T(8,128)S(1)}, f32[3,80,128]{2,1,0:T(8,128)S(1)}, u32[]{:S(2)}, u32[]{:S(2)}) collective-permute-start(f32[3,80,128]{2,1,0:T(8,128)S(1)} %pack_strip.1.strip_ref), channel_id=1, source_target_pairs={{1,0},{2,1},{3,2},{4,3},{5,4},{6,5},{7,6},{8,7},{9,8},{10,9},{11,1... | collective-permute-start | bytes 368648 | tf_op jit(solution)/shard_map/ppermute | solution.py:644
  13.6 6.0 %collective-permute-start.2 = (f32[3,80,128]{2,1,0:T(8,128)S(1)}, f32[3,80,128]{2,1,0:T(8,128)S(1)}, u32[]{:S(2)}, u32[]{:S(2)}) collective-permute-start(f32[3,80,128]{2,1,0:T(8,128)S(1)} %pack_strip.1.strip_ref), channel_id=1, source_target_pairs={{0,1},{1,2},{2,3},{3,4},{4,5},{5,6},{6,7},{7,8},{8,9},{9,10},{10,1... | collective-permute-start | bytes 368648 | tf_op jit(solution)/shard_map/ppermute | solution.py:644
  61.3 13.8 %collective-permute-start.7 = (f32[128,128]{1,0:T(8,128)S(1)}, f32[128,128]{1,0:T(8,128)S(1)}, u32[]{:S(2)}, u32[]{:S(2)}) collective-permute-start(f32[128,128]{1,0:T(8,128)S(1)} %get-tuple-element.47), channel_id=1, source_target_pairs={{1,0},{2,1},{3,2},{4,3},{5,4},{6,5},{7,6},{8,7},{9,8},{10,9},{11,1... | collective-permute-start | bytes 196616 | tf_op jit(solution)/shard_map/ppermute | solution.py:644
  62.6 12.5 %collective-permute-start.6 = (f32[128,128]{1,0:T(8,128)S(1)}, f32[128,128]{1,0:T(8,128)S(1)}, u32[]{:S(2)}, u32[]{:S(2)}) collective-permute-start(f32[128,128]{1,0:T(8,128)S(1)} %get-tuple-element.47), channel_id=1, source_target_pairs={{0,1},{1,2},{2,3},{3,4},{4,5},{5,6},{6,7},{7,8},{8,9},{9,10},{10,1... | collective-permute-start | bytes 196616 | tf_op jit(solution)/shard_map/ppermute | solution.py:644
  66.6 6.3 %collective-permute-start.4 = (f32[16,128]{1,0:T(8,128)S(1)}, f32[16,128]{1,0:T(8,128)S(1)}, u32[]{:S(2)}, u32[]{:S(2)}) collective-permute-start(f32[16,128]{1,0:T(8,128)S(1)} %get-tuple-element.45), channel_id=1, source_target_pairs={{0,16},{16,32},{32,48},{48,64},{64,80},{80,96},{96,112},{1,17},{17... | collective-permute-start | bytes 24584 | tf_op jit(solution)/shard_map/ppermute | solution.py:644
  70.2 5.0 %collective-permute-start.5 = (f32[16,128]{1,0:T(8,128)S(1)}, f32[16,128]{1,0:T(8,128)S(1)}, u32[]{:S(2)}, u32[]{:S(2)}) collective-permute-start(f32[16,128]{1,0:T(8,128)S(1)} %get-tuple-element.46), channel_id=1, source_target_pairs={{16,0},{32,16},{48,32},{64,48},{80,64},{96,80},{112,96},{17,1},{33... | collective-permute-start | bytes 24584 | tf_op jit(solution)/shard_map/ppermute | solution.py:644
  80.9 15.3 %all-to-all-start.1 = ((f32[128,2,128]{2,1,0:T(2,128)}), f32[128,2,128]{2,1,0:T(2,128)S(1)}, u32[]{:S(2)}, u32[]{:S(2)}) async-start(f32[128,2,128]{2,1,0:T(2,128)} %bitcast.5), calls=%async_computation.1 | async-start | bytes 262144 | tf_op jit(solution)/shard_map/all_to_all | solution.py:672

commit v2 on v1

--- a/solution.py
+++ b/solution.py
@@ -60,6 +60,26 @@
     return lax.axis_index("gx") * across + lax.axis_index("gy")
 
 
+def by_turns(axis, low, high):
+    odd = jnp.full(low.shape, lax.axis_index(axis) % 2) == 1
+    return jnp.where(odd, low, high), jnp.where(odd, high, low)
+
+
+def from_turns(axis, first, second):
+    at = jnp.full(first.shape, lax.axis_index(axis))
+    odd = at % 2 == 1
+    low = jnp.where(at == 0, 0.0, jnp.where(odd, first, second))
+    high = jnp.where(at == lax.axis_size(axis) - 1, 0.0, jnp.where(odd, second, first))
+    return low, high
+
+
+def swap(axis, first, second):
+    count = lax.axis_size(axis)
+    one = [(i, i ^ 1) for i in range(count)]
+    other = [(i, (i + 1 if i % 2 else i - 1) % count) for i in range(count)]
+    return lax.ppermute(first, axis, one), lax.ppermute(second, axis, other)
+
+
 HBM = pl.BlockSpec(memory_space=pltpu.HBM)
 SMEM = pl.BlockSpec(memory_space=pltpu.SMEM)
 VMEM = pl.BlockSpec(memory_space=pltpu.VMEM)
@@ -74,7 +94,7 @@
 
 def load_kernel(
     k_hbm, s_hbm, r_hbm, ids_hbm, conc_hbm, sorp_hbm,
-    east_ref, west_ref, k_ref, s_ref, r_ref, ids_ref, conc_ref, sorp_ref, sems,
+    first_ref, second_ref, k_ref, s_ref, r_ref, ids_ref, conc_ref, sorp_ref, sems,
 ):
     copies = fetch(
         [
@@ -90,18 +110,19 @@
     for copy in copies:
         copy.wait()
     high = k_ref.shape[1] - 8
-    sub = iota(east_ref.shape[1:], 0)
-    for z in range(east_ref.shape[0]):
-        east_ref[z] = jnp.where(
+    sub = iota(first_ref.shape[1:], 0)
+    for z in range(first_ref.shape[0]):
+        east = jnp.where(
             sub >= 5,
             k_ref[z, high:],
             jnp.where(sub >= 3, roll(s_ref[z, high:], -3, 0), roll(r_ref[z, high:], -5, 0)),
         )
-        west_ref[z] = jnp.where(
+        west = jnp.where(
             sub < 3,
             k_ref[z, :8],
             jnp.where(sub < 5, roll(s_ref[z, :8], 3, 0), roll(r_ref[z, :8], 5, 0)),
         )
+        first_ref[z], second_ref[z] = by_turns("gx", west, east)
 
 
 def load(*arrays):
@@ -139,8 +160,9 @@
     return strip
 
 
-def strip_kernel(inner_ref, west_ref, east_ref, out_ref):
+def strip_kernel(inner_ref, first_ref, second_ref, out_ref, west_ref, east_ref):
     layers = west_ref.shape[0]
+    west_ref[...], east_ref[...] = from_turns("gx", first_ref[...], second_ref[...])
     rows = inner_ref.shape[1]
     for index in range(3):
         out_ref[index, 8 : 8 + rows] = inner_ref[index]
@@ -148,14 +170,15 @@
         out_ref[index, 8 + rows :] = strip_of(layers, lambda z: beside(index, z, west_ref, east_ref)[1])
 
 
-def pack_strip(inner, west, east):
+def pack_strip(inner, first, second):
     rows, width = inner.shape[1:]
+    tile = jax.ShapeDtypeStruct(first.shape, F32)
     return pl.pallas_call(
         strip_kernel,
-        out_shape=jax.ShapeDtypeStruct((3, rows + 16, width), F32),
+        out_shape=[jax.ShapeDtypeStruct((3, rows + 16, width), F32), tile, tile],
         compiler_params=params(4),
         name="pack_strip",
-    )(inner, west, east)
+    )(inner, first, second)
 
 
 def column(row):
@@ -263,7 +286,7 @@
 
 
 def flow_kernel(
-    k_ref, s_ref, r_ref, west_ref, east_ref, strip_ref, south_ref, north_ref, send_ref, slots_ref,
+    k_ref, s_ref, r_ref, west_ref, east_ref, strip_ref, first_ref, second_ref, send_ref, slots_ref,
     d_out, w_out, gath_out, send_out,
     kx, sx, fw, fs, fb, rd, dd, ww, lines_ref,
 ):
@@ -278,9 +301,10 @@
 
     def side(low):
         def joined(index):
+            south, north = from_turns("gy", first_ref[index], second_ref[index])
             if low:
-                return jnp.where(slot < 4, south_ref[index], strip_ref[index])
-            return jnp.where(slot < 4, strip_ref[index], north_ref[index])
+                return jnp.where(slot < 4, south, strip_ref[index])
+            return jnp.where(slot < 4, strip_ref[index], north)
 
         k, s, r = joined(0), joined(1), joined(2)
         face_w = harmonic(k, roll(k, 1, 0))
@@ -395,7 +419,7 @@
         lax.fori_loop(0, devices, gather, 0, unroll=8)
 
 
-def flow(conductivity, storage, recharge, west, east, strip, south, north, send, slots):
+def flow(conductivity, storage, recharge, west, east, strip, first, second, send, slots):
     layers, rows, width = conductivity.shape
     tall = pltpu.VMEM((layers, rows + 16, width), F32)
     return pl.pallas_call(
@@ -414,7 +438,7 @@
         + [pltpu.VMEM((layers * rows * 16, width), F32)],
         compiler_params=params(30),
         name="flow",
-    )(conductivity, storage, recharge, west, east, strip, south, north, send, slots)
+    )(conductivity, storage, recharge, west, east, strip, first, second, send, slots)
 
 
 def minmod(a, d):
@@ -514,7 +538,7 @@
 
 
 def first_kernel(
-    rows_x, recv_ref, gath_ref, col_ref, row_ref, c_out, s_out, flux_out, east_out, west_out, misc_out, scal_out
+    rows_x, recv_ref, gath_ref, col_ref, row_ref, c_out, s_out, flux_out, first_out, second_out, misc_out, scal_out
 ):
     devices = recv_ref.shape[0] // ROWS
     width = recv_ref.shape[1]
@@ -523,7 +547,7 @@
         return recv_ref[pl.ds(at, devices, stride=ROWS), :]
 
     cols, rows = col_ref[...], row_ref[...]
-    layers = east_out.shape[0]
+    layers = first_out.shape[0]
     misc = received(8)
     sums = jnp.sum(misc, 0, keepdims=True)
     at = iota(sums.shape, 1)
@@ -562,8 +586,11 @@
     own_r = jnp.concatenate([rows[0:1], rows[1:2]], 1)
     here = (own_r // rows_x == layer) & (own_r >= 0)
     parts = split(c)
-    east_out[...] = pick(here & (own_r % rows_x == rows_x - 1), parts)
-    west_out[...] = pick(here & (own_r % rows_x == 0), parts)
+    first_out[...], second_out[...] = by_turns(
+        "gx",
+        pick(here & (own_r % rows_x == 0), parts),
+        pick(here & (own_r % rows_x == rows_x - 1), parts),
+    )
     lane = iota((devices, width), 1)
     c0, c1 = c[:devices], c[devices:]
     misc_out[...] = jnp.where(
@@ -595,25 +622,25 @@
 
 
 def second_kernel(
-    rows_x, c_ref, s_ref, flux_ref, col_ref, row_ref, west_ref, east_ref, south_ref, north_ref, out_ref
+    rows_x, c_ref, s_ref, flux_ref, col_ref, row_ref, edge1_ref, edge2_ref, misc1_ref, misc2_ref, out_ref
 ):
     c, s = c_ref[...], s_ref[...]
     devices = c.shape[0] // 2
-    beside = neighbour_values(
-        c, col_ref[...], row_ref[...], west_ref[...], east_ref[...], south_ref[...], north_ref[...], rows_x
-    )
+    west, east = from_turns("gx", edge1_ref[...], edge2_ref[...])
+    south, north = from_turns("gy", misc1_ref[...], misc2_ref[...])
+    beside = neighbour_values(c, col_ref[...], row_ref[...], west, east, south, north, rows_x)
     c = transport(c, s, [flux_ref[i] for i in range(6)], *beside)
     for k in range(2):
         out_ref[pl.ds(k, devices, stride=2), :] = c[k * devices : (k + 1) * devices]
 
 
-def second_step(c, s, fluxes, cols, rows, west, east, south, north, rows_x):
+def second_step(c, s, fluxes, cols, rows, edges, miscs, rows_x):
     return pl.pallas_call(
         functools.partial(second_kernel, rows_x),
         out_shape=jax.ShapeDtypeStruct(c.shape, F32),
         compiler_params=params(16),
         name="second_step",
-    )(c, s, fluxes, cols, rows, west, east, south, north)
+    )(c, s, fluxes, cols, rows, *edges, *miscs)
 
 
 def owner_kernel(lines, ids_ref, recv_ref, out_ref):
@@ -637,38 +664,29 @@
     )(ids, received)
 
 
-def exchange(low_side, high_side, axis):
-    count = lax.axis_size(axis)
-    forward = [(i, i + 1) for i in range(count - 1)]
-    backward = [(i + 1, i) for i in range(count - 1)]
-    return lax.ppermute(high_side, axis, forward), lax.ppermute(low_side, axis, backward)
-
-
 def body(conductivity, storage, recharge, block_ids, neighbours, concentration, sorption):
     layers, rows_x, width = conductivity.shape
     devices = lax.axis_size(AXES)
     owned = concentration.shape[0]
     ids = block_ids.reshape(devices, owned)
-    to_east, to_west, conductivity, storage, recharge, ids, concentration, sorption = load(
+    first, second, conductivity, storage, recharge, ids, concentration, sorption = load(
         conductivity, storage, recharge, ids, concentration, sorption
     )
-    west, east = exchange(to_west, to_east, "gx")
+    first, second = swap("gx", first, second)
     inner, send, cols, rows = prepare(conductivity, storage, recharge, ids, concentration, sorption)
-    strip = pack_strip(inner, west, east)
-    south, north = exchange(strip, strip, "gy")
+    strip, west, east = pack_strip(inner, first, second)
+    first, second = swap("gy", strip, strip)
     base, image, gathered, send = flow(
-        conductivity, storage, recharge, west, east, strip, south, north, send, rows[:2]
+        conductivity, storage, recharge, west, east, strip, first, second, send, rows[:2]
     )
     received = lax.all_to_all(
         send.reshape(devices, 1, ROWS * width), AXES, split_axis=0, concat_axis=0, tiled=True
     ).reshape(devices * ROWS, width)
-    c, s, flux, to_east, to_west, misc, scal = first_step(
-        received, gathered, cols, rows, layers, rows_x
-    )
-    west, east = exchange(to_west, to_east, "gx")
-    south, north = exchange(misc, misc, "gy")
+    c, s, flux, first, second, misc, scal = first_step(received, gathered, cols, rows, layers, rows_x)
+    edges = swap("gx", first, second)
+    miscs = swap("gy", misc, misc)
     head = scal[0, 0] * base + scal[0, 1] * image
-    result = second_step(c, s, flux, cols, rows, west, east, south, north, rows_x)
+    result = second_step(c, s, flux, cols, rows, edges, miscs, rows_x)
     returned = lax.all_to_all(
         result.reshape(devices, 2, width), AXES, split_axis=0, concat_axis=0, tiled=True
     ).reshape(devices * 2, width)

time: 97.6 us -> 84.7 us (0.87)
  starting transfers between devices: 28.1 us -> 18.3 us
  blocking collectives: 28.4 us -> 22.8 us
  waiting for transfers between devices: 14.2 us -> 16.9 us
    ppermute x8, starting transfers between devices: 22.8 us -> 11.2 us  [swap(): return (lax.ppermute(first, axis, one), lax.ppermute(second, axis, other))]
    all_to_all x1, blocking collectives: 28.4 us -> 22.8 us  [body(): lax.all_to_all(send.reshape(devices, 1, ROWS * width), AXES, split_axis=0...]
    ppermute x8, waiting for transfers between devices: 6.37 us -> 9.03 us  [swap(): return (lax.ppermute(first, axis, one), lax.ppermute(second, axis, other))]
    all_to_all x1, starting transfers between devices: 5.26 us -> 7.1 us  [body(): lax.all_to_all(result.reshape(devices, 2, width), AXES, split_axis=0, con...]
  transfers between devices with their start and end apart: 9 -> 9, of which waited for: 5 -> 7; matrix products, arithmetic and copies ran while one was open for 3% -> 3% of each run, Pallas kernels for 1% -> 2%
where the time goes in v2:
time: 84.7 us; the launch traced here: 84.5 us
  Pallas kernels  23 us (27%)
  blocking collectives  22.8 us (27%)
  starting transfers between devices  18.3 us (22%)
  waiting for transfers between devices  16.9 us (20%)
  other arithmetic  2.13 us (3%)
    all_to_all x1, blocking collectives, body(): lax.all_to_all(send.reshape(devices, 1, ROWS * width), AXES, split_axis=0...  22.8 us
    ppermute x8, starting transfers between devices, swap(): return (lax.ppermute(first, axis, one), lax.ppermute(second, axis, other))  11.2 us
    ppermute x8, waiting for transfers between devices, swap(): return (lax.ppermute(first, axis, one), lax.ppermute(second, axis, other))  9.03 us
    all_to_all x1, waiting for transfers between devices, body(): lax.all_to_all(result.reshape(devices, 2, width), AXES, split_axis=0, con...  7.87 us
    pallas_call x1, Pallas kernels, flow(): pl.pallas_call(flow_kernel, out_shape=[jax.ShapeDtypeStruct(conductivity....  7.35 us
    all_to_all x1, starting transfers between devices, body(): lax.all_to_all(result.reshape(devices, 2, width), AXES, split_axis=0, con...  7.1 us
    pallas_call x1, Pallas kernels, first_step(): pl.pallas_call(functools.partial(first_kernel, rows_x), out_shape=[lines,...  5.84 us
    pallas_call x1, Pallas kernels, second_step(): pl.pallas_call(functools.partial(second_kernel, rows_x), out_shape=jax.Sh...  5.81 us
  transfers between devices with their start and end apart: 9, of which 7 were waited for; matrix products, arithmetic and copies ran while one was open for 3% of the time, Pallas kernels for 2%

profile of v2, /device:TPU:1, one launch (start us, length us, event | category | flops | bytes accessed | tf_op | source)
XLA Modules:
  0.0 84.5 jit_solution(8686390613252520322)
XLA Ops:
  0.6 1.4 %load.1 = (f32[16,8,128]{2,1,0:T(8,128)S(1)}, f32[16,8,128]{2,1,0:T(8,128)S(1)}, f32[16,64,128]{2,1,0:T(8,128)S(1)}, f32[16,64,128]{2,1,0:T(8,128)S(1)}, f32[16,...) custom-call(f32[16,64,128]{2,1,0:T(8,128)} %k_hbm.1, ...), custom_call_target="tpu_custom_call" | custom-call | tf_op jit(solution)/shard_map/load/pallas_call | solution.py:131
  2.1 1.5 %collective-permute-start = (f32[16,8,128]{2,1,0:T(8,128)S(1)}, f32[16,8,128]{2,1,0:T(8,128)S(1)}, u32[]{:S(2)}, u32[]{:S(2)}) collective-permute-start(f32[16,8,128]{2,1,0:T(8,128)S(1)} %get-tuple-element.35), channel_id=1, source_target_pairs={{0,16},{16,0},{32,48},{48,32},{64,80},{80,64},{96,112},{112,96},{1... | collective-permute-start | bytes 196616 | tf_op jit(solution)/shard_map/ppermute | solution.py:80
  3.6 1.3 %collective-permute-start.1 = (f32[16,8,128]{2,1,0:T(8,128)S(1)}, f32[16,8,128]{2,1,0:T(8,128)S(1)}, u32[]{:S(2)}, u32[]{:S(2)}) collective-permute-start(f32[16,8,128]{2,1,0:T(8,128)S(1)} %get-tuple-element.36), channel_id=1, source_target_pairs={{0,112},{16,32},{32,16},{48,64},{64,48},{80,96},{96,80},{112,0},{1... | collective-permute-start | bytes 196616 | tf_op jit(solution)/shard_map/ppermute | solution.py:80
  4.9 1.4 %prepare.1 = (f32[3,64,128]{2,1,0:T(8,128)S(1)}, f32[1152,128]{1,0:T(8,128)S(1)}, s32[128,128]{1,0:T(8,128)S(1)}, s32[16,128]{1,0:T(8,128)S(1)}) custom-call(f32[16,64,128]{2,1,0:T(8,128)S(1)} %get-tuple-element.28.k_ref, f32[16,64,128]{2,1,0:T(8,128)S(1)} %get-tuple-element.29.s_ref, f32[16,64,128]{2,1,0:T(8,128)S(1)} %get-tuple-element.30.r_ref, ...), custom_call_target="tpu_custom_call" | custom-call | tf_op jit(solution)/shard_map/prepare/pallas_call | solution.py:271
  6.2 0.0 collective-permute-done.first_ref
  6.2 1.3 %collective-permute-done.1.second_ref = f32[16,8,128]{2,1,0:T(8,128)S(1)} collective-permute-done((f32[16,8,128]{2,1,0:T(8,128)S(1)}, f32[16,8,128]{2,1,0:T(8,128)S(1)}, u32[]{:S(2)}, u32[]{:S(2)}) %collective-permute-start.1) | collective-permute-done | bytes 65568 | tf_op jit(solution)/shard_map/ppermute | solution.py:80
  7.6 0.2 pack_strip.1
  7.8 6.4 %collective-permute-start.3 = (f32[3,80,128]{2,1,0:T(8,128)S(1)}, f32[3,80,128]{2,1,0:T(8,128)S(1)}, u32[]{:S(2)}, u32[]{:S(2)}) collective-permute-start(f32[3,80,128]{2,1,0:T(8,128)S(1)} %get-tuple-element.39.strip_ref), channel_id=1, source_target_pairs={{0,15},{1,2},{2,1},{3,4},{4,3},{5,6},{6,5},{7,8},{8,7},{9,10},{10,... | collective-permute-start | bytes 368648 | tf_op jit(solution)/shard_map/ppermute | solution.py:80
  14.1 0.0 collective-permute-start.2
  14.1 2.7 %collective-permute-done.3.second_ref = f32[3,80,128]{2,1,0:T(8,128)S(1)} collective-permute-done((f32[3,80,128]{2,1,0:T(8,128)S(1)}, f32[3,80,128]{2,1,0:T(8,128)S(1)}, u32[]{:S(2)}, u32[]{:S(2)}) %collective-permute-start.3) | collective-permute-done | bytes 122912 | tf_op jit(solution)/shard_map/ppermute | solution.py:80
  16.8 1.2 %collective-permute-done.2.first_ref = f32[3,80,128]{2,1,0:T(8,128)S(1)} collective-permute-done((f32[3,80,128]{2,1,0:T(8,128)S(1)}, f32[3,80,128]{2,1,0:T(8,128)S(1)}, u32[]{:S(2)}, u32[]{:S(2)}) %collective-permute-start.2) | collective-permute-done | bytes 122912 | tf_op jit(solution)/shard_map/ppermute | solution.py:80
  18.0 7.3 %flow.1 = (f32[16,64,128]{2,1,0:T(8,128)S(1)}, f32[16,64,128]{2,1,0:T(8,128)S(1)}, f32[4096,128]{1,0:T(8,128)S(1)}, f32[1152,128]{1,0:T(8,128)S(1)}) custom-call(f32[16,64,128]{2,1,0:T(8,128)S(1)} %get-tuple-element.28.k_ref, f32[16,64,128]{2,1,0:T(8,128)S(1)} %get-tuple-element.29.s_ref, f32[16,64,128]{2,1,0:T(8,128)S(1)} %get-tuple-element.30.r_ref, ...), custom_call_target="tpu_custom_call" | custom-call | tf_op jit(solution)/shard_map/flow/pallas_call | solution.py:425
  25.4 22.8 %all_to_all.10 = f32[128,1,1152]{2,1,0:T(1,128)S(1)} all-to-all(f32[128,1,1152]{2,1,0:T(1,128)S(1)} %bitcast.8), channel_id=1, replica_groups=mesh['gx'=8,'gy'=16] {'gx','gy'}, dimensions={0} | all-to-all | bytes 1179648 | tf_op jit(solution)/shard_map/all_to_all | solution.py:682
  48.2 5.8 %first_step.1 = (f32[256,128]{1,0:T(8,128)S(1)}, f32[256,128]{1,0:T(8,128)S(1)}, f32[6,256,128]{2,1,0:T(8,128)S(1)}, f32[16,128]{1,0:T(8,128)S(1)}, f32[16,128]{...) custom-call(f32[1152,128]{1,0:T(8,128)S(1)} %bitcast.7, f32[4096,128]{1,0:T(8,128)S(1)} %get-tuple-element.43.gath_ref, ...), custom_call_target="tpu_custom_call" | custom-call | tf_op jit(solution)/shard_map/first_step/pallas_call | solution.py:608
  54.1 0.7 collective-permute-start.7
  54.7 0.2 collective-permute-start.6
  54.9 1.2 %collective-permute-start.4 = (f32[16,128]{1,0:T(8,128)S(1)}, f32[16,128]{1,0:T(8,128)S(1)}, u32[]{:S(2)}, u32[]{:S(2)}) collective-permute-start(f32[16,128]{1,0:T(8,128)S(1)} %get-tuple-element.51), channel_id=1, source_target_pairs={{0,16},{16,0},{32,48},{48,32},{64,80},{80,64},{96,112},{112,96},{1... | collective-permute-start | bytes 24584 | tf_op jit(solution)/shard_map/ppermute | solution.py:80
  56.1 0.0 collective-permute-start.5
  56.1 0.6 fusion
  56.7 0.2 collective-permute-done.4.edge1_ref
  56.9 2.5 %collective-permute-done.5.edge2_ref = f32[16,128]{1,0:T(8,128)S(1)} collective-permute-done((f32[16,128]{1,0:T(8,128)S(1)}, f32[16,128]{1,0:T(8,128)S(1)}, u32[]{:S(2)}, u32[]{:S(2)}) %collective-permute-start.5) | collective-permute-done | bytes 8224 | tf_op jit(solution)/shard_map/ppermute | solution.py:80
  59.5 1.1 %collective-permute-done.7.misc2_ref = f32[128,128]{1,0:T(8,128)S(1)} collective-permute-done((f32[128,128]{1,0:T(8,128)S(1)}, f32[128,128]{1,0:T(8,128)S(1)}, u32[]{:S(2)}, u32[]{:S(2)}) %collective-permute-start.7) | collective-permute-done | bytes 65568 | tf_op jit(solution)/shard_map/ppermute | solution.py:80
  60.6 0.0 collective-permute-done.6.misc1_ref
  60.6 5.8 %second_step.1 = f32[256,128]{1,0:T(8,128)} custom-call(f32[256,128]{1,0:T(8,128)S(1)} %get-tuple-element.48.c_ref, f32[256,128]{1,0:T(8,128)S(1)} %get-tuple-element.49.s_ref, f32[6,256,128]{2,1,0:T(8,128)S(1)} %get-tuple-element.50.flux_ref, s32[128,128]{1,0:T(8,128)S(1)} %get-tuple-element.44.col_ref, s32[16,128]{1,0:T(8,128)S(1)} %get-tuple-element.41.row_ref, ...), custom_call_target="tpu_custom_call" | custom-call | tf_op jit(solution)/shard_map/second_step/pallas_call | solution.py:638
  66.4 7.1 %all-to-all-start.1 = ((f32[128,2,128]{2,1,0:T(2,128)}), f32[128,2,128]{2,1,0:T(2,128)S(1)}, u32[]{:S(2)}, u32[]{:S(2)}) async-start(f32[128,2,128]{2,1,0:T(2,128)} %bitcast.5), calls=%async_computation.1 | async-start | bytes 262144 | tf_op jit(solution)/shard_map/all_to_all | solution.py:690
  73.5 2.1 %multiply_add_fusion = f32[16,64,128]{2,1,0:T(8,128)} fusion(f32[16,64,128]{2,1,0:T(8,128)S(1)} %get-tuple-element.47, f32[16,64,128]{2,1,0:T(8,128)S(1)} %get-tuple-element.46, f32[]{:T(128)} %bitcast.4, f32[]{:T(128)} %bitcast.3), kind=kLoop, calls=%fused_computation | loop fusion | flops 393216 | bytes 1572872 | tf_op jit(solution)/shard_map/add | solution.py:688
  75.6 7.9 %all-to-all-done.1 = f32[128,2,128]{2,1,0:T(2,128)S(1)} async-done(((f32[128,2,128]{2,1,0:T(2,128)}), f32[128,2,128]{2,1,0:T(2,128)S(1)}, u32[]{:S(2)}, u32[]{:S(2)}) %all-to-all-start.1) | async-done | bytes 131104 | tf_op jit(solution)/shard_map/all_to_all | solution.py:690
  83.5 1.0 %to_owner.1 = f32[128,128]{1,0:T(8,128)} custom-call(s32[128,128]{1,0:T(8,128)S(1)} %get-tuple-element.31.ids_ref, f32[256,128]{1,0:T(8,128)S(1)} %bitcast.9), custom_call_target="tpu_custom_call" | custom-call | tf_op jit(solution)/shard_map/to_owner/pallas_call | solution.py:659
  (1 shorter events, 0.0 us)
Async XLA Ops:
  2.1 4.1 %collective-permute-start = (f32[16,8,128]{2,1,0:T(8,128)S(1)}, f32[16,8,128]{2,1,0:T(8,128)S(1)}, u32[]{:S(2)}, u32[]{:S(2)}) collective-permute-start(f32[16,8,128]{2,1,0:T(8,128)S(1)} %get-tuple-element.35), channel_id=1, source_target_pairs={{0,16},{16,0},{32,48},{48,32},{64,80},{80,64},{96,112},{112,96},{1... | collective-permute-start | bytes 196616 | tf_op jit(solution)/shard_map/ppermute | solution.py:80
  3.6 4.0 %collective-permute-start.1 = (f32[16,8,128]{2,1,0:T(8,128)S(1)}, f32[16,8,128]{2,1,0:T(8,128)S(1)}, u32[]{:S(2)}, u32[]{:S(2)}) collective-permute-start(f32[16,8,128]{2,1,0:T(8,128)S(1)} %get-tuple-element.36), channel_id=1, source_target_pairs={{0,112},{16,32},{32,16},{48,64},{64,48},{80,96},{96,80},{112,0},{1... | collective-permute-start | bytes 196616 | tf_op jit(solution)/shard_map/ppermute | solution.py:80
  7.8 9.0 %collective-permute-start.3 = (f32[3,80,128]{2,1,0:T(8,128)S(1)}, f32[3,80,128]{2,1,0:T(8,128)S(1)}, u32[]{:S(2)}, u32[]{:S(2)}) collective-permute-start(f32[3,80,128]{2,1,0:T(8,128)S(1)} %get-tuple-element.39.strip_ref), channel_id=1, source_target_pairs={{0,15},{1,2},{2,1},{3,4},{4,3},{5,6},{6,5},{7,8},{8,7},{9,10},{10,... | collective-permute-start | bytes 368648 | tf_op jit(solution)/shard_map/ppermute | solution.py:80
  14.1 3.9 %collective-permute-start.2 = (f32[3,80,128]{2,1,0:T(8,128)S(1)}, f32[3,80,128]{2,1,0:T(8,128)S(1)}, u32[]{:S(2)}, u32[]{:S(2)}) collective-permute-start(f32[3,80,128]{2,1,0:T(8,128)S(1)} %get-tuple-element.39.strip_ref), channel_id=1, source_target_pairs={{0,1},{1,0},{2,3},{3,2},{4,5},{5,4},{6,7},{7,6},{8,9},{9,8},{10,11... | collective-permute-start | bytes 368648 | tf_op jit(solution)/shard_map/ppermute | solution.py:80
  54.1 6.5 %collective-permute-start.7 = (f32[128,128]{1,0:T(8,128)S(1)}, f32[128,128]{1,0:T(8,128)S(1)}, u32[]{:S(2)}, u32[]{:S(2)}) collective-permute-start(f32[128,128]{1,0:T(8,128)S(1)} %get-tuple-element.53), channel_id=1, source_target_pairs={{0,15},{1,2},{2,1},{3,4},{4,3},{5,6},{6,5},{7,8},{8,7},{9,10},{10,... | collective-permute-start | bytes 196616 | tf_op jit(solution)/shard_map/ppermute | solution.py:80
  54.7 5.8 %collective-permute-start.6 = (f32[128,128]{1,0:T(8,128)S(1)}, f32[128,128]{1,0:T(8,128)S(1)}, u32[]{:S(2)}, u32[]{:S(2)}) collective-permute-start(f32[128,128]{1,0:T(8,128)S(1)} %get-tuple-element.53), channel_id=1, source_target_pairs={{0,1},{1,0},{2,3},{3,2},{4,5},{5,4},{6,7},{7,6},{8,9},{9,8},{10,11... | collective-permute-start | bytes 196616 | tf_op jit(solution)/shard_map/ppermute | solution.py:80
  54.9 2.0 %collective-permute-start.4 = (f32[16,128]{1,0:T(8,128)S(1)}, f32[16,128]{1,0:T(8,128)S(1)}, u32[]{:S(2)}, u32[]{:S(2)}) collective-permute-start(f32[16,128]{1,0:T(8,128)S(1)} %get-tuple-element.51), channel_id=1, source_target_pairs={{0,16},{16,0},{32,48},{48,32},{64,80},{80,64},{96,112},{112,96},{1... | collective-permute-start | bytes 24584 | tf_op jit(solution)/shard_map/ppermute | solution.py:80
  56.1 3.4 %collective-permute-start.5 = (f32[16,128]{1,0:T(8,128)S(1)}, f32[16,128]{1,0:T(8,128)S(1)}, u32[]{:S(2)}, u32[]{:S(2)}) collective-permute-start(f32[16,128]{1,0:T(8,128)S(1)} %get-tuple-element.52), channel_id=1, source_target_pairs={{0,112},{16,32},{32,16},{48,64},{64,48},{80,96},{96,80},{112,0},{1... | collective-permute-start | bytes 24584 | tf_op jit(solution)/shard_map/ppermute | solution.py:80
  66.4 17.1 %all-to-all-start.1 = ((f32[128,2,128]{2,1,0:T(2,128)}), f32[128,2,128]{2,1,0:T(2,128)S(1)}, u32[]{:S(2)}, u32[]{:S(2)}) async-start(f32[128,2,128]{2,1,0:T(2,128)} %bitcast.5), calls=%async_computation.1 | async-start | bytes 262144 | tf_op jit(solution)/shard_map/all_to_all | solution.py:690

commit v3 on v2

--- a/solution.py
+++ b/solution.py
@@ -441,37 +441,107 @@
     )(conductivity, storage, recharge, west, east, strip, first, second, send, slots)
 
 
+CHUNK = 16
+
+
 def minmod(a, d):
     return jnp.maximum(jnp.minimum(a, d), 0.0) + jnp.minimum(jnp.maximum(a, d), 0.0)
 
 
-def tridiagonal(diagonal, right):
-    width = diagonal.shape[1]
-    side = jnp.where(iota(diagonal.shape, 1) == 0, 0.0, -COUPLING)
+def to_cells(lines, scratch):
+    half = lines.shape[0] // 2
+    count = lines.shape[1] // CHUNK
+    for k in range(2):
+        scratch[k] = lines[k * half : (k + 1) * half].T
+    tiles = [
+        jnp.concatenate([scratch[k, pl.ds(j, count, stride=CHUNK), :] for k in range(2)], 1)
+        for j in range(CHUNK)
+    ]
+    return jnp.concatenate(tiles, 0)
+
+
+def to_lines(tiles, scratch):
+    half = tiles[0].shape[1] // 2
+    count = tiles[0].shape[0]
+    for k in range(2):
+        for j, tile in enumerate(tiles):
+            scratch[k, pl.ds(j, count, stride=CHUNK), :] = tile[:, k * half : (k + 1) * half]
+    return [scratch[k].T for k in range(2)]
+
+
+def stacked(x):
+    return jnp.concatenate(split(x), 0)
+
+
+def take(parts, mask):
+    chosen = jnp.where(mask, 1.0, 0.0).astype(BF16)
+    out = jnp.dot(parts, chosen, preferred_element_type=F32)
+    count = parts.shape[0] // 3
+    return (out[2 * count :] + out[count : 2 * count]) + out[:count]
+
+
+def reduction(side, diagonal, right):
+    count = diagonal.shape[0]
     step = 1
-    while step < width:
+    while step < count:
         inverse = 1.0 / diagonal
         scaled = side * inverse
         value = right * inverse
-        before = roll(inverse, step, 1)
-        right = right - side * roll(value, step, 1) - roll(side * value, -step, 1)
-        diagonal = diagonal - side * (side * before) - roll(side * scaled, -step, 1)
-        side = -side * roll(scaled, step, 1)
+        right = right - side * roll(value, step, 0) - roll(side * value, -step, 0)
+        diagonal = diagonal - side * (side * roll(inverse, step, 0)) - roll(side * scaled, -step, 0)
+        side = -side * roll(scaled, step, 0)
         step *= 2
     return right / diagonal
 
 
+def tridiagonal(diagonal, right):
+    off = -COUPLING
+    last = CHUNK - 1
+    one = jnp.ones_like(diagonal[0])
+    zero = jnp.zeros_like(one)
+    lead, lead_right = [one, diagonal[0]], [right[0]]
+    for j in range(1, last):
+        lead_right.append(right[j] * lead[j] - off * lead_right[j - 1])
+        lead.append(diagonal[j] * lead[j] - (off * off) * lead[j - 1])
+    trail, trail_right = {last: one, last + 1: zero}, {last: zero}
+    for j in range(last - 1, -1, -1):
+        trail_right[j] = right[j] * trail[j + 1] - off * trail_right[j + 1]
+        trail[j] = diagonal[j] * trail[j + 1] - (off * off) * trail[j + 2]
+    inverse = 1.0 / lead[last]
+    sub = iota(one.shape, 0)
+    top = sub == one.shape[0] - 1
+    far = off * (-off) ** (last - 1)
+    side = jnp.where(sub == 0, 0.0, (-off * far) * inverse)
+    above = jnp.where(top, 0.0, roll(trail[1] * inverse, -1, 0))
+    above_right = jnp.where(top, 0.0, roll(trail_right[0] * inverse, -1, 0))
+    z = reduction(
+        side,
+        diagonal[last] - (off * off) * (lead[last - 1] * inverse + above),
+        right[last] - off * (lead_right[last - 1] * inverse + above_right),
+    )
+    before = jnp.where(sub == 0, 0.0, roll(z, 1, 0))
+    out = []
+    for j in range(last):
+        low = lead_right[j] - (off * (-off) ** j) * before
+        high = off * trail_right[j + 1] + (off * (-off) ** (last - 1 - j)) * z
+        out.append(inverse * (trail[j + 1] * low - lead[j] * high))
+    return out + [z]
+
+
 def transport(c, sorption, fluxes, west, east, lower, upper, ends):
-    lane = iota(c.shape, 1)
-    width = c.shape[1]
-    last = lane == width - 1
-    south_one = roll(ends, -1, 1)
-    north_one = roll(ends, width - 5, 1)
-    back = jnp.where(lane == 0, south_one, roll(c, 1, 1))
-    back2 = jnp.where(lane < 2, ends, roll(c, 2, 1))
-    ahead = jnp.where(last, north_one, roll(c, -1, 1))
-    ahead2 = jnp.where(lane >= width - 2, roll(ends, width - 6, 1), roll(c, -2, 1))
     q_w, q_e, q_b, q_a, q_s, q_n = fluxes
+    south_two, south_one, north_one, north_two = ends
+    sub = iota(c[0].shape, 0)
+    bottom, top = sub == 0, sub == c[0].shape[0] - 1
+    before = [
+        jnp.where(bottom, south_two, roll(c[-2], 1, 0)),
+        jnp.where(bottom, south_one, roll(c[-1], 1, 0)),
+    ]
+    after = [
+        jnp.where(top, north_one, roll(c[0], -1, 0)),
+        jnp.where(top, north_two, roll(c[1], -1, 0)),
+    ]
+    line = before + c + after
 
     def face(q, far_left, left, right, far_right):
         rise = right - left
@@ -479,75 +549,86 @@
         negative = right + 0.5 * minmod(-rise, right - far_right)
         return jnp.maximum(q, 0.0) * positive + jnp.minimum(q, 0.0) * negative
 
-    along = face(q_s, back2, back, c, ahead)
-    beyond = face(q_n, back, c, ahead, ahead2)
-    advect = along - jnp.where(last, beyond, roll(along, -1, 1))
-    advect = advect + jnp.maximum(q_w, 0.0) * west + jnp.minimum(q_w, 0.0) * c
-    advect = advect - jnp.maximum(q_e, 0.0) * c - jnp.minimum(q_e, 0.0) * east
-    advect = advect + jnp.maximum(q_b, 0.0) * lower + jnp.minimum(q_b, 0.0) * c
-    advect = advect - jnp.maximum(q_a, 0.0) * c - jnp.minimum(q_a, 0.0) * upper
-    advect = ADVECT * advect
-    advect = advect + COUPLING * (
-        jnp.where(lane == 0, south_one, 0.0) + jnp.where(last, north_one, 0.0)
-    )
-    weight = BULK_DENSITY * sorption
-    v = c
-    source = None
+    along = [face(q_s[j], *line[j : j + 4]) for j in range(CHUNK)]
+    beyond = face(q_n, *line[CHUNK : CHUNK + 4])
+    along.append(jnp.where(top, beyond, roll(along[0], -1, 0)))
+    v = list(c)
+    source = [None] * CHUNK
+    diagonal, right = [None] * CHUNK, [None] * CHUNK
     for sweep in range(PICARD):
-        square = v * v + SOFTEN * SOFTEN
-        power = weight * jnp.exp((0.5 * (EXPONENT - 1.0)) * jnp.log(square))
-        retard = POROSITY + power
-        root = jnp.sqrt(square)
-        if sweep == 0:
-            source = POROSITY * c + power * root + advect
-            target = retard * c + advect
-        else:
-            target = power * (v - root) + source
-        v = tridiagonal(retard + 2.0 * COUPLING, target)
+        for j in range(CHUNK):
+            square = v[j] * v[j] + SOFTEN * SOFTEN
+            power = (BULK_DENSITY * sorption[j]) * jnp.exp(
+                (0.5 * (EXPONENT - 1.0)) * jnp.log(square)
+            )
+            retard = POROSITY + power
+            root = jnp.sqrt(square)
+            if sweep == 0:
+                value = c[j]
+                advect = along[j] - along[j + 1]
+                advect = advect + jnp.maximum(q_w[j], 0.0) * west[j] + jnp.minimum(q_w[j], 0.0) * value
+                advect = advect - jnp.maximum(q_e[j], 0.0) * value - jnp.minimum(q_e[j], 0.0) * east[j]
+                advect = advect + jnp.maximum(q_b[j], 0.0) * lower[j] + jnp.minimum(q_b[j], 0.0) * value
+                advect = advect - jnp.maximum(q_a[j], 0.0) * value - jnp.minimum(q_a[j], 0.0) * upper[j]
+                advect = ADVECT * advect
+                if j == 0:
+                    advect = advect + jnp.where(bottom, COUPLING * south_one, 0.0)
+                if j == CHUNK - 1:
+                    advect = advect + jnp.where(top, COUPLING * north_one, 0.0)
+                source[j] = POROSITY * value + power * root + advect
+                right[j] = retard * value + advect
+            else:
+                right[j] = power * (v[j] - root) + source[j]
+            diagonal[j] = retard + 2.0 * COUPLING
+        v = tridiagonal(diagonal, right)
     return v
 
 
-def neighbour_values(c, cols, rows, west_edge, east_edge, south_misc, north_misc, rows_x):
-    own_c = jnp.concatenate([cols[:, 0:1], cols[:, 1:2]], 0)
-    own_r = jnp.concatenate([rows[0:1], rows[1:2]], 1)
-    layers = west_edge.shape[0]
-    active = own_c >= 0
-    row_c = own_c % rows_x
-    layer_c = own_c // rows_x
-    first = active & (row_c == 0)
-    final = active & (row_c == rows_x - 1)
-    at_layer = iota((own_c.shape[0], layers), 1) == layer_c
-    parts = split(c)
-    west = pick((own_r == own_c - 1) & (row_c != 0), parts) + pick(
-        at_layer & first, split(west_edge)
-    )
-    east = pick((own_r == own_c + 1) & (row_c != rows_x - 1), parts) + pick(
-        at_layer & final, split(east_edge)
-    )
-    lower = pick(own_r == own_c - rows_x, parts)
-    upper = pick(own_r == own_c + rows_x, parts)
-    lane = iota(south_misc.shape, 1)
-    ends = None
-    for k in range(2):
-        tails = split(jnp.where(lane // 2 == k, south_misc, 0.0))
-        heads = split(jnp.where(lane // 2 == 2 + k, north_misc, 0.0))
-        part = pick((rows[6 + k : 7 + k] == own_c) & active, tails)
-        part = part + pick((rows[8 + k : 9 + k] == own_c) & active, heads)
-        ends = part if ends is None else ends + part
-    return west, east, lower, upper, ends + roll(ends, -2, 1)
+def tiles_of(x):
+    count = x.shape[0] // CHUNK
+    return [x[j * count : (j + 1) * count] for j in range(CHUNK)]
+
+
+def both(x, at, axis):
+    if axis:
+        return jnp.concatenate([x[at : at + 1], x[at + 1 : at + 2]], 1)
+    return jnp.concatenate([x[:, at : at + 1], x[:, at + 1 : at + 2]], 0)
+
+
+def inner_neighbours(c, cols, rows, rows_x):
+    own_c, own_r = both(cols, 0, 0), both(rows, 0, 1)
+    at = own_r % rows_x
+    parts = stacked(c)
+    west = take(parts, (own_c == own_r - 1) & (at != 0))
+    east = take(parts, (own_c == own_r + 1) & (at != rows_x - 1))
+    lower = take(parts, own_c == own_r - rows_x)
+    upper = take(parts, own_c == own_r + rows_x)
+    return west, east, lower, upper
+
+
+def end_values(south, north, cols, rows):
+    own_r = both(rows, 0, 1)
+    active = own_r >= 0
+    tails = take(stacked(south), (both(cols, 6, 0) == own_r) & active)
+    heads = take(stacked(north), (both(cols, 8, 0) == own_r) & active)
+    return tails[0:1], tails[1:2], heads[2:3], heads[3:4]
 
 
 def first_kernel(
-    rows_x, recv_ref, gath_ref, col_ref, row_ref, c_out, s_out, flux_out, first_out, second_out, misc_out, scal_out
+    rows_x, layers, recv_ref, gath_ref, col_ref, row_ref,
+    c_out, s_out, flux_out, edge_out, end_out, scal_out, scratch,
 ):
     devices = recv_ref.shape[0] // ROWS
+    slots = 2 * devices
     width = recv_ref.shape[1]
 
     def received(at):
         return recv_ref[pl.ds(at, devices, stride=ROWS), :]
 
+    def pair(at):
+        return jnp.concatenate([received(at), received(at + 1)], 0)
+
     cols, rows = col_ref[...], row_ref[...]
-    layers = first_out.shape[0]
     misc = received(8)
     sums = jnp.sum(misc, 0, keepdims=True)
     at = iota(sums.shape, 1)
@@ -562,85 +643,118 @@
     alpha_next = gamma_next / bend_next
     on_d = alpha + alpha_next * (1.0 + beta)
     on_w = -alpha * alpha_next
-    lane8 = iota((8, width), 1)
-    scal_out[...] = jnp.where(lane8 == 0, on_d, on_w)
-
-    c = jnp.concatenate([received(0), received(1)], 0)
-    s = jnp.concatenate([received(2), received(3)], 0)
-    layer = iota((layers, 2 * devices), 0)
-    west_codes = jnp.concatenate([rows[2:3], rows[3:4]], 1)
-    east_codes = jnp.concatenate([rows[4:5], rows[5:6]], 1)
-    west_edge = pick(layer == west_codes, split(jnp.concatenate([received(4), received(5)], 0)))
-    east_edge = pick(layer == east_codes, split(jnp.concatenate([received(6), received(7)], 0)))
+    scal_out[...] = jnp.where(iota((8, width), 1) == 0, on_d, on_w)
+
+    c = to_cells(pair(0), scratch.at[0])
+    s = to_cells(pair(2), scratch.at[1])
+    s_out[...] = s
+    beside_w = to_cells(pair(4), scratch.at[2])
+    beside_e = to_cells(pair(6), scratch.at[3])
     fluxes = []
     for i in range(6):
-        slots = 2 * devices
         flux = on_d * gath_ref[pl.ds(i, slots, stride=16), :]
         flux = flux + on_w * gath_ref[pl.ds(6 + i, slots, stride=16), :]
-        flux_out[i] = flux
-        fluxes.append(flux)
-    beside = neighbour_values(c, cols, rows, west_edge, east_edge, misc, misc, rows_x)
-    c = transport(c, s, fluxes, *beside)
+        flux = to_cells(flux, scratch.at[4 + i])
+        if i == 5:
+            flux = flux[width - width // CHUNK :]
+            flux_out[5, : flux.shape[0]] = flux
+            fluxes.append(flux)
+        else:
+            flux_out[i] = flux
+            fluxes.append(tiles_of(flux))
+    west, east, lower, upper = inner_neighbours(c, cols, rows, rows_x)
+    own_c, own_r = both(cols, 0, 0), both(rows, 0, 1)
+    layer, row = own_r // rows_x, own_r % rows_x
+    active = own_r >= 0
+    west = west + take(stacked(beside_w), (both(cols, 2, 0) == layer) & active & (row == 0))
+    east = east + take(stacked(beside_e), (both(cols, 4, 0) == layer) & active & (row == rows_x - 1))
+    turned = misc.T
+    ends = [
+        jnp.concatenate([turned[a : a + 1], turned[a + 2 : a + 3]], 1) for a in (0, 1, 4, 5)
+    ] + [jnp.zeros((4, slots), F32)]
+    ends = jnp.concatenate(ends, 0)
+    ends = end_values(ends, ends, cols, rows)
+    tiles = transport(
+        tiles_of(c), tiles_of(s), fluxes, tiles_of(west), tiles_of(east), tiles_of(lower), tiles_of(upper), ends
+    )
+    c = jnp.concatenate(tiles, 0)
     c_out[...] = c
-    s_out[...] = s
-    own_r = jnp.concatenate([rows[0:1], rows[1:2]], 1)
-    here = (own_r // rows_x == layer) & (own_r >= 0)
-    parts = split(c)
-    first_out[...], second_out[...] = by_turns(
-        "gx",
-        pick(here & (own_r % rows_x == 0), parts),
-        pick(here & (own_r % rows_x == rows_x - 1), parts),
+    count = tiles[0].shape[0]
+    end_out[...] = jnp.concatenate(
+        [
+            tiles[-2][count - 1 :],
+            tiles[-1][count - 1 :],
+            tiles[0][:1],
+            tiles[1][:1],
+            jnp.zeros((4, slots), F32),
+        ],
+        0,
     )
-    lane = iota((devices, width), 1)
-    c0, c1 = c[:devices], c[devices:]
-    misc_out[...] = jnp.where(
-        lane < 2,
-        roll(c0, 2, 1),
-        jnp.where(lane < 4, roll(c1, 4, 1), jnp.where(lane < 6, roll(c0, 4, 1), roll(c1, 6, 1))),
-    )
+    lane = iota((slots, width), 1)
+    high = (own_c % rows_x == rows_x - 1) & (own_c // rows_x == lane)
+    low = (own_c % rows_x == 0) & (own_c // rows_x + layers == lane)
+    edge = take(stacked(c), (high | low) & (own_c >= 0))
+    edge_out[...] = edge.T[: 2 * layers]
 
 
 def first_step(received, gathered, cols, rows, layers, rows_x):
     width = received.shape[1]
     devices = cols.shape[0]
-    lines = jax.ShapeDtypeStruct((2 * devices, width), F32)
-    edge = jax.ShapeDtypeStruct((layers, width), F32)
+    cells = jax.ShapeDtypeStruct((width, 2 * devices), F32)
     return pl.pallas_call(
-        functools.partial(first_kernel, rows_x),
+        functools.partial(first_kernel, rows_x, layers),
         out_shape=[
-            lines,
-            lines,
-            jax.ShapeDtypeStruct((6, 2 * devices, width), F32),
-            edge,
-            edge,
-            jax.ShapeDtypeStruct((devices, width), F32),
+            cells,
+            cells,
+            jax.ShapeDtypeStruct((6, width, 2 * devices), F32),
+            jax.ShapeDtypeStruct((2 * layers, width), F32),
+            jax.ShapeDtypeStruct((8, 2 * devices), F32),
             jax.ShapeDtypeStruct((8, width), F32),
         ],
+        scratch_shapes=[pltpu.VMEM((10, 2, width, devices), F32)],
         compiler_params=params(16),
         name="first_step",
     )(received, gathered, cols, rows)
 
 
 def second_kernel(
-    rows_x, c_ref, s_ref, flux_ref, col_ref, row_ref, edge1_ref, edge2_ref, misc1_ref, misc2_ref, out_ref
+    rows_x, c_ref, s_ref, flux_ref, col_ref, row_ref, edge1_ref, edge2_ref, end1_ref, end2_ref, out_ref, scratch
 ):
     c, s = c_ref[...], s_ref[...]
-    devices = c.shape[0] // 2
-    west, east = from_turns("gx", edge1_ref[...], edge2_ref[...])
-    south, north = from_turns("gy", misc1_ref[...], misc2_ref[...])
-    beside = neighbour_values(c, col_ref[...], row_ref[...], west, east, south, north, rows_x)
-    c = transport(c, s, [flux_ref[i] for i in range(6)], *beside)
-    for k in range(2):
-        out_ref[pl.ds(k, devices, stride=2), :] = c[k * devices : (k + 1) * devices]
-
-
-def second_step(c, s, fluxes, cols, rows, edges, miscs, rows_x):
+    width = c.shape[0]
+    devices = c.shape[1] // 2
+    cols, rows = col_ref[...], row_ref[...]
+    west, east, lower, upper = inner_neighbours(c, cols, rows, rows_x)
+    west_edge, east_edge = from_turns("gx", edge1_ref[...], edge2_ref[...])
+    layers = west_edge.shape[0] // 2
+    own_r = both(rows, 0, 1)
+    layer, row = own_r // rows_x, own_r % rows_x
+    active = own_r >= 0
+    code = iota((width, 2 * devices), 0)
+    rest = jnp.zeros((width - 2 * layers, width), F32)
+    west_edge = jnp.concatenate([west_edge, rest], 0).T
+    east_edge = jnp.concatenate([east_edge, rest], 0).T
+    west = west + take(stacked(west_edge), (code == layer) & active & (row == 0))
+    east = east + take(stacked(east_edge), (code == layer + layers) & active & (row == rows_x - 1))
+    south, north = from_turns("gy", end1_ref[...], end2_ref[...])
+    ends = end_values(south, north, cols, rows)
+    fluxes = [tiles_of(flux_ref[i]) for i in range(5)] + [flux_ref[5, : width // CHUNK]]
+    tiles = transport(
+        tiles_of(c), tiles_of(s), fluxes, tiles_of(west), tiles_of(east), tiles_of(lower), tiles_of(upper), ends
+    )
+    for k, lines in enumerate(to_lines(tiles, scratch)):
+        out_ref[pl.ds(k, devices, stride=2), :] = lines
+
+
+def second_step(c, s, fluxes, cols, rows, edges, ends, rows_x):
+    width, slots = c.shape
     return pl.pallas_call(
         functools.partial(second_kernel, rows_x),
-        out_shape=jax.ShapeDtypeStruct(c.shape, F32),
+        out_shape=jax.ShapeDtypeStruct((slots, width), F32),
+        scratch_shapes=[pltpu.VMEM((2, width, slots // 2), F32)],
         compiler_params=params(16),
         name="second_step",
-    )(c, s, fluxes, cols, rows, *edges, *miscs)
+    )(c, s, fluxes, cols, rows, *edges, *ends)
 
 
 def owner_kernel(lines, ids_ref, recv_ref, out_ref):
@@ -682,11 +796,11 @@
     received = lax.all_to_all(
         send.reshape(devices, 1, ROWS * width), AXES, split_axis=0, concat_axis=0, tiled=True
     ).reshape(devices * ROWS, width)
-    c, s, flux, first, second, misc, scal = first_step(received, gathered, cols, rows, layers, rows_x)
-    edges = swap("gx", first, second)
-    miscs = swap("gy", misc, misc)
+    c, s, flux, edge, end, scal = first_step(received, gathered, cols, rows, layers, rows_x)
+    edges = swap("gx", edge, edge)
+    ends = swap("gy", end, end)
     head = scal[0, 0] * base + scal[0, 1] * image
-    result = second_step(c, s, flux, cols, rows, edges, miscs, rows_x)
+    result = second_step(c, s, flux, cols, rows, edges, ends, rows_x)
     returned = lax.all_to_all(
         result.reshape(devices, 2, width), AXES, split_axis=0, concat_axis=0, tiled=True
     ).reshape(devices * 2, width)

time: 84.7 us -> 77.2 us (0.911)
  Pallas kernels: 23 us -> 16.2 us
    pallas_call x1, Pallas kernels: 5.81 us -> 2.27 us  [second_step(): pl.pallas_call(functools.partial(second_kernel, rows_x), out_shape=jax.Sh...]
    pallas_call x1, Pallas kernels: 5.84 us -> 2.63 us  [first_step(): pl.pallas_call(functools.partial(first_kernel, rows_x, layers), out_shape...]
  transfers between devices with their start and end apart: 9 -> 9, of which waited for: 7 -> 5; matrix products, arithmetic and copies ran while one was open for 3% -> 4% of each run, Pallas kernels for 2% -> 2%
where the time goes in v3:
time: 77.2 us; the launch traced here: 77 us
  blocking collectives  22.8 us (30%)
  starting transfers between devices  18.4 us (24%)
  Pallas kernels  16.2 us (21%)
  waiting for transfers between devices  16.1 us (21%)
  other arithmetic  2.13 us (3%)
    all_to_all x1, blocking collectives, body(): lax.all_to_all(send.reshape(devices, 1, ROWS * width), AXES, split_axis=0...  22.8 us
    ppermute x8, starting transfers between devices, swap(): return (lax.ppermute(first, axis, one), lax.ppermute(second, axis, other))  11.4 us
    ppermute x8, waiting for transfers between devices, swap(): return (lax.ppermute(first, axis, one), lax.ppermute(second, axis, other))  8.25 us
    all_to_all x1, waiting for transfers between devices, body(): lax.all_to_all(result.reshape(devices, 2, width), AXES, split_axis=0, con...  7.87 us
    pallas_call x1, Pallas kernels, flow(): pl.pallas_call(flow_kernel, out_shape=[jax.ShapeDtypeStruct(conductivity....  7.35 us
    all_to_all x1, starting transfers between devices, body(): lax.all_to_all(result.reshape(devices, 2, width), AXES, split_axis=0, con...  7.04 us
    pallas_call x1, Pallas kernels, first_step(): pl.pallas_call(functools.partial(first_kernel, rows_x, layers), out_shape...  2.63 us
    pallas_call x1, Pallas kernels, second_step(): pl.pallas_call(functools.partial(second_kernel, rows_x), out_shape=jax.Sh...  2.27 us
  transfers between devices with their start and end apart: 9, of which 5 were waited for; matrix products, arithmetic and copies ran while one was open for 4% of the time, Pallas kernels for 2%

profile of v3, /device:TPU:1, one launch (start us, length us, event | category | flops | bytes accessed | tf_op | source)
XLA Modules:
  0.0 77.0 jit_solution(1514376446283066588)
XLA Ops:
  0.6 1.4 %load.1 = (f32[16,8,128]{2,1,0:T(8,128)S(1)}, f32[16,8,128]{2,1,0:T(8,128)S(1)}, f32[16,64,128]{2,1,0:T(8,128)S(1)}, f32[16,64,128]{2,1,0:T(8,128)S(1)}, f32[16,...) custom-call(f32[16,64,128]{2,1,0:T(8,128)} %k_hbm.1, ...), custom_call_target="tpu_custom_call" | custom-call | tf_op jit(solution)/shard_map/load/pallas_call | solution.py:131
  2.1 1.5 %collective-permute-start = (f32[16,8,128]{2,1,0:T(8,128)S(1)}, f32[16,8,128]{2,1,0:T(8,128)S(1)}, u32[]{:S(2)}, u32[]{:S(2)}) collective-permute-start(f32[16,8,128]{2,1,0:T(8,128)S(1)} %get-tuple-element.34), channel_id=1, source_target_pairs={{0,16},{16,0},{32,48},{48,32},{64,80},{80,64},{96,112},{112,96},{1... | collective-permute-start | bytes 196616 | tf_op jit(solution)/shard_map/ppermute | solution.py:80
  3.6 1.3 %collective-permute-start.1 = (f32[16,8,128]{2,1,0:T(8,128)S(1)}, f32[16,8,128]{2,1,0:T(8,128)S(1)}, u32[]{:S(2)}, u32[]{:S(2)}) collective-permute-start(f32[16,8,128]{2,1,0:T(8,128)S(1)} %get-tuple-element.35), channel_id=1, source_target_pairs={{0,112},{16,32},{32,16},{48,64},{64,48},{80,96},{96,80},{112,0},{1... | collective-permute-start | bytes 196616 | tf_op jit(solution)/shard_map/ppermute | solution.py:80
  4.9 1.4 %prepare.1 = (f32[3,64,128]{2,1,0:T(8,128)S(1)}, f32[1152,128]{1,0:T(8,128)S(1)}, s32[128,128]{1,0:T(8,128)S(1)}, s32[16,128]{1,0:T(8,128)S(1)}) custom-call(f32[16,64,128]{2,1,0:T(8,128)S(1)} %get-tuple-element.27.k_ref, f32[16,64,128]{2,1,0:T(8,128)S(1)} %get-tuple-element.28.s_ref, f32[16,64,128]{2,1,0:T(8,128)S(1)} %get-tuple-element.29.r_ref, ...), custom_call_target="tpu_custom_call" | custom-call | tf_op jit(solution)/shard_map/prepare/pallas_call | solution.py:271
  6.2 0.0 collective-permute-done.first_ref
  6.2 1.3 %collective-permute-done.1.second_ref = f32[16,8,128]{2,1,0:T(8,128)S(1)} collective-permute-done((f32[16,8,128]{2,1,0:T(8,128)S(1)}, f32[16,8,128]{2,1,0:T(8,128)S(1)}, u32[]{:S(2)}, u32[]{:S(2)}) %collective-permute-start.1) | collective-permute-done | bytes 65568 | tf_op jit(solution)/shard_map/ppermute | solution.py:80
  7.6 0.2 pack_strip.1
  7.8 6.4 %collective-permute-start.3 = (f32[3,80,128]{2,1,0:T(8,128)S(1)}, f32[3,80,128]{2,1,0:T(8,128)S(1)}, u32[]{:S(2)}, u32[]{:S(2)}) collective-permute-start(f32[3,80,128]{2,1,0:T(8,128)S(1)} %get-tuple-element.38.strip_ref), channel_id=1, source_target_pairs={{0,15},{1,2},{2,1},{3,4},{4,3},{5,6},{6,5},{7,8},{8,7},{9,10},{10,... | collective-permute-start | bytes 368648 | tf_op jit(solution)/shard_map/ppermute | solution.py:80
  14.1 0.0 collective-permute-start.2
  14.1 2.7 %collective-permute-done.3.second_ref = f32[3,80,128]{2,1,0:T(8,128)S(1)} collective-permute-done((f32[3,80,128]{2,1,0:T(8,128)S(1)}, f32[3,80,128]{2,1,0:T(8,128)S(1)}, u32[]{:S(2)}, u32[]{:S(2)}) %collective-permute-start.3) | collective-permute-done | bytes 122912 | tf_op jit(solution)/shard_map/ppermute | solution.py:80
  16.8 1.2 %collective-permute-done.2.first_ref = f32[3,80,128]{2,1,0:T(8,128)S(1)} collective-permute-done((f32[3,80,128]{2,1,0:T(8,128)S(1)}, f32[3,80,128]{2,1,0:T(8,128)S(1)}, u32[]{:S(2)}, u32[]{:S(2)}) %collective-permute-start.2) | collective-permute-done | bytes 122912 | tf_op jit(solution)/shard_map/ppermute | solution.py:80
  18.0 7.3 %flow.1 = (f32[16,64,128]{2,1,0:T(8,128)S(1)}, f32[16,64,128]{2,1,0:T(8,128)S(1)}, f32[4096,128]{1,0:T(8,128)S(1)}, f32[1152,128]{1,0:T(8,128)S(1)}) custom-call(f32[16,64,128]{2,1,0:T(8,128)S(1)} %get-tuple-element.27.k_ref, f32[16,64,128]{2,1,0:T(8,128)S(1)} %get-tuple-element.28.s_ref, f32[16,64,128]{2,1,0:T(8,128)S(1)} %get-tuple-element.29.r_ref, ...), custom_call_target="tpu_custom_call" | custom-call | tf_op jit(solution)/shard_map/flow/pallas_call | solution.py:425
  25.4 22.8 %all_to_all.10 = f32[128,1,1152]{2,1,0:T(1,128)S(1)} all-to-all(f32[128,1,1152]{2,1,0:T(1,128)S(1)} %bitcast.8), channel_id=1, replica_groups=mesh['gx'=8,'gy'=16] {'gx','gy'}, dimensions={0} | all-to-all | bytes 1179648 | tf_op jit(solution)/shard_map/all_to_all | solution.py:796
  48.2 2.6 %first_step.1 = (f32[128,256]{1,0:T(8,128)S(1)}, f32[128,256]{1,0:T(8,128)S(1)}, f32[6,128,256]{2,1,0:T(8,128)S(1)}, f32[32,128]{1,0:T(8,128)S(1)}, f32[8,256]{1,0:T(8,128)S(1)}, /*index=5*/f32[8,128]{1,0:T(8,128)S(1)}) custom-call(f32[1152,128]{1,0:T(8,128)S(1)} %bitcast.7, f32[4096,128]{1,0:T(8,128)S(1)} %get-tuple-element.42.gath_ref, ...), custom_call_target="tpu_custom_call" | custom-call | tf_op jit(solution)/shard_map/first_step/pallas_call | solution.py:704
  50.8 0.7 collective-permute-start.7
  51.5 0.2 collective-permute-start.6
  51.7 1.2 %collective-permute-start.5 = (f32[32,128]{1,0:T(8,128)S(1)}, f32[32,128]{1,0:T(8,128)S(1)}, u32[]{:S(2)}, u32[]{:S(2)}) collective-permute-start(f32[32,128]{1,0:T(8,128)S(1)} %get-tuple-element.50), channel_id=1, source_target_pairs={{0,112},{16,32},{32,16},{48,64},{64,48},{80,96},{96,80},{112,0},{1... | collective-permute-start | bytes 49160 | tf_op jit(solution)/shard_map/ppermute | solution.py:80
  52.9 0.2 collective-permute-start.4
  53.1 0.6 fusion
  53.7 3.0 %collective-permute-done.7.end2_ref = f32[8,256]{1,0:T(8,128)S(1)} collective-permute-done((f32[8,256]{1,0:T(8,128)S(1)}, f32[8,256]{1,0:T(8,128)S(1)}, u32[]{:S(2)}, u32[]{:S(2)}) %collective-permute-start.7) | collective-permute-done | bytes 8224 | tf_op jit(solution)/shard_map/ppermute | solution.py:80
  56.7 0.0 collective-permute-done.6.end1_ref
  56.7 0.0 collective-permute-done.5.edge2_ref
  56.7 0.0 collective-permute-done.4.edge1_ref
  56.7 2.3 %second_step.1 = f32[256,128]{1,0:T(8,128)} custom-call(f32[128,256]{1,0:T(8,128)S(1)} %get-tuple-element.47.c_ref, f32[128,256]{1,0:T(8,128)S(1)} %get-tuple-element.48.s_ref, f32[6,128,256]{2,1,0:T(8,128)S(1)} %get-tuple-element.49.flux_ref, s32[128,128]{1,0:T(8,128)S(1)} %get-tuple-element.43.col_ref, s32[16,128]{1,0:T(8,128)S(1)} %get-tuple-element.40.row_ref, ...), custom_call_target="tpu_custom_call" | custom-call | tf_op jit(solution)/shard_map/second_step/pallas_call | solution.py:751
  59.0 7.0 %all-to-all-start.1 = ((f32[128,2,128]{2,1,0:T(2,128)}), f32[128,2,128]{2,1,0:T(2,128)S(1)}, u32[]{:S(2)}, u32[]{:S(2)}) async-start(f32[128,2,128]{2,1,0:T(2,128)} %bitcast.5), calls=%async_computation.1 | async-start | bytes 262144 | tf_op jit(solution)/shard_map/all_to_all | solution.py:804
  66.0 2.1 %multiply_add_fusion = f32[16,64,128]{2,1,0:T(8,128)} fusion(f32[16,64,128]{2,1,0:T(8,128)S(1)} %get-tuple-element.46, f32[16,64,128]{2,1,0:T(8,128)S(1)} %get-tuple-element.45, f32[]{:T(128)} %bitcast.4, f32[]{:T(128)} %bitcast.3), kind=kLoop, calls=%fused_computation | loop fusion | flops 393216 | bytes 1572872 | tf_op jit(solution)/shard_map/add | solution.py:802
  68.2 7.9 %all-to-all-done.1 = f32[128,2,128]{2,1,0:T(2,128)S(1)} async-done(((f32[128,2,128]{2,1,0:T(2,128)}), f32[128,2,128]{2,1,0:T(2,128)S(1)}, u32[]{:S(2)}, u32[]{:S(2)}) %all-to-all-start.1) | async-done | bytes 131104 | tf_op jit(solution)/shard_map/all_to_all | solution.py:804
  76.0 1.0 %to_owner.1 = f32[128,128]{1,0:T(8,128)} custom-call(s32[128,128]{1,0:T(8,128)S(1)} %get-tuple-element.30.ids_ref, f32[256,128]{1,0:T(8,128)S(1)} %bitcast.9), custom_call_target="tpu_custom_call" | custom-call | tf_op jit(solution)/shard_map/to_owner/pallas_call | solution.py:773
  (1 shorter events, 0.0 us)
Async XLA Ops:
  2.1 4.1 %collective-permute-start = (f32[16,8,128]{2,1,0:T(8,128)S(1)}, f32[16,8,128]{2,1,0:T(8,128)S(1)}, u32[]{:S(2)}, u32[]{:S(2)}) collective-permute-start(f32[16,8,128]{2,1,0:T(8,128)S(1)} %get-tuple-element.34), channel_id=1, source_target_pairs={{0,16},{16,0},{32,48},{48,32},{64,80},{80,64},{96,112},{112,96},{1... | collective-permute-start | bytes 196616 | tf_op jit(solution)/shard_map/ppermute | solution.py:80
  3.6 4.0 %collective-permute-start.1 = (f32[16,8,128]{2,1,0:T(8,128)S(1)}, f32[16,8,128]{2,1,0:T(8,128)S(1)}, u32[]{:S(2)}, u32[]{:S(2)}) collective-permute-start(f32[16,8,128]{2,1,0:T(8,128)S(1)} %get-tuple-element.35), channel_id=1, source_target_pairs={{0,112},{16,32},{32,16},{48,64},{64,48},{80,96},{96,80},{112,0},{1... | collective-permute-start | bytes 196616 | tf_op jit(solution)/shard_map/ppermute | solution.py:80
  7.8 9.0 %collective-permute-start.3 = (f32[3,80,128]{2,1,0:T(8,128)S(1)}, f32[3,80,128]{2,1,0:T(8,128)S(1)}, u32[]{:S(2)}, u32[]{:S(2)}) collective-permute-start(f32[3,80,128]{2,1,0:T(8,128)S(1)} %get-tuple-element.38.strip_ref), channel_id=1, source_target_pairs={{0,15},{1,2},{2,1},{3,4},{4,3},{5,6},{6,5},{7,8},{8,7},{9,10},{10,... | collective-permute-start | bytes 368648 | tf_op jit(solution)/shard_map/ppermute | solution.py:80
  14.1 3.9 %collective-permute-start.2 = (f32[3,80,128]{2,1,0:T(8,128)S(1)}, f32[3,80,128]{2,1,0:T(8,128)S(1)}, u32[]{:S(2)}, u32[]{:S(2)}) collective-permute-start(f32[3,80,128]{2,1,0:T(8,128)S(1)} %get-tuple-element.38.strip_ref), channel_id=1, source_target_pairs={{0,1},{1,0},{2,3},{3,2},{4,5},{5,4},{6,7},{7,6},{8,9},{9,8},{10,11... | collective-permute-start | bytes 368648 | tf_op jit(solution)/shard_map/ppermute | solution.py:80
  50.8 5.9 %collective-permute-start.7 = (f32[8,256]{1,0:T(8,128)S(1)}, f32[8,256]{1,0:T(8,128)S(1)}, u32[]{:S(2)}, u32[]{:S(2)}) collective-permute-start(f32[8,256]{1,0:T(8,128)S(1)} %get-tuple-element.51), channel_id=1, source_target_pairs={{0,15},{1,2},{2,1},{3,4},{4,3},{5,6},{6,5},{7,8},{8,7},{9,10},{10,... | collective-permute-start | bytes 24584 | tf_op jit(solution)/shard_map/ppermute | solution.py:80
  51.5 5.2 %collective-permute-start.6 = (f32[8,256]{1,0:T(8,128)S(1)}, f32[8,256]{1,0:T(8,128)S(1)}, u32[]{:S(2)}, u32[]{:S(2)}) collective-permute-start(f32[8,256]{1,0:T(8,128)S(1)} %get-tuple-element.51), channel_id=1, source_target_pairs={{0,1},{1,0},{2,3},{3,2},{4,5},{5,4},{6,7},{7,6},{8,9},{9,8},{10,11... | collective-permute-start | bytes 24584 | tf_op jit(solution)/shard_map/ppermute | solution.py:80
  51.7 5.0 %collective-permute-start.5 = (f32[32,128]{1,0:T(8,128)S(1)}, f32[32,128]{1,0:T(8,128)S(1)}, u32[]{:S(2)}, u32[]{:S(2)}) collective-permute-start(f32[32,128]{1,0:T(8,128)S(1)} %get-tuple-element.50), channel_id=1, source_target_pairs={{0,112},{16,32},{32,16},{48,64},{64,48},{80,96},{96,80},{112,0},{1... | collective-permute-start | bytes 49160 | tf_op jit(solution)/shard_map/ppermute | solution.py:80
  52.9 3.9 %collective-permute-start.4 = (f32[32,128]{1,0:T(8,128)S(1)}, f32[32,128]{1,0:T(8,128)S(1)}, u32[]{:S(2)}, u32[]{:S(2)}) collective-permute-start(f32[32,128]{1,0:T(8,128)S(1)} %get-tuple-element.50), channel_id=1, source_target_pairs={{0,16},{16,0},{32,48},{48,32},{64,80},{80,64},{96,112},{112,96},{1... | collective-permute-start | bytes 49160 | tf_op jit(solution)/shard_map/ppermute | solution.py:80
  59.0 17.0 %all-to-all-start.1 = ((f32[128,2,128]{2,1,0:T(2,128)}), f32[128,2,128]{2,1,0:T(2,128)S(1)}, u32[]{:S(2)}, u32[]{:S(2)}) async-start(f32[128,2,128]{2,1,0:T(2,128)} %bitcast.5), calls=%async_computation.1 | async-start | bytes 262144 | tf_op jit(solution)/shard_map/all_to_all | solution.py:804

commit v4 on v3

--- a/solution.py
+++ b/solution.py
@@ -92,51 +92,45 @@
     return copies
 
 
-def load_kernel(
-    k_hbm, s_hbm, r_hbm, ids_hbm, conc_hbm, sorp_hbm,
-    first_ref, second_ref, k_ref, s_ref, r_ref, ids_ref, conc_ref, sorp_ref, sems,
-):
-    copies = fetch(
-        [
-            (k_hbm, k_ref),
-            (s_hbm, s_ref),
-            (r_hbm, r_ref),
-            (ids_hbm, ids_ref),
-            (conc_hbm, conc_ref),
-            (sorp_hbm, sorp_ref),
-        ],
-        sems,
-    )
-    for copy in copies:
+def pinned(arrays):
+    return tuple(pltpu.with_memory_space_constraint(x, pltpu.HBM) for x in arrays)
+
+
+def edges_kernel(k_hbm, s_hbm, r_hbm, first_ref, second_ref, tiles, sems):
+    rows = k_hbm.shape[1]
+    pairs = []
+    for i, ref in enumerate((k_hbm, s_hbm, r_hbm)):
+        pairs.append((ref.at[:, pl.ds(rows - 8, 8), :], tiles.at[2 * i]))
+        pairs.append((ref.at[:, pl.ds(0, 8), :], tiles.at[2 * i + 1]))
+    for copy in fetch(pairs, sems):
         copy.wait()
-    high = k_ref.shape[1] - 8
     sub = iota(first_ref.shape[1:], 0)
     for z in range(first_ref.shape[0]):
         east = jnp.where(
             sub >= 5,
-            k_ref[z, high:],
-            jnp.where(sub >= 3, roll(s_ref[z, high:], -3, 0), roll(r_ref[z, high:], -5, 0)),
+            tiles[0, z],
+            jnp.where(sub >= 3, roll(tiles[2, z], -3, 0), roll(tiles[4, z], -5, 0)),
         )
         west = jnp.where(
             sub < 3,
-            k_ref[z, :8],
-            jnp.where(sub < 5, roll(s_ref[z, :8], 3, 0), roll(r_ref[z, :8], 5, 0)),
+            tiles[1, z],
+            jnp.where(sub < 5, roll(tiles[3, z], 3, 0), roll(tiles[5, z], 5, 0)),
         )
         first_ref[z], second_ref[z] = by_turns("gx", west, east)
 
 
-def load(*arrays):
+def pack_edges(*arrays):
     layers, rows, width = arrays[0].shape
     tile = jax.ShapeDtypeStruct((layers, 8, width), F32)
     return pl.pallas_call(
-        load_kernel,
-        in_specs=[HBM] * 6,
-        out_specs=[VMEM] * 8,
-        out_shape=[tile, tile] + [jax.ShapeDtypeStruct(x.shape, x.dtype) for x in arrays],
-        scratch_shapes=[pltpu.SemaphoreType.DMA((6,))],
+        edges_kernel,
+        in_specs=[HBM] * 3,
+        out_specs=[VMEM] * 2,
+        out_shape=[tile, tile],
+        scratch_shapes=[pltpu.VMEM((6, layers, 8, width), F32), pltpu.SemaphoreType.DMA((6,))],
         compiler_params=params(8),
-        name="load",
-    )(*(pltpu.with_memory_space_constraint(x, pltpu.HBM) for x in arrays))
+        name="pack_edges",
+    )(*pinned(arrays))
 
 
 def beside(index, z, west_ref, east_ref):
@@ -160,7 +154,7 @@
     return strip
 
 
-def strip_kernel(inner_ref, first_ref, second_ref, out_ref, west_ref, east_ref):
+def strip_kernel(inner_ref, first_ref, second_ref, out_ref, west_ref, east_ref, one_ref, other_ref):
     layers = west_ref.shape[0]
     west_ref[...], east_ref[...] = from_turns("gx", first_ref[...], second_ref[...])
     rows = inner_ref.shape[1]
@@ -168,6 +162,11 @@
         out_ref[index, 8 : 8 + rows] = inner_ref[index]
         out_ref[index, 0:8] = strip_of(layers, lambda z: beside(index, z, west_ref, east_ref)[0])
         out_ref[index, 8 + rows :] = strip_of(layers, lambda z: beside(index, z, west_ref, east_ref)[1])
+    k, s, r = out_ref[0], out_ref[1], out_ref[2]
+    slot = iota(k.shape, 1) % 8
+    south = jnp.where(slot >= 4, k, jnp.where(slot >= 2, roll(s, -2, 1), roll(r, -4, 1)))
+    north = jnp.where(slot < 4, k, jnp.where(slot < 6, roll(s, 2, 1), roll(r, 4, 1)))
+    one_ref[...], other_ref[...] = by_turns("gy", south, north)
 
 
 def pack_strip(inner, first, second):
@@ -175,7 +174,8 @@
     tile = jax.ShapeDtypeStruct(first.shape, F32)
     return pl.pallas_call(
         strip_kernel,
-        out_shape=[jax.ShapeDtypeStruct((3, rows + 16, width), F32), tile, tile],
+        out_shape=[jax.ShapeDtypeStruct((3, rows + 16, width), F32), tile, tile]
+        + [jax.ShapeDtypeStruct((rows + 16, width), F32)] * 2,
         compiler_params=params(4),
         name="pack_strip",
     )(inner, first, second)
@@ -191,47 +191,116 @@
     return jnp.sum(jnp.where(iota((n, n), 0) == iota((n, n), 1), col, 0.0), 0, keepdims=True)
 
 
-def prepare_kernel(
-    down, across, k_ref, s_ref, r_ref, ids_ref, conc_ref, sorp_ref, inner_ref, out_ref, col_ref, row_ref
+def slot_codes(ids, target, lines):
+    brick = ids // lines
+    key = iota(ids.shape, 1) * lines + ids % lines
+    mine = brick == target
+    first = jnp.min(jnp.where(mine, key, ids.shape[1] * lines).astype(F32), 1, keepdims=True)
+    second = jnp.max(jnp.where(mine, key, -1).astype(F32), 1, keepdims=True)
+    cols = [
+        jnp.where(second >= 0.0, code.astype(jnp.int32) % lines, NONE).astype(F32)
+        for code in (first, second)
+    ]
+    rows = [as_row(col) for col in cols]
+    return jnp.concatenate(cols, 0).astype(jnp.int32), jnp.concatenate(rows, 1).astype(jnp.int32)
+
+
+def load_kernel(
+    down, across,
+    k_hbm, s_hbm, r_hbm, ids_hbm, conc_hbm, sorp_hbm,
+    k_ref, s_ref, r_ref, ids_ref, conc_ref, sorp_ref, own_ref,
+    inner_ref, ends_ref, sides_ref, edges_ref, pick_ref, slots_ref,
+    sems,
 ):
+    refs = (k_ref, s_ref, r_ref)
+    copies = fetch(
+        [
+            (ids_hbm, ids_ref),
+            (k_hbm, k_ref),
+            (s_hbm, s_ref),
+            (r_hbm, r_ref),
+            (conc_hbm, conc_ref),
+            (sorp_hbm, sorp_ref),
+        ],
+        sems,
+    )
     layers, rows_x = k_ref.shape[:2]
+    slots = slots_ref.shape[1]
+    lines = layers * rows_x
+    me = place()
+    gx, gy = me // across, me % across
+    copies[0].wait()
+    ids = ids_ref[...]
+    code, slot = slot_codes(ids, me, lines)
+    west, _ = slot_codes(ids, jnp.where(gx > 0, me - across, -1), lines)
+    east, _ = slot_codes(ids, jnp.where(gx < down - 1, me + across, -1), lines)
+    south, _ = slot_codes(ids, jnp.where(gy > 0, me - 1, -1), lines)
+    north, _ = slot_codes(ids, jnp.where(gy < across - 1, me + 1, -1), lines)
+    slots_ref[...] = slot
+    active = slot >= 0
+    layer, row = slot // rows_x, slot % rows_x
+    low, high = active & (row == 0), active & (row == rows_x - 1)
+
+    def ones(mask):
+        return jnp.where(mask, 1.0, 0.0).astype(BF16)
+
+    inner_ref[:, :slots] = ones((code == slot - 1) & (row != 0))
+    inner_ref[:, slots : 2 * slots] = ones((code == slot + 1) & (row != rows_x - 1))
+    inner_ref[:, 2 * slots : 3 * slots] = ones(code == slot - rows_x)
+    inner_ref[:, 3 * slots :] = ones(code == slot + rows_x)
+    ends_ref[:, :slots] = ones((south == slot) & active)
+    ends_ref[:, slots:] = ones((north == slot) & active)
+    sides_ref[:, :slots] = ones((west == slot + rows_x - 1) & low)
+    sides_ref[:, slots:] = ones((east == slot - rows_x + 1) & high)
+    at = iota((edges_ref.shape[0], slots), 0)
+    edges_ref[:, :slots] = ones((at == layer) & low)
+    edges_ref[:, slots:] = ones((at == layer + layers) & high)
+    at = iota((slots, pick_ref.shape[1]), 1)
+    pick_ref[...] = ones(
+        (code >= 0)
+        & (
+            ((code % rows_x == rows_x - 1) & (code // rows_x == at))
+            | ((code % rows_x == 0) & (code // rows_x + layers == at))
+        )
+    )
+    for index, ref in enumerate(refs):
+        copies[1 + index].wait()
+        own_ref[index] = strip_of(layers, lambda z: ref[z])
+    copies[4].wait()
+    copies[5].wait()
+
+
+def load(*arrays):
+    rows, width = arrays[0].shape[1:]
+    layers = arrays[0].shape[0]
+    slots = 2 * arrays[3].shape[0]
+    kernel = functools.partial(load_kernel, lax.axis_size("gx"), lax.axis_size("gy"))
+    return pl.pallas_call(
+        kernel,
+        in_specs=[HBM] * 6,
+        out_specs=[VMEM] * 13,
+        out_shape=[jax.ShapeDtypeStruct(x.shape, x.dtype) for x in arrays]
+        + [
+            jax.ShapeDtypeStruct((3, rows, width), F32),
+            jax.ShapeDtypeStruct((slots, 4 * slots), BF16),
+            jax.ShapeDtypeStruct((slots, 2 * slots), BF16),
+            jax.ShapeDtypeStruct((slots, 2 * slots), BF16),
+            jax.ShapeDtypeStruct((2 * layers, 2 * slots), BF16),
+            jax.ShapeDtypeStruct((slots, width), BF16),
+            jax.ShapeDtypeStruct((1, slots), jnp.int32),
+        ],
+        scratch_shapes=[pltpu.SemaphoreType.DMA((6,))],
+        compiler_params=params(8),
+        name="load",
+    )(*pinned(arrays))
+
+
+def send_kernel(
+    across, rows_x, layers, ids_ref, conc_ref, sorp_ref, out_ref, mask_ref
+):
     devices, owned = ids_ref.shape
     lines = layers * rows_x
     me = place()
-    ids = ids_ref[...]
-    brick = ids // lines
-    key = iota(ids.shape, 1) * lines + ids % lines
-    gx, gy = me // across, me % across
-    cols, rows = [], []
-    for target, ok, edge in (
-        (me, None, None),
-        (me - across, gx > 0, rows_x - 1),
-        (me + across, gx < down - 1, 0),
-        (me - 1, gy > 0, None),
-        (me + 1, gy < across - 1, None),
-    ):
-        if ok is not None:
-            target = jnp.where(ok, target, -1)
-        mine = brick == target
-        first = jnp.min(jnp.where(mine, key, owned * lines).astype(F32), 1, keepdims=True)
-        second = jnp.max(jnp.where(mine, key, -1).astype(F32), 1, keepdims=True)
-        for code in (first, second):
-            line = code.astype(jnp.int32) % lines
-            keep = second >= 0.0
-            if edge is not None:
-                keep = keep & (line % rows_x == edge)
-                line = line // rows_x
-            value = jnp.where(keep, line, NONE).astype(F32)
-            cols.append(value)
-            rows.append(as_row(value))
-    lane = iota((devices, 128), 1)
-    packed = jnp.zeros((devices, 128), F32)
-    for at, value in enumerate(cols):
-        packed = jnp.where(lane == at, value, packed)
-    col_ref[...] = packed.astype(jnp.int32)
-    row_ref[...] = jnp.concatenate(
-        rows + [jnp.zeros((16 - len(rows), devices), F32)], 0
-    ).astype(jnp.int32)
     own = ids_ref[pl.ds(me, 1), :]
     own_brick = own // lines
     own_row = own % lines % rows_x
@@ -239,6 +308,8 @@
     square = (owned, owned)
     same = (brick_col == own_brick) & (iota(square, 0) < iota(square, 1))
     rank = jnp.sum(jnp.where(same, 1.0, 0.0), 0, keepdims=True).astype(jnp.int32)
+    back = jnp.where(iota((2 * devices, owned), 0) == own_brick * 2 + rank, 1.0, 0.0)
+    mask_ref[...] = back.T.astype(BF16)
     dest = iota((devices, owned), 0)
     conc = conc_ref[...]
     conc_parts = split(conc)
@@ -260,35 +331,66 @@
         south = (dest == own_brick - 1) & ranked & (own_brick % across > 0)
         misc = misc + pick(north, split(tails)) + pick(south, split(heads))
     out_ref[pl.ds(8, devices, stride=ROWS), :] = misc
-    for index, ref in enumerate((k_ref, s_ref, r_ref)):
-        inner_ref[index] = strip_of(layers, lambda z: ref[z])
-
-
-def prepare(conductivity, storage, recharge, ids, concentration, sorption):
+
+
+def pack_send(ids, concentration, sorption, layers, rows_x):
     devices, owned = ids.shape
-    layers, rows_x, width = conductivity.shape
-    kernel = functools.partial(prepare_kernel, lax.axis_size("gx"), lax.axis_size("gy"))
+    width = concentration.shape[1]
+    slots = 2 * devices
+    kernel = functools.partial(send_kernel, lax.axis_size("gy"), rows_x, layers)
     return pl.pallas_call(
         kernel,
         out_shape=[
-            jax.ShapeDtypeStruct((3, rows_x, width), F32),
             jax.ShapeDtypeStruct((devices * ROWS, width), F32),
-            jax.ShapeDtypeStruct((devices, 128), jnp.int32),
-            jax.ShapeDtypeStruct((16, devices), jnp.int32),
+            jax.ShapeDtypeStruct((owned, slots), BF16),
         ],
         compiler_params=params(8),
-        name="prepare",
-    )(conductivity, storage, recharge, ids, concentration, sorption)
+        name="pack_send",
+    )(ids, concentration, sorption)
 
 
 def harmonic(a, c):
     return jnp.where(jnp.minimum(a, c) > 0.0, 2.0 * a * c / (a + c), jnp.maximum(a, c))
 
 
+def faces_kernel(k_ref, s_ref, west_ref, east_ref, fw, fs, fb, part):
+    layers, rows, width = k_ref.shape
+    shape = (rows + 16, width)
+    lane = iota(shape, 1)
+    fb[0] = jnp.zeros(shape, F32)
+
+    def step(z, carry):
+        k = widened(0, z, k_ref, west_ref, east_ref)
+        face_w = harmonic(k, roll(k, 1, 0))
+        face_s = jnp.where(lane == 0, 0.0, harmonic(k, roll(k, 1, 1)))
+        upper = widened(0, jnp.minimum(z + 1, layers - 1), k_ref, west_ref, east_ref)
+        face_a = jnp.where(z < layers - 1, VERTICAL * harmonic(k, upper), 0.0)
+        s = widened(1, z, s_ref, west_ref, east_ref)
+        fw[z] = face_w
+        fs[z] = face_s
+        part[z] = s + face_w + roll(face_w, -1, 0) + face_s + roll(face_s, -1, 1) + fb[z] + face_a
+        fb[z + 1] = face_a
+        return carry
+
+    lax.fori_loop(0, layers, step, 0, unroll=2)
+
+
+def faces_of(conductivity, storage, west, east):
+    layers, rows, width = conductivity.shape
+    tall = jax.ShapeDtypeStruct((layers, rows + 16, width), F32)
+    return pl.pallas_call(
+        faces_kernel,
+        out_shape=[tall, tall, jax.ShapeDtypeStruct((layers + 1, rows + 16, width), F32), tall],
+        compiler_params=params(8),
+        name="faces",
+    )(conductivity, storage, west, east)
+
+
 def flow_kernel(
     k_ref, s_ref, r_ref, west_ref, east_ref, strip_ref, first_ref, second_ref, send_ref, slots_ref,
+    fw, fs, fb, part,
     d_out, w_out, gath_out, send_out,
-    kx, sx, fw, fs, fb, rd, dd, ww, lines_ref,
+    rd, dd, ww, lines_ref,
 ):
     layers, rows, width = k_ref.shape
     tall = rows + 16
@@ -301,10 +403,11 @@
 
     def side(low):
         def joined(index):
-            south, north = from_turns("gy", first_ref[index], second_ref[index])
+            south, north = from_turns("gy", first_ref[...], second_ref[...])
+            shift = 2 * index
             if low:
-                return jnp.where(slot < 4, south, strip_ref[index])
-            return jnp.where(slot < 4, strip_ref[index], north)
+                return jnp.where(slot < 4, roll(south, -shift, 1), strip_ref[index])
+            return jnp.where(slot < 4, strip_ref[index], roll(north, shift, 1))
 
         k, s, r = joined(0), joined(1), joined(2)
         face_w = harmonic(k, roll(k, 1, 0))
@@ -337,33 +440,19 @@
         shift = lax.rem(width - 5 + width - z * 8, width)
         return jnp.where(lane == width - 1, roll(strip, shift, 1), roll(field, -1, 1))
 
-    def widen(z, carry):
-        kx[z] = widened(0, z, k_ref, west_ref, east_ref)
-        return carry
-
-    lax.fori_loop(0, layers, widen, 0, unroll=4)
-    fb[0] = jnp.zeros(shape, F32)
-
-    def faces(z, carry):
-        k = kx[z]
-        face_w = harmonic(k, roll(k, 1, 0))
-        face_s = with_low(z, harmonic(k, roll(k, 1, 1)), low_face)
-        face_n = north_of(z, face_s, high_face)
-        upper = kx[jnp.minimum(z + 1, layers - 1)]
-        face_a = jnp.where(z < layers - 1, VERTICAL * harmonic(k, upper), 0.0)
-        s = widened(1, z, s_ref, west_ref, east_ref)
+    def scale(z, carry):
+        k = widened(0, z, k_ref, west_ref, east_ref)
         r = widened(2, z, r_ref, west_ref, east_ref)
-        diagonal = s + face_w + roll(face_w, -1, 0) + face_s + face_n + fb[z] + face_a
+        low = jnp.where(lane == 0, roll(low_face, width - 4 - z * 8, 1), 0.0)
+        shift = lax.rem(width - 5 + width - z * 8, width)
+        high = jnp.where(lane == width - 1, roll(high_face, shift, 1), 0.0)
+        diagonal = part[z] + low + high
         inverse = jnp.where(k > 0.0, 1.0 / diagonal, 0.0)
-        fw[z] = face_w
-        fs[z] = face_s
-        fb[z + 1] = face_a
         rd[z] = inverse
         dd[z] = r * inverse
-        sx[z] = s
         return carry
 
-    lax.fori_loop(0, layers, faces, 0, unroll=2)
+    lax.fori_loop(0, layers, scale, 0, unroll=8)
 
     def total(x):
         return jnp.sum(x[8 : 8 + rows].reshape(rows // 8, 8, width), 0)
@@ -381,7 +470,8 @@
         for at, flux in enumerate((flux_w, flux_e, flux_b, flux_a, flux_s, flux_n)):
             start = z * (rows * 16) + (block + at)
             lines_ref[pl.ds(start, rows, stride=16), :] = flux[8 : 8 + rows]
-        return h, sx[z] * h + (flux_e - flux_w) + (flux_a - flux_b) + (flux_n - flux_s)
+        s = widened(1, z, s_ref, west_ref, east_ref)
+        return h, s * h + (flux_e - flux_w) + (flux_a - flux_b) + (flux_n - flux_s)
 
     zero = jnp.zeros((8, width), F32)
 
@@ -395,13 +485,13 @@
         gamma = jnp.sum((r * d[8 : 8 + rows]).reshape(rows // 8, 8, width), 0)
         return sums[0] + gamma, sums[1] + total(d * image), sums[2] + total(image * w)
 
-    gamma, bend, curve = lax.fori_loop(0, layers, first, (zero, zero, zero), unroll=2)
+    gamma, bend, curve = lax.fori_loop(0, layers, first, (zero, zero, zero), unroll=8)
 
     def second(z, acc):
         w, image = apply(z, ww, low_w, high_w, 6)
         return acc + total(w * image)
 
-    twist = lax.fori_loop(0, layers, second, zero, unroll=2)
+    twist = lax.fori_loop(0, layers, second, zero, unroll=8)
     lane_row = iota((devices, width), 1)
     misc = send_ref[pl.ds(8, devices, stride=ROWS), :]
     for at, part in enumerate((gamma, bend, curve, twist)):
@@ -411,7 +501,7 @@
     for k in range(2):
 
         def gather(i, carry):
-            line = pl.multiple_of(jnp.maximum(slots_ref[k, i], 0) * 16, 16)
+            line = pl.multiple_of(jnp.maximum(slots_ref[0, k * devices + i], 0) * 16, 16)
             slot = pl.multiple_of((k * devices + i) * 16, 16)
             gath_out[pl.ds(slot, 16), :] = lines_ref[pl.ds(line, 16), :]
             return carry
@@ -419,7 +509,7 @@
         lax.fori_loop(0, devices, gather, 0, unroll=8)
 
 
-def flow(conductivity, storage, recharge, west, east, strip, first, second, send, slots):
+def flow(conductivity, storage, recharge, west, east, strip, first, second, send, slots, faces):
     layers, rows, width = conductivity.shape
     tall = pltpu.VMEM((layers, rows + 16, width), F32)
     return pl.pallas_call(
@@ -427,18 +517,15 @@
         out_shape=[
             jax.ShapeDtypeStruct(conductivity.shape, F32),
             jax.ShapeDtypeStruct(conductivity.shape, F32),
-            jax.ShapeDtypeStruct((2 * slots.shape[1] * 16, width), F32),
+            jax.ShapeDtypeStruct((slots.shape[1] * 16, width), F32),
             jax.ShapeDtypeStruct(send.shape, F32),
         ],
-        in_specs=[VMEM] * 9 + [SMEM],
+        in_specs=[VMEM] * 9 + [SMEM] + [VMEM] * 4,
         out_specs=[VMEM] * 4,
-        scratch_shapes=[tall] * 4
-        + [pltpu.VMEM((layers + 1, rows + 16, width), F32)]
-        + [tall] * 3
-        + [pltpu.VMEM((layers * rows * 16, width), F32)],
-        compiler_params=params(30),
+        scratch_shapes=[tall] * 3 + [pltpu.VMEM((layers * rows * 16, width), F32)],
+        compiler_params=params(20),
         name="flow",
-    )(conductivity, storage, recharge, west, east, strip, first, second, send, slots)
+    )(conductivity, storage, recharge, west, east, strip, first, second, send, slots, *faces)
 
 
 CHUNK = 16
@@ -473,8 +560,7 @@
     return jnp.concatenate(split(x), 0)
 
 
-def take(parts, mask):
-    chosen = jnp.where(mask, 1.0, 0.0).astype(BF16)
+def take(parts, chosen):
     out = jnp.dot(parts, chosen, preferred_element_type=F32)
     count = parts.shape[0] // 3
     return (out[2 * count :] + out[count : 2 * count]) + out[:count]
@@ -589,33 +675,21 @@
     return [x[j * count : (j + 1) * count] for j in range(CHUNK)]
 
 
-def both(x, at, axis):
-    if axis:
-        return jnp.concatenate([x[at : at + 1], x[at + 1 : at + 2]], 1)
-    return jnp.concatenate([x[:, at : at + 1], x[:, at + 1 : at + 2]], 0)
-
-
-def inner_neighbours(c, cols, rows, rows_x):
-    own_c, own_r = both(cols, 0, 0), both(rows, 0, 1)
-    at = own_r % rows_x
-    parts = stacked(c)
-    west = take(parts, (own_c == own_r - 1) & (at != 0))
-    east = take(parts, (own_c == own_r + 1) & (at != rows_x - 1))
-    lower = take(parts, own_c == own_r - rows_x)
-    upper = take(parts, own_c == own_r + rows_x)
-    return west, east, lower, upper
-
-
-def end_values(south, north, cols, rows):
-    own_r = both(rows, 0, 1)
-    active = own_r >= 0
-    tails = take(stacked(south), (both(cols, 6, 0) == own_r) & active)
-    heads = take(stacked(north), (both(cols, 8, 0) == own_r) & active)
+def inner_neighbours(c, chosen):
+    slots = c.shape[1]
+    values = take(stacked(c), chosen)
+    return [values[:, i * slots : (i + 1) * slots] for i in range(4)]
+
+
+def end_values(south, north, chosen):
+    slots = south.shape[1]
+    tails = take(stacked(south), chosen[:, :slots])
+    heads = take(stacked(north), chosen[:, slots:])
     return tails[0:1], tails[1:2], heads[2:3], heads[3:4]
 
 
 def first_kernel(
-    rows_x, layers, recv_ref, gath_ref, col_ref, row_ref,
+    recv_ref, gath_ref, inner_ref, ends_ref, sides_ref, pick_ref,
     c_out, s_out, flux_out, edge_out, end_out, scal_out, scratch,
 ):
     devices = recv_ref.shape[0] // ROWS
@@ -628,7 +702,6 @@
     def pair(at):
         return jnp.concatenate([received(at), received(at + 1)], 0)
 
-    cols, rows = col_ref[...], row_ref[...]
     misc = received(8)
     sums = jnp.sum(misc, 0, keepdims=True)
     at = iota(sums.shape, 1)
@@ -662,18 +735,15 @@
         else:
             flux_out[i] = flux
             fluxes.append(tiles_of(flux))
-    west, east, lower, upper = inner_neighbours(c, cols, rows, rows_x)
-    own_c, own_r = both(cols, 0, 0), both(rows, 0, 1)
-    layer, row = own_r // rows_x, own_r % rows_x
-    active = own_r >= 0
-    west = west + take(stacked(beside_w), (both(cols, 2, 0) == layer) & active & (row == 0))
-    east = east + take(stacked(beside_e), (both(cols, 4, 0) == layer) & active & (row == rows_x - 1))
+    west, east, lower, upper = inner_neighbours(c, inner_ref[...])
+    west = west + take(stacked(beside_w), sides_ref[:, :slots])
+    east = east + take(stacked(beside_e), sides_ref[:, slots:])
     turned = misc.T
     ends = [
         jnp.concatenate([turned[a : a + 1], turned[a + 2 : a + 3]], 1) for a in (0, 1, 4, 5)
     ] + [jnp.zeros((4, slots), F32)]
     ends = jnp.concatenate(ends, 0)
-    ends = end_values(ends, ends, cols, rows)
+    ends = end_values(ends, ends, ends_ref[...])
     tiles = transport(
         tiles_of(c), tiles_of(s), fluxes, tiles_of(west), tiles_of(east), tiles_of(lower), tiles_of(upper), ends
     )
@@ -690,54 +760,46 @@
         ],
         0,
     )
-    lane = iota((slots, width), 1)
-    high = (own_c % rows_x == rows_x - 1) & (own_c // rows_x == lane)
-    low = (own_c % rows_x == 0) & (own_c // rows_x + layers == lane)
-    edge = take(stacked(c), (high | low) & (own_c >= 0))
-    edge_out[...] = edge.T[: 2 * layers]
-
-
-def first_step(received, gathered, cols, rows, layers, rows_x):
+    edge = take(stacked(c), pick_ref[...])
+    edge_out[...] = edge.T[: edge_out.shape[0]]
+
+
+def first_step(received, gathered, inner, ends, sides, picks, layers):
     width = received.shape[1]
-    devices = cols.shape[0]
-    cells = jax.ShapeDtypeStruct((width, 2 * devices), F32)
+    slots = inner.shape[0]
+    cells = jax.ShapeDtypeStruct((width, slots), F32)
     return pl.pallas_call(
-        functools.partial(first_kernel, rows_x, layers),
+        first_kernel,
         out_shape=[
             cells,
             cells,
-            jax.ShapeDtypeStruct((6, width, 2 * devices), F32),
+            jax.ShapeDtypeStruct((6, width, slots), F32),
             jax.ShapeDtypeStruct((2 * layers, width), F32),
-            jax.ShapeDtypeStruct((8, 2 * devices), F32),
+            jax.ShapeDtypeStruct((8, slots), F32),
             jax.ShapeDtypeStruct((8, width), F32),
         ],
-        scratch_shapes=[pltpu.VMEM((10, 2, width, devices), F32)],
+        scratch_shapes=[pltpu.VMEM((10, 2, width, slots // 2), F32)],
         compiler_params=params(16),
         name="first_step",
-    )(received, gathered, cols, rows)
+    )(received, gathered, inner, ends, sides, picks)
 
 
 def second_kernel(
-    rows_x, c_ref, s_ref, flux_ref, col_ref, row_ref, edge1_ref, edge2_ref, end1_ref, end2_ref, out_ref, scratch
+    c_ref, s_ref, flux_ref, inner_ref, ends_ref, edges_ref, edge1_ref, edge2_ref, end1_ref, end2_ref, out_ref, scratch
 ):
     c, s = c_ref[...], s_ref[...]
-    width = c.shape[0]
-    devices = c.shape[1] // 2
-    cols, rows = col_ref[...], row_ref[...]
-    west, east, lower, upper = inner_neighbours(c, cols, rows, rows_x)
+    width, slots = c.shape
+    devices = slots // 2
+    west, east, lower, upper = inner_neighbours(c, inner_ref[...])
     west_edge, east_edge = from_turns("gx", edge1_ref[...], edge2_ref[...])
-    layers = west_edge.shape[0] // 2
-    own_r = both(rows, 0, 1)
-    layer, row = own_r // rows_x, own_r % rows_x
-    active = own_r >= 0
-    code = iota((width, 2 * devices), 0)
-    rest = jnp.zeros((width - 2 * layers, width), F32)
-    west_edge = jnp.concatenate([west_edge, rest], 0).T
-    east_edge = jnp.concatenate([east_edge, rest], 0).T
-    west = west + take(stacked(west_edge), (code == layer) & active & (row == 0))
-    east = east + take(stacked(east_edge), (code == layer + layers) & active & (row == rows_x - 1))
+    rest = jnp.zeros((width - west_edge.shape[0], width), F32)
+    count = west_edge.shape[0]
+    west_edge = jnp.concatenate([west_edge, rest], 0).T[:, :count]
+    east_edge = jnp.concatenate([east_edge, rest], 0).T[:, :count]
+    west = west + take(stacked(west_edge), edges_ref[:, :slots])
+    east = east + take(stacked(east_edge), edges_ref[:, slots:])
     south, north = from_turns("gy", end1_ref[...], end2_ref[...])
-    ends = end_values(south, north, cols, rows)
+    ends = end_values(south, north, ends_ref[...])
     fluxes = [tiles_of(flux_ref[i]) for i in range(5)] + [flux_ref[5, : width // CHUNK]]
     tiles = transport(
         tiles_of(c), tiles_of(s), fluxes, tiles_of(west), tiles_of(east), tiles_of(lower), tiles_of(upper), ends
@@ -746,36 +808,32 @@
         out_ref[pl.ds(k, devices, stride=2), :] = lines
 
 
-def second_step(c, s, fluxes, cols, rows, edges, ends, rows_x):
+def second_step(c, s, fluxes, inner, ends, edges, edge, end):
     width, slots = c.shape
     return pl.pallas_call(
-        functools.partial(second_kernel, rows_x),
+        second_kernel,
         out_shape=jax.ShapeDtypeStruct((slots, width), F32),
         scratch_shapes=[pltpu.VMEM((2, width, slots // 2), F32)],
         compiler_params=params(16),
         name="second_step",
-    )(c, s, fluxes, cols, rows, *edges, *ends)
-
-
-def owner_kernel(lines, ids_ref, recv_ref, out_ref):
-    devices, owned = ids_ref.shape
-    own = ids_ref[pl.ds(place(), 1), :]
-    brick = own // lines
-    brick_col = column(brick.astype(F32)).astype(jnp.int32)
-    square = (owned, owned)
-    same = (brick_col == brick) & (iota(square, 1) < iota(square, 0))
-    rank = jnp.sum(jnp.where(same, 1.0, 0.0), 1, keepdims=True).astype(jnp.int32)
-    mask = brick_col * 2 + rank == iota((owned, 2 * devices), 1)
-    out_ref[...] = pick(mask, split(recv_ref[...]))
-
-
-def to_owner(ids, received, lines):
+    )(c, s, fluxes, inner, ends, edges, *edge, *end)
+
+
+def owner_kernel(mask_ref, recv_ref, out_ref):
+    chosen = mask_ref[...]
+    high, middle, low = (
+        jnp.dot(chosen, part, preferred_element_type=F32) for part in split(recv_ref[...])
+    )
+    out_ref[...] = (low + middle) + high
+
+
+def to_owner(mask, received):
     return pl.pallas_call(
-        functools.partial(owner_kernel, lines),
-        out_shape=jax.ShapeDtypeStruct((ids.shape[1], received.shape[1]), F32),
-        compiler_params=params(16),
+        owner_kernel,
+        out_shape=jax.ShapeDtypeStruct((mask.shape[0], received.shape[1]), F32),
+        compiler_params=params(4),
         name="to_owner",
-    )(ids, received)
+    )(mask, received)
 
 
 def body(conductivity, storage, recharge, block_ids, neighbours, concentration, sorption):
@@ -783,28 +841,30 @@
     devices = lax.axis_size(AXES)
     owned = concentration.shape[0]
     ids = block_ids.reshape(devices, owned)
-    first, second, conductivity, storage, recharge, ids, concentration, sorption = load(
-        conductivity, storage, recharge, ids, concentration, sorption
-    )
-    first, second = swap("gx", first, second)
-    inner, send, cols, rows = prepare(conductivity, storage, recharge, ids, concentration, sorption)
-    strip, west, east = pack_strip(inner, first, second)
-    first, second = swap("gy", strip, strip)
+    first, second = swap("gx", *pack_edges(conductivity, storage, recharge))
+    (
+        conductivity, storage, recharge, ids, concentration, sorption, own,
+        inner, ends, sides, edges, picks, slots,
+    ) = load(conductivity, storage, recharge, ids, concentration, sorption)
+    strip, west, east, first, second = pack_strip(own, first, second)
+    first, second = swap("gy", first, second)
+    send, mask = pack_send(ids, concentration, sorption, layers, rows_x)
+    faces = faces_of(conductivity, storage, west, east)
     base, image, gathered, send = flow(
-        conductivity, storage, recharge, west, east, strip, first, second, send, rows[:2]
+        conductivity, storage, recharge, west, east, strip, first, second, send, slots, faces
     )
     received = lax.all_to_all(
         send.reshape(devices, 1, ROWS * width), AXES, split_axis=0, concat_axis=0, tiled=True
     ).reshape(devices * ROWS, width)
-    c, s, flux, edge, end, scal = first_step(received, gathered, cols, rows, layers, rows_x)
-    edges = swap("gx", edge, edge)
-    ends = swap("gy", end, end)
+    c, s, flux, edge, end, scal = first_step(received, gathered, inner, ends, sides, picks, layers)
+    edge = swap("gx", edge, edge)
+    end = swap("gy", end, end)
     head = scal[0, 0] * base + scal[0, 1] * image
-    result = second_step(c, s, flux, cols, rows, edges, ends, rows_x)
+    result = second_step(c, s, flux, inner, ends, edges, edge, end)
     returned = lax.all_to_all(
         result.reshape(devices, 2, width), AXES, split_axis=0, concat_axis=0, tiled=True
     ).reshape(devices * 2, width)
-    return head, to_owner(ids, returned, layers * rows_x)
+    return head, to_owner(mask, returned)
 
 
 def solution(mesh):

time: 77.2 us -> 73.4 us (0.951)
  waiting for transfers between devices: 16.1 us -> 11 us
    ppermute x8, waiting for transfers between devices: 8.25 us -> 3.2 us  [swap(): return (lax.ppermute(first, axis, one), lax.ppermute(second, axis, other))]
    pallas_call x5 -> x7, Pallas kernels: 8.69 us -> 10.7 us  [the longest x1 2.51 us: load(): pl.pallas_call(kernel, in_specs=[HBM] * 6, out_specs=[VMEM] * 13, out_sha...]
    pallas_call x1, Pallas kernels: 7.35 us -> 5.8 us  [flow(): pl.pallas_call(flow_kernel, out_shape=[jax.ShapeDtypeStruct(conductivity....]
  transfers between devices with their start and end apart: 9 -> 9, of which waited for: 5 -> 3; matrix products, arithmetic and copies ran while one was open for 4% -> 4% of each run, Pallas kernels for 2% -> 6%
where the time goes in v4:
time: 73.4 us; the launch traced here: 73.2 us
  blocking collectives  23.3 us (32%)
  starting transfers between devices  18.5 us (25%)
  Pallas kernels  16.8 us (23%)
  waiting for transfers between devices  11 us (15%)
  other arithmetic  2.2 us (3%)
    all_to_all x1, blocking collectives, body(): lax.all_to_all(send.reshape(devices, 1, ROWS * width), AXES, split_axis=0...  23.3 us
    ppermute x8, starting transfers between devices, swap(): return (lax.ppermute(first, axis, one), lax.ppermute(second, axis, other))  11.5 us
    all_to_all x1, waiting for transfers between devices, body(): lax.all_to_all(result.reshape(devices, 2, width), AXES, split_axis=0, con...  7.8 us
    all_to_all x1, starting transfers between devices, body(): lax.all_to_all(result.reshape(devices, 2, width), AXES, split_axis=0, con...  7.03 us
    pallas_call x1, Pallas kernels, flow(): pl.pallas_call(flow_kernel, out_shape=[jax.ShapeDtypeStruct(conductivity....  5.8 us
    ppermute x8, waiting for transfers between devices, swap(): return (lax.ppermute(first, axis, one), lax.ppermute(second, axis, other))  3.2 us
    pallas_call x1, Pallas kernels, load(): pl.pallas_call(kernel, in_specs=[HBM] * 6, out_specs=[VMEM] * 13, out_sha...  2.51 us
    add x1, other arithmetic, body(): head = scal[0, 0] * base + scal[0, 1] * image  2.2 us
  transfers between devices with their start and end apart: 9, of which 3 were waited for; matrix products, arithmetic and copies ran while one was open for 4% of the time, Pallas kernels for 6%

profile of v4, /device:TPU:1, one launch (start us, length us, event | category | flops | bytes accessed | tf_op | source)
XLA Modules:
  0.0 73.2 jit_solution(13727567043205339040)
XLA Ops:
  0.6 1.1 %pack_edges.1 = (f32[16,8,128]{2,1,0:T(8,128)S(1)}, f32[16,8,128]{2,1,0:T(8,128)S(1)}) custom-call(f32[16,64,128]{2,1,0:T(8,128)} %k_hbm.3, f32[16,64,128]{2,1,0:T(8,128)} %s_hbm.3, f32[16,64,128]{2,1,0:T(8,128)} %r_hbm.3), custom_call_target="tpu_custom_call" | custom-call | tf_op jit(solution)/shard_map/pack_edges/pallas_call | solution.py:125
  1.7 1.5 %collective-permute-start = (f32[16,8,128]{2,1,0:T(8,128)S(1)}, f32[16,8,128]{2,1,0:T(8,128)S(1)}, u32[]{:S(2)}, u32[]{:S(2)}) collective-permute-start(f32[16,8,128]{2,1,0:T(8,128)S(1)} %get-tuple-element.42), channel_id=1, source_target_pairs={{0,16},{16,0},{32,48},{48,32},{64,80},{80,64},{96,112},{112,96},{1... | collective-permute-start | bytes 196616 | tf_op jit(solution)/shard_map/ppermute | solution.py:80
  3.2 1.3 %collective-permute-start.1 = (f32[16,8,128]{2,1,0:T(8,128)S(1)}, f32[16,8,128]{2,1,0:T(8,128)S(1)}, u32[]{:S(2)}, u32[]{:S(2)}) collective-permute-start(f32[16,8,128]{2,1,0:T(8,128)S(1)} %get-tuple-element.43), channel_id=1, source_target_pairs={{0,112},{16,32},{32,16},{48,64},{64,48},{80,96},{96,80},{112,0},{1... | collective-permute-start | bytes 196616 | tf_op jit(solution)/shard_map/ppermute | solution.py:80
  4.5 2.5 %load.1 = (f32[16,64,128]{2,1,0:T(8,128)S(1)}, f32[16,64,128]{2,1,0:T(8,128)S(1)}, f32[16,64,128]{2,1,0:T(8,128)S(1)}, s32[128,128]{1,0:T(8,128)S(1)}, f32[128,1...) custom-call(f32[16,64,128]{2,1,0:T(8,128)} %k_hbm.3, ...), custom_call_target="tpu_custom_call" | custom-call | tf_op jit(solution)/shard_map/load/pallas_call | solution.py:278
  7.0 0.0 collective-permute-done.first_ref
  7.0 0.2 collective-permute-done.1.second_ref
  7.2 0.3 pack_strip.1
  7.5 1.8 %collective-permute-start.2 = (f32[80,128]{1,0:T(8,128)S(1)}, f32[80,128]{1,0:T(8,128)S(1)}, u32[]{:S(2)}, u32[]{:S(2)}) collective-permute-start(f32[80,128]{1,0:T(8,128)S(1)} %get-tuple-element.47), channel_id=1, source_target_pairs={{0,1},{1,0},{2,3},{3,2},{4,5},{5,4},{6,7},{7,6},{8,9},{9,8},{10,11... | collective-permute-start | bytes 122888 | tf_op jit(solution)/shard_map/ppermute | solution.py:80
  9.3 4.7 %collective-permute-start.3 = (f32[80,128]{1,0:T(8,128)S(1)}, f32[80,128]{1,0:T(8,128)S(1)}, u32[]{:S(2)}, u32[]{:S(2)}) collective-permute-start(f32[80,128]{1,0:T(8,128)S(1)} %get-tuple-element.48), channel_id=1, source_target_pairs={{0,15},{1,2},{2,1},{3,4},{4,3},{5,6},{6,5},{7,8},{8,7},{9,10},{10,... | collective-permute-start | bytes 122888 | tf_op jit(solution)/shard_map/ppermute | solution.py:80
  14.0 0.6 pack_send.1
  14.6 1.4 %faces.1 = (f32[16,80,128]{2,1,0:T(8,128)S(1)}, f32[16,80,128]{2,1,0:T(8,128)S(1)}, f32[17,80,128]{2,1,0:T(8,128)S(1)}, f32[16,80,128]{2,1,0:T(8,128)S(1)}) custom-call(f32[16,64,128]{2,1,0:T(8,128)S(1)} %get-tuple-element.38.k_ref, f32[16,64,128]{2,1,0:T(8,128)S(1)} %get-tuple-element.39.s_ref, f32[16,8,128]{2,1,0:T(8,128)S(1)} %get-tuple-element.44.west_ref, ...), custom_call_target="tpu_custom_call" | custom-call | tf_op jit(solution)/shard_map/faces/pallas_call | solution.py:381
  16.0 0.0 collective-permute-done.2.first_ref
  16.0 0.0 collective-permute-done.3.second_ref
  16.0 5.8 %flow.1 = (f32[16,64,128]{2,1,0:T(8,128)S(1)}, f32[16,64,128]{2,1,0:T(8,128)S(1)}, f32[4096,128]{1,0:T(8,128)S(1)}, f32[1152,128]{1,0:T(8,128)S(1)}) custom-call(f32[16,64,128]{2,1,0:T(8,128)S(1)} %get-tuple-element.38.k_ref, f32[16,64,128]{2,1,0:T(8,128)S(1)} %get-tuple-element.39.s_ref, f32[16,64,128]{2,1,0:T(8,128)S(1)} %get-tuple-element.40.r_ref, ...), custom_call_target="tpu_custom_call" | custom-call | tf_op jit(solution)/shard_map/flow/pallas_call | solution.py:515
  21.8 23.3 %all_to_all.10 = f32[128,1,1152]{2,1,0:T(1,128)S(1)} all-to-all(f32[128,1,1152]{2,1,0:T(1,128)S(1)} %bitcast.8), channel_id=1, replica_groups=mesh['gx'=8,'gy'=16] {'gx','gy'}, dimensions={0} | all-to-all | bytes 1179648 | tf_op jit(solution)/shard_map/all_to_all | solution.py:856
  45.1 2.2 %first_step.1 = (f32[128,256]{1,0:T(8,128)S(1)}, f32[128,256]{1,0:T(8,128)S(1)}, f32[6,128,256]{2,1,0:T(8,128)S(1)}, f32[32,128]{1,0:T(8,128)S(1)}, f32[8,256]{1,0:T(8,128)S(1)}, /*index=5*/f32[8,128]{1,0:T(8,128)S(1)}) custom-call(f32[1152,128]{1,0:T(8,128)S(1)} %bitcast.7, f32[4096,128]{1,0:T(8,128)S(1)} %get-tuple-element.59.gath_ref, ...), custom_call_target="tpu_custom_call" | custom-call | tf_op jit(solution)/shard_map/first_step/pallas_call | solution.py:771
  47.3 0.7 collective-permute-start.7
  48.0 0.2 collective-permute-start.6
  48.2 1.2 %collective-permute-start.5 = (f32[32,128]{1,0:T(8,128)S(1)}, f32[32,128]{1,0:T(8,128)S(1)}, u32[]{:S(2)}, u32[]{:S(2)}) collective-permute-start(f32[32,128]{1,0:T(8,128)S(1)} %get-tuple-element.72), channel_id=1, source_target_pairs={{0,112},{16,32},{32,16},{48,64},{64,48},{80,96},{96,80},{112,0},{1... | collective-permute-start | bytes 49160 | tf_op jit(solution)/shard_map/ppermute | solution.py:80
  49.3 0.2 collective-permute-start.4
  49.5 0.7 fusion
  50.2 3.0 %collective-permute-done.7.end2_ref = f32[8,256]{1,0:T(8,128)S(1)} collective-permute-done((f32[8,256]{1,0:T(8,128)S(1)}, f32[8,256]{1,0:T(8,128)S(1)}, u32[]{:S(2)}, u32[]{:S(2)}) %collective-permute-start.7) | collective-permute-done | bytes 8224 | tf_op jit(solution)/shard_map/ppermute | solution.py:80
  53.2 0.0 collective-permute-done.6.end1_ref
  53.2 0.0 collective-permute-done.5.edge2_ref
  53.2 0.0 collective-permute-done.4.edge1_ref
  53.2 2.1 %second_step.1 = f32[256,128]{1,0:T(8,128)} custom-call(f32[128,256]{1,0:T(8,128)S(1)} %get-tuple-element.68.c_ref, f32[128,256]{1,0:T(8,128)S(1)} %get-tuple-element.69.s_ref, f32[6,128,256]{2,1,0:T(8,128)S(1)} %get-tuple-element.70.flux_ref, bf16[256,1024]{1,0:T(8,128)(2,1)S(1)} %get-tuple-element.60.inner_ref, ...), custom_call_target="tpu_custom_call" | custom-call | tf_op jit(solution)/shard_map/second_step/pallas_call | solution.py:813
  55.3 7.0 %all-to-all-start.1 = ((f32[128,2,128]{2,1,0:T(2,128)}), f32[128,2,128]{2,1,0:T(2,128)S(1)}, u32[]{:S(2)}, u32[]{:S(2)}) async-start(f32[128,2,128]{2,1,0:T(2,128)} %bitcast.5), calls=%async_computation.1 | async-start | bytes 262144 | tf_op jit(solution)/shard_map/all_to_all | solution.py:864
  62.3 2.2 %multiply_add_fusion = f32[16,64,128]{2,1,0:T(8,128)} fusion(f32[16,64,128]{2,1,0:T(8,128)S(1)} %get-tuple-element.66, f32[16,64,128]{2,1,0:T(8,128)S(1)} %get-tuple-element.65, f32[]{:T(128)} %bitcast.4, f32[]{:T(128)} %bitcast.3), kind=kLoop, calls=%fused_computation | loop fusion | flops 393216 | bytes 1572872 | tf_op jit(solution)/shard_map/add | solution.py:862
  64.5 7.8 %all-to-all-done.1 = f32[128,2,128]{2,1,0:T(2,128)S(1)} async-done(((f32[128,2,128]{2,1,0:T(2,128)}), f32[128,2,128]{2,1,0:T(2,128)S(1)}, u32[]{:S(2)}, u32[]{:S(2)}) %all-to-all-start.1) | async-done | bytes 131104 | tf_op jit(solution)/shard_map/all_to_all | solution.py:864
  72.3 0.8 %to_owner.1 = f32[128,128]{1,0:T(8,128)} custom-call(bf16[128,256]{1,0:T(8,128)(2,1)S(1)} %get-tuple-element.67.mask_ref, f32[256,128]{1,0:T(8,128)S(1)} %bitcast.9), custom_call_target="tpu_custom_call" | custom-call | tf_op jit(solution)/shard_map/to_owner/pallas_call | solution.py:831
Async XLA Ops:
  1.7 5.3 %collective-permute-start = (f32[16,8,128]{2,1,0:T(8,128)S(1)}, f32[16,8,128]{2,1,0:T(8,128)S(1)}, u32[]{:S(2)}, u32[]{:S(2)}) collective-permute-start(f32[16,8,128]{2,1,0:T(8,128)S(1)} %get-tuple-element.42), channel_id=1, source_target_pairs={{0,16},{16,0},{32,48},{48,32},{64,80},{80,64},{96,112},{112,96},{1... | collective-permute-start | bytes 196616 | tf_op jit(solution)/shard_map/ppermute | solution.py:80
  3.2 4.0 %collective-permute-start.1 = (f32[16,8,128]{2,1,0:T(8,128)S(1)}, f32[16,8,128]{2,1,0:T(8,128)S(1)}, u32[]{:S(2)}, u32[]{:S(2)}) collective-permute-start(f32[16,8,128]{2,1,0:T(8,128)S(1)} %get-tuple-element.43), channel_id=1, source_target_pairs={{0,112},{16,32},{32,16},{48,64},{64,48},{80,96},{96,80},{112,0},{1... | collective-permute-start | bytes 196616 | tf_op jit(solution)/shard_map/ppermute | solution.py:80
  7.5 8.5 %collective-permute-start.2 = (f32[80,128]{1,0:T(8,128)S(1)}, f32[80,128]{1,0:T(8,128)S(1)}, u32[]{:S(2)}, u32[]{:S(2)}) collective-permute-start(f32[80,128]{1,0:T(8,128)S(1)} %get-tuple-element.47), channel_id=1, source_target_pairs={{0,1},{1,0},{2,3},{3,2},{4,5},{5,4},{6,7},{7,6},{8,9},{9,8},{10,11... | collective-permute-start | bytes 122888 | tf_op jit(solution)/shard_map/ppermute | solution.py:80
  9.3 6.7 %collective-permute-start.3 = (f32[80,128]{1,0:T(8,128)S(1)}, f32[80,128]{1,0:T(8,128)S(1)}, u32[]{:S(2)}, u32[]{:S(2)}) collective-permute-start(f32[80,128]{1,0:T(8,128)S(1)} %get-tuple-element.48), channel_id=1, source_target_pairs={{0,15},{1,2},{2,1},{3,4},{4,3},{5,6},{6,5},{7,8},{8,7},{9,10},{10,... | collective-permute-start | bytes 122888 | tf_op jit(solution)/shard_map/ppermute | solution.py:80
  47.3 5.9 %collective-permute-start.7 = (f32[8,256]{1,0:T(8,128)S(1)}, f32[8,256]{1,0:T(8,128)S(1)}, u32[]{:S(2)}, u32[]{:S(2)}) collective-permute-start(f32[8,256]{1,0:T(8,128)S(1)} %get-tuple-element.73), channel_id=1, source_target_pairs={{0,15},{1,2},{2,1},{3,4},{4,3},{5,6},{6,5},{7,8},{8,7},{9,10},{10,... | collective-permute-start | bytes 24584 | tf_op jit(solution)/shard_map/ppermute | solution.py:80
  48.0 5.2 %collective-permute-start.6 = (f32[8,256]{1,0:T(8,128)S(1)}, f32[8,256]{1,0:T(8,128)S(1)}, u32[]{:S(2)}, u32[]{:S(2)}) collective-permute-start(f32[8,256]{1,0:T(8,128)S(1)} %get-tuple-element.73), channel_id=1, source_target_pairs={{0,1},{1,0},{2,3},{3,2},{4,5},{5,4},{6,7},{7,6},{8,9},{9,8},{10,11... | collective-permute-start | bytes 24584 | tf_op jit(solution)/shard_map/ppermute | solution.py:80
  48.2 5.0 %collective-permute-start.5 = (f32[32,128]{1,0:T(8,128)S(1)}, f32[32,128]{1,0:T(8,128)S(1)}, u32[]{:S(2)}, u32[]{:S(2)}) collective-permute-start(f32[32,128]{1,0:T(8,128)S(1)} %get-tuple-element.72), channel_id=1, source_target_pairs={{0,112},{16,32},{32,16},{48,64},{64,48},{80,96},{96,80},{112,0},{1... | collective-permute-start | bytes 49160 | tf_op jit(solution)/shard_map/ppermute | solution.py:80
  49.3 3.9 %collective-permute-start.4 = (f32[32,128]{1,0:T(8,128)S(1)}, f32[32,128]{1,0:T(8,128)S(1)}, u32[]{:S(2)}, u32[]{:S(2)}) collective-permute-start(f32[32,128]{1,0:T(8,128)S(1)} %get-tuple-element.72), channel_id=1, source_target_pairs={{0,16},{16,0},{32,48},{48,32},{64,80},{80,64},{96,112},{112,96},{1... | collective-permute-start | bytes 49160 | tf_op jit(solution)/shard_map/ppermute | solution.py:80
  55.3 17.0 %all-to-all-start.1 = ((f32[128,2,128]{2,1,0:T(2,128)}), f32[128,2,128]{2,1,0:T(2,128)S(1)}, u32[]{:S(2)}, u32[]{:S(2)}) async-start(f32[128,2,128]{2,1,0:T(2,128)} %bitcast.5), calls=%async_computation.1 | async-start | bytes 262144 | tf_op jit(solution)/shard_map/all_to_all | solution.py:864

commit v5 on v4

--- a/solution.py
+++ b/solution.py
@@ -76,8 +76,18 @@
 def swap(axis, first, second):
     count = lax.axis_size(axis)
     one = [(i, i ^ 1) for i in range(count)]
-    other = [(i, (i + 1 if i % 2 else i - 1) % count) for i in range(count)]
-    return lax.ppermute(first, axis, one), lax.ppermute(second, axis, other)
+    if axis == "gx":
+        other = [(i, (i + 1 if i % 2 else i - 1) % count) for i in range(count)]
+        return lax.ppermute(first, axis, one), lax.ppermute(second, axis, other)
+    pairs = []
+    for row in range(lax.axis_size("gx")):
+        for i in range(count):
+            partner = i + 1 if i % 2 else i - 1
+            if 0 <= partner < count:
+                pairs.append((row * count + i, row * count + partner))
+            else:
+                pairs.append((row * count + i, (row ^ 1) * count + i))
+    return lax.ppermute(first, axis, one), lax.ppermute(second, AXES, pairs)
 
 
 HBM = pl.BlockSpec(memory_space=pltpu.HBM)

time: 73.4 us -> 71 us (0.967)
  starting transfers between devices: 18.5 us -> 15.8 us
  blocking collectives: 23.3 us -> 25.3 us
  waiting for transfers between devices: 11 us -> 9.34 us
    ppermute x8 -> x4, starting transfers between devices: 11.5 us -> 4.11 us  [swap(): return (lax.ppermute(first, axis, one), lax.ppermute(second, axis, other))]
    ppermute x0 -> x4, starting transfers between devices: none -> 4.39 us  [swap(): return (lax.ppermute(first, axis, one), lax.ppermute(second, AXES, pairs))]
    ppermute x8 -> x4, waiting for transfers between devices: 3.2 us -> 1.02 us  [swap(): return (lax.ppermute(first, axis, one), lax.ppermute(second, axis, other))]
    all_to_all x1, blocking collectives: 23.3 us -> 25.3 us  [body(): lax.all_to_all(send.reshape(devices, 1, ROWS * width), AXES, split_axis=0...]
  transfers between devices with their start and end apart: 9 -> 9, of which waited for: 3 -> 4; matrix products, arithmetic and copies ran while one was open for 4% -> 4% of each run, Pallas kernels for 6% -> 6%
where the time goes in v5:
time: 71 us; the launch traced here: 70.8 us
  blocking collectives  25.3 us (36%)
  Pallas kernels  16.8 us (24%)
  starting transfers between devices  15.8 us (22%)
  waiting for transfers between devices  9.34 us (13%)
  other arithmetic  2.2 us (3%)
  between operations  0.71 us (1%)
    all_to_all x1, blocking collectives, body(): lax.all_to_all(send.reshape(devices, 1, ROWS * width), AXES, split_axis=0...  25.3 us
    all_to_all x1, waiting for transfers between devices, body(): lax.all_to_all(result.reshape(devices, 2, width), AXES, split_axis=0, con...  7.8 us
    all_to_all x1, starting transfers between devices, body(): lax.all_to_all(result.reshape(devices, 2, width), AXES, split_axis=0, con...  7.35 us
    pallas_call x1, Pallas kernels, flow(): pl.pallas_call(flow_kernel, out_shape=[jax.ShapeDtypeStruct(conductivity....  5.8 us
    ppermute x4, starting transfers between devices, swap(): return (lax.ppermute(first, axis, one), lax.ppermute(second, AXES, pairs))  4.39 us
    ppermute x4, starting transfers between devices, swap(): return (lax.ppermute(first, axis, one), lax.ppermute(second, axis, other))  4.11 us
    pallas_call x1, Pallas kernels, load(): pl.pallas_call(kernel, in_specs=[HBM] * 6, out_specs=[VMEM] * 13, out_sha...  2.51 us
    add x1, other arithmetic, body(): head = scal[0, 0] * base + scal[0, 1] * image  2.2 us
  transfers between devices with their start and end apart: 9, of which 4 were waited for; matrix products, arithmetic and copies ran while one was open for 4% of the time, Pallas kernels for 6%

profile of v5, /device:TPU:1, one launch (start us, length us, event | category | flops | bytes accessed | tf_op | source)
XLA Modules:
  0.0 70.8 jit_solution(10073782437441827114)
XLA Ops:
  0.6 1.1 %pack_edges.1 = (f32[16,8,128]{2,1,0:T(8,128)S(1)}, f32[16,8,128]{2,1,0:T(8,128)S(1)}) custom-call(f32[16,64,128]{2,1,0:T(8,128)} %k_hbm.3, f32[16,64,128]{2,1,0:T(8,128)} %s_hbm.3, f32[16,64,128]{2,1,0:T(8,128)} %r_hbm.3), custom_call_target="tpu_custom_call" | custom-call | tf_op jit(solution)/shard_map/pack_edges/pallas_call | solution.py:135
  1.7 1.5 %collective-permute-start = (f32[16,8,128]{2,1,0:T(8,128)S(1)}, f32[16,8,128]{2,1,0:T(8,128)S(1)}, u32[]{:S(2)}, u32[]{:S(2)}) collective-permute-start(f32[16,8,128]{2,1,0:T(8,128)S(1)} %get-tuple-element.42), channel_id=1, source_target_pairs={{0,16},{16,0},{32,48},{48,32},{64,80},{80,64},{96,112},{112,96},{1... | collective-permute-start | bytes 196616 | tf_op jit(solution)/shard_map/ppermute | solution.py:81
  3.2 1.3 %collective-permute-start.1 = (f32[16,8,128]{2,1,0:T(8,128)S(1)}, f32[16,8,128]{2,1,0:T(8,128)S(1)}, u32[]{:S(2)}, u32[]{:S(2)}) collective-permute-start(f32[16,8,128]{2,1,0:T(8,128)S(1)} %get-tuple-element.43), channel_id=1, source_target_pairs={{0,112},{16,32},{32,16},{48,64},{64,48},{80,96},{96,80},{112,0},{1... | collective-permute-start | bytes 196616 | tf_op jit(solution)/shard_map/ppermute | solution.py:81
  4.5 2.5 %load.1 = (f32[16,64,128]{2,1,0:T(8,128)S(1)}, f32[16,64,128]{2,1,0:T(8,128)S(1)}, f32[16,64,128]{2,1,0:T(8,128)S(1)}, s32[128,128]{1,0:T(8,128)S(1)}, f32[128,1...) custom-call(f32[16,64,128]{2,1,0:T(8,128)} %k_hbm.3, ...), custom_call_target="tpu_custom_call" | custom-call | tf_op jit(solution)/shard_map/load/pallas_call | solution.py:288
  7.0 0.0 collective-permute-done.first_ref
  7.0 0.2 collective-permute-done.1.second_ref
  7.2 0.3 pack_strip.1
  7.5 1.8 %collective-permute-start.2 = (f32[80,128]{1,0:T(8,128)S(1)}, f32[80,128]{1,0:T(8,128)S(1)}, u32[]{:S(2)}, u32[]{:S(2)}) collective-permute-start(f32[80,128]{1,0:T(8,128)S(1)} %get-tuple-element.47), channel_id=1, source_target_pairs={{0,1},{1,0},{2,3},{3,2},{4,5},{5,4},{6,7},{7,6},{8,9},{9,8},{10,11... | collective-permute-start | bytes 122888 | tf_op jit(solution)/shard_map/ppermute | solution.py:90
  9.3 1.7 %collective-permute-start.3 = (f32[80,128]{1,0:T(8,128)S(1)}, f32[80,128]{1,0:T(8,128)S(1)}, u32[]{:S(2)}, u32[]{:S(2)}) collective-permute-start(f32[80,128]{1,0:T(8,128)S(1)} %get-tuple-element.48), channel_id=1, source_target_pairs={{0,16},{1,2},{2,1},{3,4},{4,3},{5,6},{6,5},{7,8},{8,7},{9,10},{10,... | collective-permute-start | bytes 122888 | tf_op jit(solution)/shard_map/ppermute | solution.py:90
  11.0 0.6 pack_send.1
  11.6 1.4 %faces.1 = (f32[16,80,128]{2,1,0:T(8,128)S(1)}, f32[16,80,128]{2,1,0:T(8,128)S(1)}, f32[17,80,128]{2,1,0:T(8,128)S(1)}, f32[16,80,128]{2,1,0:T(8,128)S(1)}) custom-call(f32[16,64,128]{2,1,0:T(8,128)S(1)} %get-tuple-element.38.k_ref, f32[16,64,128]{2,1,0:T(8,128)S(1)} %get-tuple-element.39.s_ref, f32[16,8,128]{2,1,0:T(8,128)S(1)} %get-tuple-element.44.west_ref, ...), custom_call_target="tpu_custom_call" | custom-call | tf_op jit(solution)/shard_map/faces/pallas_call | solution.py:391
  13.0 0.0 collective-permute-done.2.first_ref
  13.0 0.0 collective-permute-done.3.second_ref
  13.0 5.8 %flow.1 = (f32[16,64,128]{2,1,0:T(8,128)S(1)}, f32[16,64,128]{2,1,0:T(8,128)S(1)}, f32[4096,128]{1,0:T(8,128)S(1)}, f32[1152,128]{1,0:T(8,128)S(1)}) custom-call(f32[16,64,128]{2,1,0:T(8,128)S(1)} %get-tuple-element.38.k_ref, f32[16,64,128]{2,1,0:T(8,128)S(1)} %get-tuple-element.39.s_ref, f32[16,64,128]{2,1,0:T(8,128)S(1)} %get-tuple-element.40.r_ref, ...), custom_call_target="tpu_custom_call" | custom-call | tf_op jit(solution)/shard_map/flow/pallas_call | solution.py:525
  18.8 25.3 %all_to_all.10 = f32[128,1,1152]{2,1,0:T(1,128)S(1)} all-to-all(f32[128,1,1152]{2,1,0:T(1,128)S(1)} %bitcast.8), channel_id=1, replica_groups=mesh['gx'=8,'gy'=16] {'gx','gy'}, dimensions={0} | all-to-all | bytes 1179648 | tf_op jit(solution)/shard_map/all_to_all | solution.py:866
  44.1 2.2 %first_step.1 = (f32[128,256]{1,0:T(8,128)S(1)}, f32[128,256]{1,0:T(8,128)S(1)}, f32[6,128,256]{2,1,0:T(8,128)S(1)}, f32[32,128]{1,0:T(8,128)S(1)}, f32[8,256]{1,0:T(8,128)S(1)}, /*index=5*/f32[8,128]{1,0:T(8,128)S(1)}) custom-call(f32[1152,128]{1,0:T(8,128)S(1)} %bitcast.7, f32[4096,128]{1,0:T(8,128)S(1)} %get-tuple-element.59.gath_ref, ...), custom_call_target="tpu_custom_call" | custom-call | tf_op jit(solution)/shard_map/first_step/pallas_call | solution.py:781
  46.3 0.9 %collective-permute-start.7 = (f32[8,256]{1,0:T(8,128)S(1)}, f32[8,256]{1,0:T(8,128)S(1)}, u32[]{:S(2)}, u32[]{:S(2)}) collective-permute-start(f32[8,256]{1,0:T(8,128)S(1)} %get-tuple-element.73), channel_id=1, source_target_pairs={{0,16},{1,2},{2,1},{3,4},{4,3},{5,6},{6,5},{7,8},{8,7},{9,10},{10,... | collective-permute-start | bytes 24584 | tf_op jit(solution)/shard_map/ppermute | solution.py:90
  47.2 0.0 collective-permute-start.6
  47.2 1.2 %collective-permute-start.5 = (f32[32,128]{1,0:T(8,128)S(1)}, f32[32,128]{1,0:T(8,128)S(1)}, u32[]{:S(2)}, u32[]{:S(2)}) collective-permute-start(f32[32,128]{1,0:T(8,128)S(1)} %get-tuple-element.72), channel_id=1, source_target_pairs={{0,112},{16,32},{32,16},{48,64},{64,48},{80,96},{96,80},{112,0},{1... | collective-permute-start | bytes 49160 | tf_op jit(solution)/shard_map/ppermute | solution.py:81
  48.3 0.2 collective-permute-start.4
  48.5 0.7 fusion
  49.2 0.0 collective-permute-done.7.end2_ref
  49.2 0.5 collective-permute-done.6.end1_ref
  49.7 0.8 %collective-permute-done.5.edge2_ref = f32[32,128]{1,0:T(8,128)S(1)} collective-permute-done((f32[32,128]{1,0:T(8,128)S(1)}, f32[32,128]{1,0:T(8,128)S(1)}, u32[]{:S(2)}, u32[]{:S(2)}) %collective-permute-start.5) | collective-permute-done | bytes 16416 | tf_op jit(solution)/shard_map/ppermute | solution.py:81
  50.5 0.0 collective-permute-done.4.edge1_ref
  50.5 2.1 %second_step.1 = f32[256,128]{1,0:T(8,128)} custom-call(f32[128,256]{1,0:T(8,128)S(1)} %get-tuple-element.68.c_ref, f32[128,256]{1,0:T(8,128)S(1)} %get-tuple-element.69.s_ref, f32[6,128,256]{2,1,0:T(8,128)S(1)} %get-tuple-element.70.flux_ref, bf16[256,1024]{1,0:T(8,128)(2,1)S(1)} %get-tuple-element.60.inner_ref, ...), custom_call_target="tpu_custom_call" | custom-call | tf_op jit(solution)/shard_map/second_step/pallas_call | solution.py:823
  52.6 7.4 %all-to-all-start.1 = ((f32[128,2,128]{2,1,0:T(2,128)}), f32[128,2,128]{2,1,0:T(2,128)S(1)}, u32[]{:S(2)}, u32[]{:S(2)}) async-start(f32[128,2,128]{2,1,0:T(2,128)} %bitcast.5), calls=%async_computation.1 | async-start | bytes 262144 | tf_op jit(solution)/shard_map/all_to_all | solution.py:874
  60.0 2.2 %multiply_add_fusion = f32[16,64,128]{2,1,0:T(8,128)} fusion(f32[16,64,128]{2,1,0:T(8,128)S(1)} %get-tuple-element.66, f32[16,64,128]{2,1,0:T(8,128)S(1)} %get-tuple-element.65, f32[]{:T(128)} %bitcast.4, f32[]{:T(128)} %bitcast.3), kind=kLoop, calls=%fused_computation | loop fusion | flops 393216 | bytes 1572872 | tf_op jit(solution)/shard_map/add | solution.py:872
  62.2 7.8 %all-to-all-done.1 = f32[128,2,128]{2,1,0:T(2,128)S(1)} async-done(((f32[128,2,128]{2,1,0:T(2,128)}), f32[128,2,128]{2,1,0:T(2,128)S(1)}, u32[]{:S(2)}, u32[]{:S(2)}) %all-to-all-start.1) | async-done | bytes 131104 | tf_op jit(solution)/shard_map/all_to_all | solution.py:874
  70.0 0.8 %to_owner.1 = f32[128,128]{1,0:T(8,128)} custom-call(bf16[128,256]{1,0:T(8,128)(2,1)S(1)} %get-tuple-element.67.mask_ref, f32[256,128]{1,0:T(8,128)S(1)} %bitcast.9), custom_call_target="tpu_custom_call" | custom-call | tf_op jit(solution)/shard_map/to_owner/pallas_call | solution.py:841
Async XLA Ops:
  1.7 5.3 %collective-permute-start = (f32[16,8,128]{2,1,0:T(8,128)S(1)}, f32[16,8,128]{2,1,0:T(8,128)S(1)}, u32[]{:S(2)}, u32[]{:S(2)}) collective-permute-start(f32[16,8,128]{2,1,0:T(8,128)S(1)} %get-tuple-element.42), channel_id=1, source_target_pairs={{0,16},{16,0},{32,48},{48,32},{64,80},{80,64},{96,112},{112,96},{1... | collective-permute-start | bytes 196616 | tf_op jit(solution)/shard_map/ppermute | solution.py:81
  3.2 4.0 %collective-permute-start.1 = (f32[16,8,128]{2,1,0:T(8,128)S(1)}, f32[16,8,128]{2,1,0:T(8,128)S(1)}, u32[]{:S(2)}, u32[]{:S(2)}) collective-permute-start(f32[16,8,128]{2,1,0:T(8,128)S(1)} %get-tuple-element.43), channel_id=1, source_target_pairs={{0,112},{16,32},{32,16},{48,64},{64,48},{80,96},{96,80},{112,0},{1... | collective-permute-start | bytes 196616 | tf_op jit(solution)/shard_map/ppermute | solution.py:81
  7.5 5.5 %collective-permute-start.2 = (f32[80,128]{1,0:T(8,128)S(1)}, f32[80,128]{1,0:T(8,128)S(1)}, u32[]{:S(2)}, u32[]{:S(2)}) collective-permute-start(f32[80,128]{1,0:T(8,128)S(1)} %get-tuple-element.47), channel_id=1, source_target_pairs={{0,1},{1,0},{2,3},{3,2},{4,5},{5,4},{6,7},{7,6},{8,9},{9,8},{10,11... | collective-permute-start | bytes 122888 | tf_op jit(solution)/shard_map/ppermute | solution.py:90
  9.3 3.7 %collective-permute-start.3 = (f32[80,128]{1,0:T(8,128)S(1)}, f32[80,128]{1,0:T(8,128)S(1)}, u32[]{:S(2)}, u32[]{:S(2)}) collective-permute-start(f32[80,128]{1,0:T(8,128)S(1)} %get-tuple-element.48), channel_id=1, source_target_pairs={{0,16},{1,2},{2,1},{3,4},{4,3},{5,6},{6,5},{7,8},{8,7},{9,10},{10,... | collective-permute-start | bytes 122888 | tf_op jit(solution)/shard_map/ppermute | solution.py:90
  46.3 2.9 %collective-permute-start.7 = (f32[8,256]{1,0:T(8,128)S(1)}, f32[8,256]{1,0:T(8,128)S(1)}, u32[]{:S(2)}, u32[]{:S(2)}) collective-permute-start(f32[8,256]{1,0:T(8,128)S(1)} %get-tuple-element.73), channel_id=1, source_target_pairs={{0,16},{1,2},{2,1},{3,4},{4,3},{5,6},{6,5},{7,8},{8,7},{9,10},{10,... | collective-permute-start | bytes 24584 | tf_op jit(solution)/shard_map/ppermute | solution.py:90
  47.2 2.5 %collective-permute-start.6 = (f32[8,256]{1,0:T(8,128)S(1)}, f32[8,256]{1,0:T(8,128)S(1)}, u32[]{:S(2)}, u32[]{:S(2)}) collective-permute-start(f32[8,256]{1,0:T(8,128)S(1)} %get-tuple-element.73), channel_id=1, source_target_pairs={{0,1},{1,0},{2,3},{3,2},{4,5},{5,4},{6,7},{7,6},{8,9},{9,8},{10,11... | collective-permute-start | bytes 24584 | tf_op jit(solution)/shard_map/ppermute | solution.py:90
  47.2 3.3 %collective-permute-start.5 = (f32[32,128]{1,0:T(8,128)S(1)}, f32[32,128]{1,0:T(8,128)S(1)}, u32[]{:S(2)}, u32[]{:S(2)}) collective-permute-start(f32[32,128]{1,0:T(8,128)S(1)} %get-tuple-element.72), channel_id=1, source_target_pairs={{0,112},{16,32},{32,16},{48,64},{64,48},{80,96},{96,80},{112,0},{1... | collective-permute-start | bytes 49160 | tf_op jit(solution)/shard_map/ppermute | solution.py:81
  48.3 2.2 %collective-permute-start.4 = (f32[32,128]{1,0:T(8,128)S(1)}, f32[32,128]{1,0:T(8,128)S(1)}, u32[]{:S(2)}, u32[]{:S(2)}) collective-permute-start(f32[32,128]{1,0:T(8,128)S(1)} %get-tuple-element.72), channel_id=1, source_target_pairs={{0,16},{16,0},{32,48},{48,32},{64,80},{80,64},{96,112},{112,96},{1... | collective-permute-start | bytes 49160 | tf_op jit(solution)/shard_map/ppermute | solution.py:81
  52.6 17.4 %all-to-all-start.1 = ((f32[128,2,128]{2,1,0:T(2,128)}), f32[128,2,128]{2,1,0:T(2,128)S(1)}, u32[]{:S(2)}, u32[]{:S(2)}) async-start(f32[128,2,128]{2,1,0:T(2,128)} %bitcast.5), calls=%async_computation.1 | async-start | bytes 262144 | tf_op jit(solution)/shard_map/all_to_all | solution.py:874

commit v6 on v5

--- a/solution.py
+++ b/solution.py
@@ -382,7 +382,7 @@
         fb[z + 1] = face_a
         return carry
 
-    lax.fori_loop(0, layers, step, 0, unroll=2)
+    lax.fori_loop(0, layers, step, 0, unroll=8)
 
 
 def faces_of(conductivity, storage, west, east):
@@ -700,7 +700,7 @@
 
 def first_kernel(
     recv_ref, gath_ref, inner_ref, ends_ref, sides_ref, pick_ref,
-    c_out, s_out, flux_out, edge_out, end_out, scal_out, scratch,
+    c_out, s_out, flux_out, edge_out, end_out, on_d_out, on_w_out, scratch,
 ):
     devices = recv_ref.shape[0] // ROWS
     slots = 2 * devices
@@ -726,7 +726,8 @@
     alpha_next = gamma_next / bend_next
     on_d = alpha + alpha_next * (1.0 + beta)
     on_w = -alpha * alpha_next
-    scal_out[...] = jnp.where(iota((8, width), 1) == 0, on_d, on_w)
+    on_d_out[...] = jnp.broadcast_to(on_d, (1, width))
+    on_w_out[...] = jnp.broadcast_to(on_w, (1, width))
 
     c = to_cells(pair(0), scratch.at[0])
     s = to_cells(pair(2), scratch.at[1])
@@ -786,7 +787,8 @@
             jax.ShapeDtypeStruct((6, width, slots), F32),
             jax.ShapeDtypeStruct((2 * layers, width), F32),
             jax.ShapeDtypeStruct((8, slots), F32),
-            jax.ShapeDtypeStruct((8, width), F32),
+            jax.ShapeDtypeStruct((1, width), F32),
+            jax.ShapeDtypeStruct((1, width), F32),
         ],
         scratch_shapes=[pltpu.VMEM((10, 2, width, slots // 2), F32)],
         compiler_params=params(16),
@@ -866,10 +868,10 @@
     received = lax.all_to_all(
         send.reshape(devices, 1, ROWS * width), AXES, split_axis=0, concat_axis=0, tiled=True
     ).reshape(devices * ROWS, width)
-    c, s, flux, edge, end, scal = first_step(received, gathered, inner, ends, sides, picks, layers)
+    c, s, flux, edge, end, on_base, on_image = first_step(received, gathered, inner, ends, sides, picks, layers)
     edge = swap("gx", edge, edge)
     end = swap("gy", end, end)
-    head = scal[0, 0] * base + scal[0, 1] * image
+    head = on_base[None] * base + on_image[None] * image
     result = second_step(c, s, flux, inner, ends, edges, edge, end)
     returned = lax.all_to_all(
         result.reshape(devices, 2, width), AXES, split_axis=0, concat_axis=0, tiled=True

time: 71 us -> 71.6 us (level)
  waiting for transfers between devices: 9.34 us -> 11.5 us
  other arithmetic: 2.2 us -> 0.87 us
    ppermute x4, waiting for transfers between devices: 0.52 us -> 2.21 us  [swap(): return (lax.ppermute(first, axis, one), lax.ppermute(second, AXES, pairs))]
    all_to_all x1, waiting for transfers between devices: 7.8 us -> 9.14 us  [body(): lax.all_to_all(result.reshape(devices, 2, width), AXES, split_axis=0, con...]
    add x1, other arithmetic: 2.2 us -> 0.87 us  [body(): head = on_base[None] * base + on_image[None] * image]
    ppermute x4, waiting for transfers between devices: 1.02 us -> 0.19 us  [swap(): return (lax.ppermute(first, axis, one), lax.ppermute(second, axis, other))]
  transfers between devices with their start and end apart: 9 -> 9, of which waited for: 4 -> 4; matrix products, arithmetic and copies ran while one was open for 4% -> 1% of each run, Pallas kernels for 6% -> 6%
where the time goes in v6:
time: 71.6 us; the launch traced here: 71.4 us
  blocking collectives  25.7 us (36%)
  Pallas kernels  16.3 us (23%)
  starting transfers between devices  16.3 us (23%)
  waiting for transfers between devices  11.5 us (16%)
  other arithmetic  0.87 us (1%)
  between operations  0.72 us (1%)
    all_to_all x1, blocking collectives, body(): lax.all_to_all(send.reshape(devices, 1, ROWS * width), AXES, split_axis=0...  25.7 us
    all_to_all x1, waiting for transfers between devices, body(): lax.all_to_all(result.reshape(devices, 2, width), AXES, split_axis=0, con...  9.14 us
    all_to_all x1, starting transfers between devices, body(): lax.all_to_all(result.reshape(devices, 2, width), AXES, split_axis=0, con...  7.77 us
    pallas_call x1, Pallas kernels, flow(): pl.pallas_call(flow_kernel, out_shape=[jax.ShapeDtypeStruct(conductivity....  5.78 us
    ppermute x4, starting transfers between devices, swap(): return (lax.ppermute(first, axis, one), lax.ppermute(second, AXES, pairs))  4.3 us
    ppermute x4, starting transfers between devices, swap(): return (lax.ppermute(first, axis, one), lax.ppermute(second, axis, other))  4.19 us
    pallas_call x1, Pallas kernels, load(): pl.pallas_call(kernel, in_specs=[HBM] * 6, out_specs=[VMEM] * 13, out_sha...  2.51 us
    ppermute x4, waiting for transfers between devices, swap(): return (lax.ppermute(first, axis, one), lax.ppermute(second, AXES, pairs))  2.21 us
  transfers between devices with their start and end apart: 9, of which 4 were waited for; matrix products, arithmetic and copies ran while one was open for 1% of the time, Pallas kernels for 6%

profile of v6, /device:TPU:1, one launch (start us, length us, event | category | flops | bytes accessed | tf_op | source)
XLA Modules:
  0.0 71.4 jit_solution(3065710695815439865)
XLA Ops:
  0.6 1.1 %pack_edges.1 = (f32[16,8,128]{2,1,0:T(8,128)S(1)}, f32[16,8,128]{2,1,0:T(8,128)S(1)}) custom-call(f32[16,64,128]{2,1,0:T(8,128)} %k_hbm.3, f32[16,64,128]{2,1,0:T(8,128)} %s_hbm.3, f32[16,64,128]{2,1,0:T(8,128)} %r_hbm.3), custom_call_target="tpu_custom_call" | custom-call | tf_op jit(solution)/shard_map/pack_edges/pallas_call | solution.py:135
  1.7 1.5 %collective-permute-start = (f32[16,8,128]{2,1,0:T(8,128)S(1)}, f32[16,8,128]{2,1,0:T(8,128)S(1)}, u32[]{:S(2)}, u32[]{:S(2)}) collective-permute-start(f32[16,8,128]{2,1,0:T(8,128)S(1)} %get-tuple-element.43), channel_id=1, source_target_pairs={{0,16},{16,0},{32,48},{48,32},{64,80},{80,64},{96,112},{112,96},{1... | collective-permute-start | bytes 196616 | tf_op jit(solution)/shard_map/ppermute | solution.py:81
  3.2 1.3 %collective-permute-start.1 = (f32[16,8,128]{2,1,0:T(8,128)S(1)}, f32[16,8,128]{2,1,0:T(8,128)S(1)}, u32[]{:S(2)}, u32[]{:S(2)}) collective-permute-start(f32[16,8,128]{2,1,0:T(8,128)S(1)} %get-tuple-element.44), channel_id=1, source_target_pairs={{0,112},{16,32},{32,16},{48,64},{64,48},{80,96},{96,80},{112,0},{1... | collective-permute-start | bytes 196616 | tf_op jit(solution)/shard_map/ppermute | solution.py:81
  4.5 2.5 %load.1 = (f32[16,64,128]{2,1,0:T(8,128)S(1)}, f32[16,64,128]{2,1,0:T(8,128)S(1)}, f32[16,64,128]{2,1,0:T(8,128)S(1)}, s32[128,128]{1,0:T(8,128)S(1)}, f32[128,1...) custom-call(f32[16,64,128]{2,1,0:T(8,128)} %k_hbm.3, ...), custom_call_target="tpu_custom_call" | custom-call | tf_op jit(solution)/shard_map/load/pallas_call | solution.py:288
  7.0 0.0 collective-permute-done.first_ref
  7.0 0.2 collective-permute-done.1.second_ref
  7.2 0.3 pack_strip.1
  7.5 1.8 %collective-permute-start.2 = (f32[80,128]{1,0:T(8,128)S(1)}, f32[80,128]{1,0:T(8,128)S(1)}, u32[]{:S(2)}, u32[]{:S(2)}) collective-permute-start(f32[80,128]{1,0:T(8,128)S(1)} %get-tuple-element.48), channel_id=1, source_target_pairs={{0,1},{1,0},{2,3},{3,2},{4,5},{5,4},{6,7},{7,6},{8,9},{9,8},{10,11... | collective-permute-start | bytes 122888 | tf_op jit(solution)/shard_map/ppermute | solution.py:90
  9.3 1.7 %collective-permute-start.3 = (f32[80,128]{1,0:T(8,128)S(1)}, f32[80,128]{1,0:T(8,128)S(1)}, u32[]{:S(2)}, u32[]{:S(2)}) collective-permute-start(f32[80,128]{1,0:T(8,128)S(1)} %get-tuple-element.49), channel_id=1, source_target_pairs={{0,16},{1,2},{2,1},{3,4},{4,3},{5,6},{6,5},{7,8},{8,7},{9,10},{10,... | collective-permute-start | bytes 122888 | tf_op jit(solution)/shard_map/ppermute | solution.py:90
  11.0 0.6 pack_send.1
  11.6 1.0 %faces.1 = (f32[16,80,128]{2,1,0:T(8,128)S(1)}, f32[16,80,128]{2,1,0:T(8,128)S(1)}, f32[17,80,128]{2,1,0:T(8,128)S(1)}, f32[16,80,128]{2,1,0:T(8,128)S(1)}) custom-call(f32[16,64,128]{2,1,0:T(8,128)S(1)} %get-tuple-element.39.k_ref, f32[16,64,128]{2,1,0:T(8,128)S(1)} %get-tuple-element.40.s_ref, f32[16,8,128]{2,1,0:T(8,128)S(1)} %get-tuple-element.45.west_ref, ...), custom_call_target="tpu_custom_call" | custom-call | tf_op jit(solution)/shard_map/faces/pallas_call | solution.py:391
  12.6 0.0 collective-permute-done.2.first_ref
  12.6 0.0 collective-permute-done.3.second_ref
  12.6 5.8 %flow.1 = (f32[16,64,128]{2,1,0:T(8,128)S(1)}, f32[16,64,128]{2,1,0:T(8,128)S(1)}, f32[4096,128]{1,0:T(8,128)S(1)}, f32[1152,128]{1,0:T(8,128)S(1)}) custom-call(f32[16,64,128]{2,1,0:T(8,128)S(1)} %get-tuple-element.39.k_ref, f32[16,64,128]{2,1,0:T(8,128)S(1)} %get-tuple-element.40.s_ref, f32[16,64,128]{2,1,0:T(8,128)S(1)} %get-tuple-element.41.r_ref, ...), custom_call_target="tpu_custom_call" | custom-call | tf_op jit(solution)/shard_map/flow/pallas_call | solution.py:525
  18.4 25.7 %all_to_all.10 = f32[128,1,1152]{2,1,0:T(1,128)S(1)} all-to-all(f32[128,1,1152]{2,1,0:T(1,128)S(1)} %bitcast.8), channel_id=1, replica_groups=mesh['gx'=8,'gy'=16] {'gx','gy'}, dimensions={0} | all-to-all | bytes 1179648 | tf_op jit(solution)/shard_map/all_to_all | solution.py:868
  44.1 2.2 %first_step.1 = (f32[128,256]{1,0:T(8,128)S(1)}, f32[128,256]{1,0:T(8,128)S(1)}, f32[6,128,256]{2,1,0:T(8,128)S(1)}, f32[32,128]{1,0:T(8,128)S(1)}, f32[8,256]{1...) custom-call(f32[1152,128]{1,0:T(8,128)S(1)} %bitcast.7, f32[4096,128]{1,0:T(8,128)S(1)} %get-tuple-element.60.gath_ref, ...), custom_call_target="tpu_custom_call" | custom-call | tf_op jit(solution)/shard_map/first_step/pallas_call | solution.py:782
  46.3 1.1 %collective-permute-start.5 = (f32[32,128]{1,0:T(8,128)S(1)}, f32[32,128]{1,0:T(8,128)S(1)}, u32[]{:S(2)}, u32[]{:S(2)}) collective-permute-start(f32[32,128]{1,0:T(8,128)S(1)} %get-tuple-element.74), channel_id=1, source_target_pairs={{0,112},{16,32},{32,16},{48,64},{64,48},{80,96},{96,80},{112,0},{1... | collective-permute-start | bytes 49160 | tf_op jit(solution)/shard_map/ppermute | solution.py:81
  47.4 0.3 collective-permute-start.4
  47.7 0.2 collective-permute-start.7
  47.9 0.6 collective-permute-start.6
  48.5 0.4 collective-permute-done.7.end2_ref
  48.9 1.8 %collective-permute-done.6.end1_ref = f32[8,256]{1,0:T(8,128)S(1)} collective-permute-done((f32[8,256]{1,0:T(8,128)S(1)}, f32[8,256]{1,0:T(8,128)S(1)}, u32[]{:S(2)}, u32[]{:S(2)}) %collective-permute-start.6) | collective-permute-done | bytes 8224 | tf_op jit(solution)/shard_map/ppermute | solution.py:90
  50.7 0.0 collective-permute-done.5.edge2_ref
  50.7 0.0 collective-permute-done.4.edge1_ref
  50.7 2.1 %second_step.1 = f32[256,128]{1,0:T(8,128)} custom-call(f32[128,256]{1,0:T(8,128)S(1)} %get-tuple-element.70.c_ref, f32[128,256]{1,0:T(8,128)S(1)} %get-tuple-element.71.s_ref, f32[6,128,256]{2,1,0:T(8,128)S(1)} %get-tuple-element.72.flux_ref, bf16[256,1024]{1,0:T(8,128)(2,1)S(1)} %get-tuple-element.61.inner_ref, ...), custom_call_target="tpu_custom_call" | custom-call | tf_op jit(solution)/shard_map/second_step/pallas_call | solution.py:825
  52.8 7.8 %all-to-all-start.1 = ((f32[128,2,128]{2,1,0:T(2,128)}), f32[128,2,128]{2,1,0:T(2,128)S(1)}, u32[]{:S(2)}, u32[]{:S(2)}) async-start(f32[128,2,128]{2,1,0:T(2,128)} %bitcast.5), calls=%async_computation.1 | async-start | bytes 262144 | tf_op jit(solution)/shard_map/all_to_all | solution.py:876
  60.6 0.9 %multiply_add_fusion = f32[16,64,128]{2,1,0:T(8,128)} fusion(f32[16,64,128]{2,1,0:T(8,128)S(1)} %get-tuple-element.68, f32[16,64,128]{2,1,0:T(8,128)S(1)} %get-tuple-element.66, f32[128]{0:T(128)S(1)} %bitcast.11, f32[128]{0:T(128)S(1)} %bitcast.10), kind=kLoop, calls=%fused_computation | loop fusion | flops 393216 | bytes 1573888 | tf_op jit(solution)/shard_map/add | solution.py:874
  61.4 9.1 %all-to-all-done.1 = f32[128,2,128]{2,1,0:T(2,128)S(1)} async-done(((f32[128,2,128]{2,1,0:T(2,128)}), f32[128,2,128]{2,1,0:T(2,128)S(1)}, u32[]{:S(2)}, u32[]{:S(2)}) %all-to-all-start.1) | async-done | bytes 131104 | tf_op jit(solution)/shard_map/all_to_all | solution.py:876
  70.6 0.8 %to_owner.1 = f32[128,128]{1,0:T(8,128)} custom-call(bf16[128,256]{1,0:T(8,128)(2,1)S(1)} %get-tuple-element.69.mask_ref, f32[256,128]{1,0:T(8,128)S(1)} %bitcast.9), custom_call_target="tpu_custom_call" | custom-call | tf_op jit(solution)/shard_map/to_owner/pallas_call | solution.py:843
Async XLA Ops:
  1.7 5.3 %collective-permute-start = (f32[16,8,128]{2,1,0:T(8,128)S(1)}, f32[16,8,128]{2,1,0:T(8,128)S(1)}, u32[]{:S(2)}, u32[]{:S(2)}) collective-permute-start(f32[16,8,128]{2,1,0:T(8,128)S(1)} %get-tuple-element.43), channel_id=1, source_target_pairs={{0,16},{16,0},{32,48},{48,32},{64,80},{80,64},{96,112},{112,96},{1... | collective-permute-start | bytes 196616 | tf_op jit(solution)/shard_map/ppermute | solution.py:81
  3.2 4.0 %collective-permute-start.1 = (f32[16,8,128]{2,1,0:T(8,128)S(1)}, f32[16,8,128]{2,1,0:T(8,128)S(1)}, u32[]{:S(2)}, u32[]{:S(2)}) collective-permute-start(f32[16,8,128]{2,1,0:T(8,128)S(1)} %get-tuple-element.44), channel_id=1, source_target_pairs={{0,112},{16,32},{32,16},{48,64},{64,48},{80,96},{96,80},{112,0},{1... | collective-permute-start | bytes 196616 | tf_op jit(solution)/shard_map/ppermute | solution.py:81
  7.5 5.1 %collective-permute-start.2 = (f32[80,128]{1,0:T(8,128)S(1)}, f32[80,128]{1,0:T(8,128)S(1)}, u32[]{:S(2)}, u32[]{:S(2)}) collective-permute-start(f32[80,128]{1,0:T(8,128)S(1)} %get-tuple-element.48), channel_id=1, source_target_pairs={{0,1},{1,0},{2,3},{3,2},{4,5},{5,4},{6,7},{7,6},{8,9},{9,8},{10,11... | collective-permute-start | bytes 122888 | tf_op jit(solution)/shard_map/ppermute | solution.py:90
  9.3 3.3 %collective-permute-start.3 = (f32[80,128]{1,0:T(8,128)S(1)}, f32[80,128]{1,0:T(8,128)S(1)}, u32[]{:S(2)}, u32[]{:S(2)}) collective-permute-start(f32[80,128]{1,0:T(8,128)S(1)} %get-tuple-element.49), channel_id=1, source_target_pairs={{0,16},{1,2},{2,1},{3,4},{4,3},{5,6},{6,5},{7,8},{8,7},{9,10},{10,... | collective-permute-start | bytes 122888 | tf_op jit(solution)/shard_map/ppermute | solution.py:90
  46.3 4.4 %collective-permute-start.5 = (f32[32,128]{1,0:T(8,128)S(1)}, f32[32,128]{1,0:T(8,128)S(1)}, u32[]{:S(2)}, u32[]{:S(2)}) collective-permute-start(f32[32,128]{1,0:T(8,128)S(1)} %get-tuple-element.74), channel_id=1, source_target_pairs={{0,112},{16,32},{32,16},{48,64},{64,48},{80,96},{96,80},{112,0},{1... | collective-permute-start | bytes 49160 | tf_op jit(solution)/shard_map/ppermute | solution.py:81
  47.4 3.3 %collective-permute-start.4 = (f32[32,128]{1,0:T(8,128)S(1)}, f32[32,128]{1,0:T(8,128)S(1)}, u32[]{:S(2)}, u32[]{:S(2)}) collective-permute-start(f32[32,128]{1,0:T(8,128)S(1)} %get-tuple-element.74), channel_id=1, source_target_pairs={{0,16},{16,0},{32,48},{48,32},{64,80},{80,64},{96,112},{112,96},{1... | collective-permute-start | bytes 49160 | tf_op jit(solution)/shard_map/ppermute | solution.py:81
  47.7 1.2 %collective-permute-start.7 = (f32[8,256]{1,0:T(8,128)S(1)}, f32[8,256]{1,0:T(8,128)S(1)}, u32[]{:S(2)}, u32[]{:S(2)}) collective-permute-start(f32[8,256]{1,0:T(8,128)S(1)} %get-tuple-element.75), channel_id=1, source_target_pairs={{0,16},{1,2},{2,1},{3,4},{4,3},{5,6},{6,5},{7,8},{8,7},{9,10},{10,... | collective-permute-start | bytes 24584 | tf_op jit(solution)/shard_map/ppermute | solution.py:90
  47.9 2.8 %collective-permute-start.6 = (f32[8,256]{1,0:T(8,128)S(1)}, f32[8,256]{1,0:T(8,128)S(1)}, u32[]{:S(2)}, u32[]{:S(2)}) collective-permute-start(f32[8,256]{1,0:T(8,128)S(1)} %get-tuple-element.75), channel_id=1, source_target_pairs={{0,1},{1,0},{2,3},{3,2},{4,5},{5,4},{6,7},{7,6},{8,9},{9,8},{10,11... | collective-permute-start | bytes 24584 | tf_op jit(solution)/shard_map/ppermute | solution.py:90
  52.8 17.8 %all-to-all-start.1 = ((f32[128,2,128]{2,1,0:T(2,128)}), f32[128,2,128]{2,1,0:T(2,128)S(1)}, u32[]{:S(2)}, u32[]{:S(2)}) async-start(f32[128,2,128]{2,1,0:T(2,128)} %bitcast.5), calls=%async_computation.1 | async-start | bytes 262144 | tf_op jit(solution)/shard_map/all_to_all | solution.py:876

commit v7 on v5

--- a/solution.py
+++ b/solution.py
@@ -382,7 +382,7 @@
         fb[z + 1] = face_a
         return carry
 
-    lax.fori_loop(0, layers, step, 0, unroll=2)
+    lax.fori_loop(0, layers, step, 0, unroll=8)
 
 
 def faces_of(conductivity, storage, west, east):

time: 71 us -> 71 us (level)
  no operation moved by 1% of the time
where the time goes in v7:
time: 71 us; the launch traced here: 70.8 us
  blocking collectives  25.7 us (36%)
  Pallas kernels  16.4 us (23%)
  starting transfers between devices  15.8 us (22%)
  waiting for transfers between devices  9.34 us (13%)
  other arithmetic  2.2 us (3%)
  between operations  0.72 us (1%)
    all_to_all x1, blocking collectives, body(): lax.all_to_all(send.reshape(devices, 1, ROWS * width), AXES, split_axis=0...  25.7 us
    all_to_all x1, waiting for transfers between devices, body(): lax.all_to_all(result.reshape(devices, 2, width), AXES, split_axis=0, con...  7.8 us
    all_to_all x1, starting transfers between devices, body(): lax.all_to_all(result.reshape(devices, 2, width), AXES, split_axis=0, con...  7.35 us
    pallas_call x1, Pallas kernels, flow(): pl.pallas_call(flow_kernel, out_shape=[jax.ShapeDtypeStruct(conductivity....  5.8 us
    ppermute x4, starting transfers between devices, swap(): return (lax.ppermute(first, axis, one), lax.ppermute(second, AXES, pairs))  4.39 us
    ppermute x4, starting transfers between devices, swap(): return (lax.ppermute(first, axis, one), lax.ppermute(second, axis, other))  4.11 us
    pallas_call x1, Pallas kernels, load(): pl.pallas_call(kernel, in_specs=[HBM] * 6, out_specs=[VMEM] * 13, out_sha...  2.51 us
    add x1, other arithmetic, body(): head = scal[0, 0] * base + scal[0, 1] * image  2.2 us
  transfers between devices with their start and end apart: 9, of which 4 were waited for; matrix products, arithmetic and copies ran while one was open for 4% of the time, Pallas kernels for 6%

profile of v7, /device:TPU:1, one launch (start us, length us, event | category | flops | bytes accessed | tf_op | source)
XLA Modules:
  0.0 70.8 jit_solution(9283960615535821008)
XLA Ops:
  0.6 1.1 %pack_edges.1 = (f32[16,8,128]{2,1,0:T(8,128)S(1)}, f32[16,8,128]{2,1,0:T(8,128)S(1)}) custom-call(f32[16,64,128]{2,1,0:T(8,128)} %k_hbm.3, f32[16,64,128]{2,1,0:T(8,128)} %s_hbm.3, f32[16,64,128]{2,1,0:T(8,128)} %r_hbm.3), custom_call_target="tpu_custom_call" | custom-call | tf_op jit(solution)/shard_map/pack_edges/pallas_call | solution.py:135
  1.7 1.5 %collective-permute-start = (f32[16,8,128]{2,1,0:T(8,128)S(1)}, f32[16,8,128]{2,1,0:T(8,128)S(1)}, u32[]{:S(2)}, u32[]{:S(2)}) collective-permute-start(f32[16,8,128]{2,1,0:T(8,128)S(1)} %get-tuple-element.42), channel_id=1, source_target_pairs={{0,16},{16,0},{32,48},{48,32},{64,80},{80,64},{96,112},{112,96},{1... | collective-permute-start | bytes 196616 | tf_op jit(solution)/shard_map/ppermute | solution.py:81
  3.2 1.3 %collective-permute-start.1 = (f32[16,8,128]{2,1,0:T(8,128)S(1)}, f32[16,8,128]{2,1,0:T(8,128)S(1)}, u32[]{:S(2)}, u32[]{:S(2)}) collective-permute-start(f32[16,8,128]{2,1,0:T(8,128)S(1)} %get-tuple-element.43), channel_id=1, source_target_pairs={{0,112},{16,32},{32,16},{48,64},{64,48},{80,96},{96,80},{112,0},{1... | collective-permute-start | bytes 196616 | tf_op jit(solution)/shard_map/ppermute | solution.py:81
  4.5 2.5 %load.1 = (f32[16,64,128]{2,1,0:T(8,128)S(1)}, f32[16,64,128]{2,1,0:T(8,128)S(1)}, f32[16,64,128]{2,1,0:T(8,128)S(1)}, s32[128,128]{1,0:T(8,128)S(1)}, f32[128,1...) custom-call(f32[16,64,128]{2,1,0:T(8,128)} %k_hbm.3, ...), custom_call_target="tpu_custom_call" | custom-call | tf_op jit(solution)/shard_map/load/pallas_call | solution.py:288
  7.0 0.0 collective-permute-done.first_ref
  7.0 0.2 collective-permute-done.1.second_ref
  7.2 0.3 pack_strip.1
  7.5 1.8 %collective-permute-start.2 = (f32[80,128]{1,0:T(8,128)S(1)}, f32[80,128]{1,0:T(8,128)S(1)}, u32[]{:S(2)}, u32[]{:S(2)}) collective-permute-start(f32[80,128]{1,0:T(8,128)S(1)} %get-tuple-element.47), channel_id=1, source_target_pairs={{0,1},{1,0},{2,3},{3,2},{4,5},{5,4},{6,7},{7,6},{8,9},{9,8},{10,11... | collective-permute-start | bytes 122888 | tf_op jit(solution)/shard_map/ppermute | solution.py:90
  9.3 1.7 %collective-permute-start.3 = (f32[80,128]{1,0:T(8,128)S(1)}, f32[80,128]{1,0:T(8,128)S(1)}, u32[]{:S(2)}, u32[]{:S(2)}) collective-permute-start(f32[80,128]{1,0:T(8,128)S(1)} %get-tuple-element.48), channel_id=1, source_target_pairs={{0,16},{1,2},{2,1},{3,4},{4,3},{5,6},{6,5},{7,8},{8,7},{9,10},{10,... | collective-permute-start | bytes 122888 | tf_op jit(solution)/shard_map/ppermute | solution.py:90
  11.0 0.6 pack_send.1
  11.6 1.0 %faces.1 = (f32[16,80,128]{2,1,0:T(8,128)S(1)}, f32[16,80,128]{2,1,0:T(8,128)S(1)}, f32[17,80,128]{2,1,0:T(8,128)S(1)}, f32[16,80,128]{2,1,0:T(8,128)S(1)}) custom-call(f32[16,64,128]{2,1,0:T(8,128)S(1)} %get-tuple-element.38.k_ref, f32[16,64,128]{2,1,0:T(8,128)S(1)} %get-tuple-element.39.s_ref, f32[16,8,128]{2,1,0:T(8,128)S(1)} %get-tuple-element.44.west_ref, ...), custom_call_target="tpu_custom_call" | custom-call | tf_op jit(solution)/shard_map/faces/pallas_call | solution.py:391
  12.6 0.0 collective-permute-done.2.first_ref
  12.6 0.0 collective-permute-done.3.second_ref
  12.6 5.8 %flow.1 = (f32[16,64,128]{2,1,0:T(8,128)S(1)}, f32[16,64,128]{2,1,0:T(8,128)S(1)}, f32[4096,128]{1,0:T(8,128)S(1)}, f32[1152,128]{1,0:T(8,128)S(1)}) custom-call(f32[16,64,128]{2,1,0:T(8,128)S(1)} %get-tuple-element.38.k_ref, f32[16,64,128]{2,1,0:T(8,128)S(1)} %get-tuple-element.39.s_ref, f32[16,64,128]{2,1,0:T(8,128)S(1)} %get-tuple-element.40.r_ref, ...), custom_call_target="tpu_custom_call" | custom-call | tf_op jit(solution)/shard_map/flow/pallas_call | solution.py:525
  18.4 25.7 %all_to_all.10 = f32[128,1,1152]{2,1,0:T(1,128)S(1)} all-to-all(f32[128,1,1152]{2,1,0:T(1,128)S(1)} %bitcast.8), channel_id=1, replica_groups=mesh['gx'=8,'gy'=16] {'gx','gy'}, dimensions={0} | all-to-all | bytes 1179648 | tf_op jit(solution)/shard_map/all_to_all | solution.py:866
  44.1 2.2 %first_step.1 = (f32[128,256]{1,0:T(8,128)S(1)}, f32[128,256]{1,0:T(8,128)S(1)}, f32[6,128,256]{2,1,0:T(8,128)S(1)}, f32[32,128]{1,0:T(8,128)S(1)}, f32[8,256]{1,0:T(8,128)S(1)}, /*index=5*/f32[8,128]{1,0:T(8,128)S(1)}) custom-call(f32[1152,128]{1,0:T(8,128)S(1)} %bitcast.7, f32[4096,128]{1,0:T(8,128)S(1)} %get-tuple-element.59.gath_ref, ...), custom_call_target="tpu_custom_call" | custom-call | tf_op jit(solution)/shard_map/first_step/pallas_call | solution.py:781
  46.3 0.9 %collective-permute-start.7 = (f32[8,256]{1,0:T(8,128)S(1)}, f32[8,256]{1,0:T(8,128)S(1)}, u32[]{:S(2)}, u32[]{:S(2)}) collective-permute-start(f32[8,256]{1,0:T(8,128)S(1)} %get-tuple-element.73), channel_id=1, source_target_pairs={{0,16},{1,2},{2,1},{3,4},{4,3},{5,6},{6,5},{7,8},{8,7},{9,10},{10,... | collective-permute-start | bytes 24584 | tf_op jit(solution)/shard_map/ppermute | solution.py:90
  47.2 0.0 collective-permute-start.6
  47.2 1.2 %collective-permute-start.5 = (f32[32,128]{1,0:T(8,128)S(1)}, f32[32,128]{1,0:T(8,128)S(1)}, u32[]{:S(2)}, u32[]{:S(2)}) collective-permute-start(f32[32,128]{1,0:T(8,128)S(1)} %get-tuple-element.72), channel_id=1, source_target_pairs={{0,112},{16,32},{32,16},{48,64},{64,48},{80,96},{96,80},{112,0},{1... | collective-permute-start | bytes 49160 | tf_op jit(solution)/shard_map/ppermute | solution.py:81
  48.3 0.2 collective-permute-start.4
  48.5 0.7 fusion
  49.2 0.0 collective-permute-done.7.end2_ref
  49.2 0.5 collective-permute-done.6.end1_ref
  49.7 0.8 %collective-permute-done.5.edge2_ref = f32[32,128]{1,0:T(8,128)S(1)} collective-permute-done((f32[32,128]{1,0:T(8,128)S(1)}, f32[32,128]{1,0:T(8,128)S(1)}, u32[]{:S(2)}, u32[]{:S(2)}) %collective-permute-start.5) | collective-permute-done | bytes 16416 | tf_op jit(solution)/shard_map/ppermute | solution.py:81
  50.5 0.0 collective-permute-done.4.edge1_ref
  50.5 2.1 %second_step.1 = f32[256,128]{1,0:T(8,128)} custom-call(f32[128,256]{1,0:T(8,128)S(1)} %get-tuple-element.68.c_ref, f32[128,256]{1,0:T(8,128)S(1)} %get-tuple-element.69.s_ref, f32[6,128,256]{2,1,0:T(8,128)S(1)} %get-tuple-element.70.flux_ref, bf16[256,1024]{1,0:T(8,128)(2,1)S(1)} %get-tuple-element.60.inner_ref, ...), custom_call_target="tpu_custom_call" | custom-call | tf_op jit(solution)/shard_map/second_step/pallas_call | solution.py:823
  52.6 7.4 %all-to-all-start.1 = ((f32[128,2,128]{2,1,0:T(2,128)}), f32[128,2,128]{2,1,0:T(2,128)S(1)}, u32[]{:S(2)}, u32[]{:S(2)}) async-start(f32[128,2,128]{2,1,0:T(2,128)} %bitcast.5), calls=%async_computation.1 | async-start | bytes 262144 | tf_op jit(solution)/shard_map/all_to_all | solution.py:874
  60.0 2.2 %multiply_add_fusion = f32[16,64,128]{2,1,0:T(8,128)} fusion(f32[16,64,128]{2,1,0:T(8,128)S(1)} %get-tuple-element.66, f32[16,64,128]{2,1,0:T(8,128)S(1)} %get-tuple-element.65, f32[]{:T(128)} %bitcast.4, f32[]{:T(128)} %bitcast.3), kind=kLoop, calls=%fused_computation | loop fusion | flops 393216 | bytes 1572872 | tf_op jit(solution)/shard_map/add | solution.py:872
  62.2 7.8 %all-to-all-done.1 = f32[128,2,128]{2,1,0:T(2,128)S(1)} async-done(((f32[128,2,128]{2,1,0:T(2,128)}), f32[128,2,128]{2,1,0:T(2,128)S(1)}, u32[]{:S(2)}, u32[]{:S(2)}) %all-to-all-start.1) | async-done | bytes 131104 | tf_op jit(solution)/shard_map/all_to_all | solution.py:874
  70.0 0.8 %to_owner.1 = f32[128,128]{1,0:T(8,128)} custom-call(bf16[128,256]{1,0:T(8,128)(2,1)S(1)} %get-tuple-element.67.mask_ref, f32[256,128]{1,0:T(8,128)S(1)} %bitcast.9), custom_call_target="tpu_custom_call" | custom-call | tf_op jit(solution)/shard_map/to_owner/pallas_call | solution.py:841
Async XLA Ops:
  1.7 5.3 %collective-permute-start = (f32[16,8,128]{2,1,0:T(8,128)S(1)}, f32[16,8,128]{2,1,0:T(8,128)S(1)}, u32[]{:S(2)}, u32[]{:S(2)}) collective-permute-start(f32[16,8,128]{2,1,0:T(8,128)S(1)} %get-tuple-element.42), channel_id=1, source_target_pairs={{0,16},{16,0},{32,48},{48,32},{64,80},{80,64},{96,112},{112,96},{1... | collective-permute-start | bytes 196616 | tf_op jit(solution)/shard_map/ppermute | solution.py:81
  3.2 4.0 %collective-permute-start.1 = (f32[16,8,128]{2,1,0:T(8,128)S(1)}, f32[16,8,128]{2,1,0:T(8,128)S(1)}, u32[]{:S(2)}, u32[]{:S(2)}) collective-permute-start(f32[16,8,128]{2,1,0:T(8,128)S(1)} %get-tuple-element.43), channel_id=1, source_target_pairs={{0,112},{16,32},{32,16},{48,64},{64,48},{80,96},{96,80},{112,0},{1... | collective-permute-start | bytes 196616 | tf_op jit(solution)/shard_map/ppermute | solution.py:81
  7.5 5.1 %collective-permute-start.2 = (f32[80,128]{1,0:T(8,128)S(1)}, f32[80,128]{1,0:T(8,128)S(1)}, u32[]{:S(2)}, u32[]{:S(2)}) collective-permute-start(f32[80,128]{1,0:T(8,128)S(1)} %get-tuple-element.47), channel_id=1, source_target_pairs={{0,1},{1,0},{2,3},{3,2},{4,5},{5,4},{6,7},{7,6},{8,9},{9,8},{10,11... | collective-permute-start | bytes 122888 | tf_op jit(solution)/shard_map/ppermute | solution.py:90
  9.3 3.3 %collective-permute-start.3 = (f32[80,128]{1,0:T(8,128)S(1)}, f32[80,128]{1,0:T(8,128)S(1)}, u32[]{:S(2)}, u32[]{:S(2)}) collective-permute-start(f32[80,128]{1,0:T(8,128)S(1)} %get-tuple-element.48), channel_id=1, source_target_pairs={{0,16},{1,2},{2,1},{3,4},{4,3},{5,6},{6,5},{7,8},{8,7},{9,10},{10,... | collective-permute-start | bytes 122888 | tf_op jit(solution)/shard_map/ppermute | solution.py:90
  46.3 2.9 %collective-permute-start.7 = (f32[8,256]{1,0:T(8,128)S(1)}, f32[8,256]{1,0:T(8,128)S(1)}, u32[]{:S(2)}, u32[]{:S(2)}) collective-permute-start(f32[8,256]{1,0:T(8,128)S(1)} %get-tuple-element.73), channel_id=1, source_target_pairs={{0,16},{1,2},{2,1},{3,4},{4,3},{5,6},{6,5},{7,8},{8,7},{9,10},{10,... | collective-permute-start | bytes 24584 | tf_op jit(solution)/shard_map/ppermute | solution.py:90
  47.2 2.5 %collective-permute-start.6 = (f32[8,256]{1,0:T(8,128)S(1)}, f32[8,256]{1,0:T(8,128)S(1)}, u32[]{:S(2)}, u32[]{:S(2)}) collective-permute-start(f32[8,256]{1,0:T(8,128)S(1)} %get-tuple-element.73), channel_id=1, source_target_pairs={{0,1},{1,0},{2,3},{3,2},{4,5},{5,4},{6,7},{7,6},{8,9},{9,8},{10,11... | collective-permute-start | bytes 24584 | tf_op jit(solution)/shard_map/ppermute | solution.py:90
  47.2 3.3 %collective-permute-start.5 = (f32[32,128]{1,0:T(8,128)S(1)}, f32[32,128]{1,0:T(8,128)S(1)}, u32[]{:S(2)}, u32[]{:S(2)}) collective-permute-start(f32[32,128]{1,0:T(8,128)S(1)} %get-tuple-element.72), channel_id=1, source_target_pairs={{0,112},{16,32},{32,16},{48,64},{64,48},{80,96},{96,80},{112,0},{1... | collective-permute-start | bytes 49160 | tf_op jit(solution)/shard_map/ppermute | solution.py:81
  48.3 2.2 %collective-permute-start.4 = (f32[32,128]{1,0:T(8,128)S(1)}, f32[32,128]{1,0:T(8,128)S(1)}, u32[]{:S(2)}, u32[]{:S(2)}) collective-permute-start(f32[32,128]{1,0:T(8,128)S(1)} %get-tuple-element.72), channel_id=1, source_target_pairs={{0,16},{16,0},{32,48},{48,32},{64,80},{80,64},{96,112},{112,96},{1... | collective-permute-start | bytes 49160 | tf_op jit(solution)/shard_map/ppermute | solution.py:81
  52.6 17.4 %all-to-all-start.1 = ((f32[128,2,128]{2,1,0:T(2,128)}), f32[128,2,128]{2,1,0:T(2,128)S(1)}, u32[]{:S(2)}, u32[]{:S(2)}) async-start(f32[128,2,128]{2,1,0:T(2,128)} %bitcast.5), calls=%async_computation.1 | async-start | bytes 262144 | tf_op jit(solution)/shard_map/all_to_all | solution.py:874
